TPU v7x, 256 devices: a whole 4x4x8 slice. The times are simulated.
256 devices in a mesh: row: 8 (over z), col: 16 (over y, x_lo, core), rep: 2 (over x_hi).
Axes of the slice: x: 4 (x_hi: 2, x_lo: 2; x = x_hi * 2 + x_lo), y: 4, z: 8, core: 2. Of those that a mesh axis runs over, the one named last changes fastest.
Arguments:
- hamiltonian: bfloat16 [8192, 8192], P('row', ('rep', 'col')), may hold values from -0.109375 to 0.109375
- density: bfloat16 [8192, 8192], P(('rep', 'row'), 'col'), may hold values from -6 to 6
- ham_pattern: int32 [128, 128], P('row', ('rep', 'col')), may hold values 0 or 1
- den_pattern: int32 [128, 128], P(('rep', 'row'), 'col'), may hold values 0 or 1
- tile_basis: bfloat16 [64, 16, 2048], P(None, None, 'col'), may hold values from -0.75 to 0.75
- offsets: int32 [128], P(('row', 'rep')), may hold values from 0 to 31
Outputs:
- product: bfloat16 [8192, 8192], P(('row', 'rep'), 'col')
- grid_density: float32 [512, 2048], P(('row', 'rep'), 'col')
All inputs are finite; a program needn't handle non-finite values. No bound on the sum of `ham_pattern` or of `den_pattern` on one device may be relied on, other than what follows from the above.
Results may differ from a plain program's by a relative error of at most 0.0004.
Values may be sent and summed in bfloat16 or wider, within the bound.
No kernel may reach another device: no remote copies, remote signals or barrier semaphores. Data moves between devices by JAX's collectives and lax.ppermute only.
A program may use at most 128 MiB of HBM per device.

v0:
```python
import math

import jax
import jax.numpy as jnp
from jax import lax
from jax.sharding import PartitionSpec as P

SX = 32
TX = 16


def shifted(value, axis, steps):
    count = lax.axis_size(axis)
    pairs = [(source, (source + steps) % count) for source in range(count)]
    return lax.ppermute(value, axis, pairs)


def expand(matrix, pattern):
    rows_b, cols_b = pattern.shape
    block = matrix.shape[0] // rows_b
    weight = pattern.astype(matrix.dtype)
    shaped = matrix.reshape(rows_b, block, cols_b, block) * weight[:, None, :, None]
    return shaped.reshape(matrix.shape)


def row_charges(full_rows):
    return lax.psum(jnp.sum(full_rows, axis=1), "col")


def shards(hamiltonian, density, ham_pattern, den_pattern, tile_basis, offsets):
    ham = expand(hamiltonian, ham_pattern)
    dens = expand(density, den_pattern)
    n_col = lax.axis_size("col")
    den_half = lax.all_gather(dens, "row", axis=0, tiled=True)
    partial_terms = jnp.dot(
        lax.all_gather(ham, "col", axis=1, tiled=True), den_half, preferred_element_type=jnp.float32
    )
    full_rows = lax.psum_scatter(partial_terms, "rep", scatter_dimension=0, tiled=True)
    sums = row_charges(full_rows)
    total_order = full_rows.shape[1] * n_col
    atoms = offsets.shape[0]
    amplitudes = (sums * (1.0 / math.sqrt(total_order))).reshape(atoms, -1)
    tiles = jnp.einsum(
        "am,mtp->atp", amplitudes, tile_basis.astype(jnp.float32), precision=lax.Precision.HIGHEST
    )
    planes = offsets[:, None] + jnp.arange(TX, dtype=jnp.int32)[None, :]
    onehot = (planes[:, :, None] == jnp.arange(SX + TX, dtype=jnp.int32)[None, None, :]).astype(
        jnp.float32
    )
    extended = jnp.einsum("atx,atp->xp", onehot, tiles, precision=lax.Precision.HIGHEST)
    own_planes = extended[:SX]
    incoming = shifted(extended[SX:], ("row", "rep"), 1)
    grid_density = jnp.concatenate([own_planes[:TX] + incoming, own_planes[TX:]], axis=0)
    return (full_rows.astype(jnp.bfloat16), grid_density)


def solution(mesh):
    in_specs = (
        P("row", ("rep", "col")),
        P(("rep", "row"), "col"),
        P("row", ("rep", "col")),
        P(("rep", "row"), "col"),
        P(None, None, "col"),
        P(("row", "rep")),
    )
    out_specs = (P(("row", "rep"), "col"), P(("row", "rep"), "col"))
    return jax.shard_map(shards, mesh=mesh, in_specs=in_specs, out_specs=out_specs, check_vma=False)
```

profile of v0, /device:TPU:1, one launch (start us, length us, event | category | flops | bytes accessed | tf_op | source)
XLA Modules:
  0.0 226.0 jit_solution(1121275618799733982)
XLA Ops:
  7.2 0.0 copy-start
  7.2 0.0 copy-start.2
  7.2 0.0 copy-start.1
  7.2 0.0 all-gather.5.cloned.1.call-start
  7.2 0.8 convert_element_type.12
  8.0 0.2 mul.31
  8.2 0.6 mul.32
  8.8 2.0 mul.33
  10.9 0.0 all-gather.5.cloned.1.call-update
  10.9 0.0 all-gather.3.cloned.1.call-start
  10.9 0.0 copy-done.2
  10.9 0.1 copy.8
  11.0 0.3 mul.28
  11.4 0.7 mul.29
  12.1 0.0 copy-done.1
  12.1 0.9 mul.30
  13.0 0.0 all-gather.3.cloned.1.call-update
  13.0 0.0 copy-start.3
  13.0 0.0 reduce-scatter.2.cloned.1.call-start
  13.1 56.6 %all-gather.5.cloned.1.call-done = bf16[4096,512]{1,0:T(8,128)(2,1)} async-done(((bf16[512,512]{1,0:T(8,128)(2,1)}), bf16[4096,512]{1,0:T(8,128)(2,1)}) %all-gather.5.cloned.1.call-update) | async-done | bytes 4194320 | tf_op jit(solution)/shard_map/all_gather | solution.py:34
  69.7 66.5 %all-gather.3.cloned.1.call-done = bf16[1024,4096]{1,0:T(8,128)(2,1)} async-done(((bf16[1024,256]{1,0:T(8,128)(2,1)}), bf16[1024,4096]{1,0:T(8,128)(2,1)}) %all-gather.3.cloned.1.call-update) | async-done | bytes 8388624 | tf_op jit(solution)/shard_map/all_gather | solution.py:36
  136.2 10.4 %fusion.5 = f32[1024,512]{1,0:T(8,128)} fusion(bf16[1024,4096]{1,0:T(8,128)(2,1)} %all-gather.3.cloned.1.call-done, bf16[4096,512]{1,0:T(8,128)(2,1)} %all-gather.5.cloned.1.call-done), kind=kOutput, calls=%fused_computation.11 | convolution fusion | flops 4294967296 | bytes 14680064 | tf_op jit(solution)/shard_map/dot_general | solution.py:35
  146.6 0.0 reduce-scatter.2.cloned.1.call-update
  146.6 0.0 copy-done.3
  146.6 0.1 iota_add_fusion
  146.7 35.7 %reduce-scatter.2.cloned.1.call-done = f32[512,512]{1,0:T(8,128)} async-done(((f32[1024,512]{1,0:T(8,128)}), f32[512,512]{1,0:T(8,128)}) %reduce-scatter.2.cloned.1.call-update) | async-done | bytes 1048592 | tf_op jit(solution)/shard_map/reduce_scatter | solution.py:38
  182.4 2.5 %fusion.4 = (f32[512]{0:T(512)S(1)}, bf16[512,512]{1,0:T(8,128)(2,1)}) fusion(f32[512,512]{1,0:T(8,128)} %reduce-scatter.2.cloned.1.call-done), kind=kLoop, calls=%fused_computation.10 | loop fusion | flops 523776 | bytes 1574912 | tf_op jit(solution)/shard_map/reduce_sum | solution.py:27
  184.9 27.1 %psum.7 = f32[512]{0:T(512)S(1)} all-reduce(f32[512]{0:T(512)S(1)} %get-tuple-element.2), channel_id=1, replica_groups=mesh['row'=8,'col'=16,'rep'=2] {'col'}, use_global_device_ids=true, to_apply=%region_2.0 | all-reduce | flops 512 | bytes 4096 | tf_op jit(solution)/shard_map/psum | solution.py:27
  212.0 0.1 reshape.37
  212.1 0.0 copy-done
  212.1 0.2 fusion
  212.3 0.3 convolution_bitcast_fusion
  212.6 0.9 collective-permute-start
  213.5 5.3 %collective-permute-done = f32[16,128]{1,0:T(8,128)S(1)} collective-permute-done((f32[16,128]{1,0:T(8,128)S(1)}, f32[16,128]{1,0:T(8,128)S(1)}, u32[]{:S(2)}, u32[]{:S(2)}) %collective-permute-start) | collective-permute-done | bytes 8224 | tf_op jit(solution)/shard_map/ppermute | solution.py:15
  218.8 0.6 pad_maximum_fusion
  (4 shorter events, 0.0 us)
Async XLA Ops:
  7.2 204.9 %copy-start = (bf16[64,16,128]{2,1,0:T(8,128)(2,1)S(1)}, bf16[64,16,128]{2,1,0:T(8,128)(2,1)}, u32[]{:S(2)}) copy-start(bf16[64,16,128]{2,1,0:T(8,128)(2,1)} %param.10) | copy-start | bytes 786436
  7.2 3.7 %copy-start.2 = (s32[16,4]{0,1:T(4,128)S(1)}, s32[16,4]{0,1:T(4,128)}, u32[]{:S(2)}) copy-start(s32[16,4]{0,1:T(4,128)} %param.8) | copy-start | bytes 772
  7.2 4.9 %copy-start.1 = (bf16[1024,256]{1,0:T(8,128)(2,1)S(1)}, bf16[1024,256]{1,0:T(8,128)(2,1)}, u32[]{:S(2)}) copy-start(bf16[1024,256]{1,0:T(8,128)(2,1)} %param.6) | copy-start | bytes 1572868
  7.2 62.5 %all-gather.5.cloned.1.call-start = ((), (), s32[]{:S(2)}) async-start(), calls=%async_computation.2 | async-start | bytes 4718592 | tf_op jit(solution)/shard_map/all_gather | solution.py:34
  10.9 125.3 %all-gather.3.cloned.1.call-start = ((), (), s32[]{:S(2)}) async-start(), calls=%async_computation.1 | async-start | bytes 8912896 | tf_op jit(solution)/shard_map/all_gather | solution.py:36
  13.0 133.6 %copy-start.3 = (s32[8]{0:T(128)S(1)}, s32[8]{0:T(128)}, u32[]{:S(2)}) copy-start(s32[8]{0:T(128)} %param.11) | copy-start | bytes 100
  13.0 169.4 %reduce-scatter.2.cloned.1.call-start = ((), (), s32[]{:S(2)}) async-start(), calls=%async_computation.3 | async-start | bytes 3145728 | tf_op jit(solution)/shard_map/reduce_scatter | solution.py:38
  212.6 6.2 %collective-permute-start = (f32[16,128]{1,0:T(8,128)S(1)}, f32[16,128]{1,0:T(8,128)S(1)}, u32[]{:S(2)}, u32[]{:S(2)}) collective-permute-start(f32[16,128]{1,0:T(8,128)S(1)} %slice.16), channel_id=1, source_target_pairs={{0,1},{1,32},{32,33},{33,64},{64,65},{65,96},{96,97},{97,128},{128... | collective-permute-start | bytes 24584 | tf_op jit(solution)/shard_map/ppermute | solution.py:15
Sparse Core Ops, SparseCore 0:
  11.0 58.6 all-gather.4
  72.0 64.1 all-gather.2
  146.7 35.6 reduce-scatter.1
where the time goes:
time: 227 us; the launch traced here: 226 us
  waiting for transfers between devices  164 us (72%)
  blocking collectives  27.1 us (12%)
  between operations  13.8 us (6%)
  matrix products  10.9 us (5%)
  other arithmetic  6.89 us (3%)
    all_gather x1, waiting for transfers between devices, shards(): lax.all_gather(ham, 'col', axis=1, tiled=True)  66.5 us
    all_gather x1, waiting for transfers between devices, shards(): den_half = lax.all_gather(dens, 'row', axis=0, tiled=True)  56.6 us
    reduce_scatter x1, waiting for transfers between devices, shards(): lax.psum_scatter(partial_terms, 'rep', scatter_dimension=0, tiled=True)  35.7 us
    psum x1, blocking collectives, row_charges(): return lax.psum(jnp.sum(full_rows, axis=1), 'col')  27.1 us
    dot_general x1, matrix products, shards(): jnp.dot(lax.all_gather(ham, 'col', axis=1, tiled=True), den_half, preferr...  10.4 us
    ppermute x1, waiting for transfers between devices, shifted(): return lax.ppermute(value, axis, pairs)  5.33 us
  transfers between devices with their start and end apart: 4, of which 4 were waited for; matrix products, arithmetic and copies ran while one was open for 1% of the time, Pallas kernels for 0%

commit v1 on v0

v1 whole, which is shorter than its diff:
```python
import functools
import math

import jax
import jax.numpy as jnp
from jax import lax
from jax.experimental import pallas as pl
from jax.experimental.pallas import tpu as pltpu
from jax.sharding import PartitionSpec as P

SX = 32
TX = 16
BLK = 64
MIB = 1 << 20

NZ = 8
NY = 4
CHUNKS = 2
F32 = jnp.float32
BF16 = jnp.bfloat16


def over_row(value, steps):
    return lax.ppermute(value, "row", [(i, (i + steps) % NZ) for i in range(NZ)])


def row_swap(value, bit):
    return lax.ppermute(value, "row", [(i, i ^ bit) for i in range(NZ)])


def over_y(value, steps):
    pairs = []
    for c in range(4 * NY):
        pairs.append((c, ((c // 4 + steps) % NY) * 4 + c % 4))
    return lax.ppermute(value, "col", pairs)


def col_swap(value, bit):
    return lax.ppermute(value, "col", [(c, c ^ bit) for c in range(4 * NY)])


def rep_swap(value):
    return lax.ppermute(value, "rep", [(0, 1), (1, 0)])


def spread(pattern_ref, rows, cols):
    pattern = pattern_ref[...].astype(F32).astype(BF16)
    rows_b, cols_b = pattern.shape
    left = (
        lax.broadcasted_iota(jnp.int32, (rows, rows_b), 0) // BLK
        == lax.broadcasted_iota(jnp.int32, (rows, rows_b), 1)
    )
    right = (
        lax.broadcasted_iota(jnp.int32, (cols_b, cols), 1) // BLK
        == lax.broadcasted_iota(jnp.int32, (cols_b, cols), 0)
    )
    wide = jnp.dot(pattern, right.astype(F32).astype(BF16), preferred_element_type=F32)
    return jnp.dot(
        left.astype(F32).astype(BF16), wide.astype(BF16), preferred_element_type=F32
    ).astype(BF16)


def dens_mask_kernel(pattern_ref, dens_ref, *chunk_refs):
    rows, cols = dens_ref.shape
    masked = dens_ref[...] * spread(pattern_ref, rows, cols)
    width = cols // len(chunk_refs)
    for i, ref in enumerate(chunk_refs):
        ref[...] = masked[:, i * width : (i + 1) * width]


def ham_mask_kernel(pattern_ref, ham_ref, out_ref):
    rows, cols = ham_ref.shape
    out_ref[...] = ham_ref[...] * spread(pattern_ref, rows, cols)


def mask_dens(pattern, dens):
    rows, cols = dens.shape
    shapes = [jax.ShapeDtypeStruct((rows, cols // CHUNKS), BF16)] * CHUNKS
    return pl.pallas_call(
        dens_mask_kernel,
        out_shape=shapes,
        compiler_params=pltpu.CompilerParams(vmem_limit_bytes=24 * MIB),
        name="mask_dens",
    )(pattern, dens)


def mask_ham(pattern, ham):
    return pl.pallas_call(
        ham_mask_kernel,
        out_shape=jax.ShapeDtypeStruct(ham.shape, BF16),
        compiler_params=pltpu.CompilerParams(vmem_limit_bytes=24 * MIB),
        name="mask_ham",
    )(pattern, ham)


def place():
    row = lax.axis_index("row")
    col = lax.axis_index("col")
    return row, col // 4, (col // 2) % 2, col % 2, lax.axis_index("rep")


def rows_kernel(other, *refs):
    n_ham, n_den = len(HAM_KEYS), NZ * CHUNKS
    ham_refs, den_refs = refs[:n_ham], refs[n_ham : n_ham + n_den]
    out_ref, sums_ref, ham_buf = refs[n_ham + n_den :]
    row, y, x, core, rep = place()
    part = (1 - rep) if other else rep
    rows = out_ref.shape[0]
    first = pl.multiple_of(part * rows, rows)
    for n, (dy, dx, dk) in enumerate(HAM_KEYS):
        chip = lax.rem(y + dy, NY) * 2 + (x + dx - 2 * x * dx)
        half = core + dk - 2 * core * dk
        ham_buf[chip, half] = ham_refs[n][pl.ds(first, rows), :]
    half = ham_buf.shape[3]
    width = out_ref.shape[1] // CHUNKS
    for s in range(NZ):
        chip = lax.rem(row + s, NZ)
        for i in range(CHUNKS):
            den_ref = den_refs[s * CHUNKS + i]
            term = jnp.dot(ham_buf[chip, 0], den_ref[:half], preferred_element_type=F32)
            term += jnp.dot(ham_buf[chip, 1], den_ref[half:], preferred_element_type=F32)
            cols = pl.ds(i * width, width)
            if s == 0:
                out_ref[:, cols] = term
            else:
                out_ref[:, cols] += term
    lanes = 128
    folded = out_ref[:, :lanes]
    for j in range(lanes, out_ref.shape[1], lanes):
        folded += out_ref[:, j : j + lanes]
    sums_ref[...] = lax.dot_general(
        jnp.ones((8, lanes), F32),
        folded,
        (((1,), (1,)), ((), ())),
        precision=lax.Precision.HIGHEST,
        preferred_element_type=F32,
    )


def rows_of(other, ham_blocks, den_blocks):
    rows = ham_blocks[0].shape[0] // 2
    half = ham_blocks[0].shape[1]
    depth = den_blocks[0].shape[0]
    cols = den_blocks[0].shape[1] * CHUNKS
    n = len(ham_blocks) + len(den_blocks)
    return pl.pallas_call(
        functools.partial(rows_kernel, other),
        out_shape=(
            jax.ShapeDtypeStruct((rows, cols), F32),
            jax.ShapeDtypeStruct((8, rows), F32),
        ),
        in_specs=[pl.BlockSpec(memory_space=pltpu.VMEM)] * n,
        scratch_shapes=[pltpu.VMEM((NZ, 2, rows, half), BF16)],
        compiler_params=pltpu.CompilerParams(vmem_limit_bytes=30 * MIB),
        cost_estimate=pl.CostEstimate(
            flops=2 * rows * cols * depth * NZ, bytes_accessed=8 * MIB, transcendentals=0
        ),
        name="rows_other" if other else "rows_own",
    )(*ham_blocks, *den_blocks)


HAM_KEYS = [(dy, dx, dk) for dy in range(NY) for dx in range(2) for dk in range(2)]


def gather_dens(chunks):
    den = [[None] * CHUNKS for _ in range(NZ)]
    den[0] = list(chunks)
    up, down = list(chunks), list(chunks)
    for step in range(1, 5):
        for i in range(CHUNKS):
            if step < 4 or i % 2 == 0:
                up[i] = over_row(up[i], 1)
                den[(NZ - step) % NZ][i] = up[i]
        for i in range(CHUNKS):
            if step < 4 or i % 2 == 1:
                down[i] = over_row(down[i], -1)
                den[step][i] = down[i]
    return [block for blocks in den for block in blocks]


def gather_ham(ham):
    got = {(0, 0): ham}
    got[(3, 0)] = over_y(ham, 1)
    got[(1, 0)] = over_y(ham, -1)
    got[(0, 1)] = col_swap(ham, 2)
    got[(3, 1)] = over_y(got[(0, 1)], 1)
    got[(1, 1)] = over_y(got[(0, 1)], -1)
    got[(2, 0)] = over_y(got[(3, 0)], 1)
    got[(2, 1)] = over_y(got[(1, 1)], -1)
    blocks = {}
    for (dy, dx), block in got.items():
        blocks[(dy, dx, 0)] = block
        blocks[(dy, dx, 1)] = col_swap(block, 1)
    return [blocks[key] for key in HAM_KEYS]


def shards(hamiltonian, density, ham_pattern, den_pattern, tile_basis, offsets):
    chunks = mask_dens(den_pattern, density)
    ham = mask_ham(ham_pattern, hamiltonian)
    den_blocks = gather_dens(chunks)
    ham_blocks = gather_ham(ham)

    part, part_sums = rows_of(True, ham_blocks, den_blocks)
    sent = rep_swap(part)
    part_sums = rep_swap(part_sums)
    kept, sums = rows_of(False, ham_blocks, den_blocks)
    product = (kept + sent).astype(BF16)

    sums = sums + part_sums
    for bit in (1, 2, 4, 8):
        sums = sums + col_swap(sums, bit)
    charges = sums[:1]
    total_order = density.shape[1] * lax.axis_size("col")
    atoms = offsets.shape[0]
    amplitudes = (charges * (1.0 / math.sqrt(total_order))).reshape(atoms, -1)
    tiles = jnp.einsum(
        "am,mtp->atp", amplitudes, tile_basis.astype(F32), precision=lax.Precision.HIGHEST
    )
    planes = offsets[:, None] + jnp.arange(TX, dtype=jnp.int32)[None, :]
    onehot = (planes[:, :, None] == jnp.arange(SX + TX, dtype=jnp.int32)[None, None, :]).astype(F32)
    extended = jnp.einsum("atx,atp->xp", onehot, tiles, precision=lax.Precision.HIGHEST)
    own_planes = extended[:SX]
    count = lax.axis_size("row") * lax.axis_size("rep")
    incoming = lax.ppermute(
        extended[SX:], ("row", "rep"), [(i, (i + 1) % count) for i in range(count)]
    )
    grid_density = jnp.concatenate([own_planes[:TX] + incoming, own_planes[TX:]], axis=0)

    return (product, grid_density)


def solution(mesh):
    in_specs = (
        P("row", ("rep", "col")),
        P(("rep", "row"), "col"),
        P("row", ("rep", "col")),
        P(("rep", "row"), "col"),
        P(None, None, "col"),
        P(("row", "rep")),
    )
    out_specs = (P(("row", "rep"), "col"), P(("row", "rep"), "col"))
    return jax.shard_map(shards, mesh=mesh, in_specs=in_specs, out_specs=out_specs, check_vma=False)
```

time: 227 us -> 122 us (0.54)
  waiting for transfers between devices: 164 us -> 64 us
  starting transfers between devices: 0.99 us -> 45.3 us
  blocking collectives: 27.1 us -> 0 us
  between operations: 13.8 us -> 0.77 us
  matrix products: 10.9 us -> 0.52 us
  Pallas kernels: 0 us -> 6.49 us
  other arithmetic: 6.89 us -> 2.89 us
    all_gather x2 -> x0, waiting for transfers between devices: 123 us -> none  [the longest x1 66.5 us: shards(): lax.all_gather(ham, 'col', axis=1, tiled=True)]
    ppermute x1 -> x36, waiting for transfers between devices: 5.33 us -> 64 us  [the longest x14 29.8 us: over_row(): lax.ppermute(value, 'row', [(i, (i + steps) % NZ) for i in range(NZ)])]
    ppermute x1 -> x36, starting transfers between devices: 0.87 us -> 45.3 us  [the longest x14 16.8 us: over_row(): lax.ppermute(value, 'row', [(i, (i + steps) % NZ) for i in range(NZ)])]
    reduce_scatter x1 -> x0, waiting for transfers between devices: 35.7 us -> none  [shards(): lax.psum_scatter(partial_terms, 'rep', scatter_dimension=0, tiled=True)]
    psum x1 -> x0, blocking collectives: 27.1 us -> none  [row_charges(): return lax.psum(jnp.sum(full_rows, axis=1), 'col')]
    dot_general x2 -> x1, matrix products: 10.6 us -> 0.22 us  [shards(): jnp.einsum('am,mtp->atp', amplitudes, tile_basis.astype(F32), precision=l...]
    pallas_call x0 -> x4, Pallas kernels: none -> 6.49 us  [the longest x2 5.69 us: rows_of(): pl.pallas_call(functools.partial(rows_kernel, other), out_shape=(jax.Shap...]
    mul x3 -> x1, other arithmetic: 2.94 us -> 0.02 us  [shards(): amplitudes = (charges * (1.0 / math.sqrt(total_order))).reshape(atoms, -1)]
  transfers between devices with their start and end apart: 4 -> 36, of which waited for: 4 -> 20; matrix products, arithmetic and copies ran while one was open for 1% -> 1% of each run, Pallas kernels for 0% -> 3%
where the time goes in v1:
time: 122 us
  waiting for transfers between devices  64 us (52%)
  starting transfers between devices  45.3 us (37%)
  Pallas kernels  6.49 us (5%)
  other arithmetic  2.89 us (2%)
  local copies, waits for them, and re-layouts  1.95 us (2%)
    ppermute x14, waiting for transfers between devices, over_row(): lax.ppermute(value, 'row', [(i, (i + steps) % NZ) for i in range(NZ)])  29.8 us
    ppermute x14, starting transfers between devices, over_row(): lax.ppermute(value, 'row', [(i, (i + steps) % NZ) for i in range(NZ)])  16.8 us
    ppermute x13, starting transfers between devices, col_swap(): return lax.ppermute(value, 'col', [(c, c ^ bit) for c in range(4 * NY)])  16.8 us
    ppermute x1, waiting for transfers between devices, shards(): lax.ppermute(extended[SX:], ('row', 'rep'), [(i, (i + 1) % count) for i i...  12.6 us
    ppermute x13, waiting for transfers between devices, col_swap(): return lax.ppermute(value, 'col', [(c, c ^ bit) for c in range(4 * NY)])  11.7 us
    ppermute x6, waiting for transfers between devices, over_y(): return lax.ppermute(value, 'col', pairs)  8.56 us
    ppermute x6, starting transfers between devices, over_y(): return lax.ppermute(value, 'col', pairs)  5.85 us
    pallas_call x2, Pallas kernels, rows_of(): pl.pallas_call(functools.partial(rows_kernel, other), out_shape=(jax.Shap...  5.69 us
  transfers between devices with their start and end apart: 36, of which 20 were waited for; matrix products, arithmetic and copies ran while one was open for 1% of the time, Pallas kernels for 3%

profile of v1, /device:TPU:1, one launch (start us, length us, event | category | flops | bytes accessed | tf_op | source)
XLA Modules:
  0.0 121.9 jit_solution(2040809489302076052)
XLA Ops:
  0.7 1.1 copy-done.1
  1.7 0.7 copy-done.3
  2.4 0.4 mask_dens.1
  2.8 2.5 %collective-permute-start.21 = (bf16[512,256]{1,0:T(8,128)(2,1)S(1)}, bf16[512,256]{1,0:T(8,128)(2,1)S(1)}, u32[]{:S(2)}, u32[]{:S(2)}) collective-permute-start(bf16[512,256]{1,0:T(8,128)(2,1)S(1)} %get-tuple-element.8.refs_16_), channel_id=1, source_target_pairs={{0,32},{32,64},{64,96},{96,128},{128,160},{160,192},{192,224},{224... | collective-permute-start | bytes 786440 | tf_op jit(solution)/shard_map/ppermute | solution.py:24
  5.4 0.4 mask_ham.1.refs_0_
  5.9 1.3 %collective-permute-start.1 = (bf16[1024,256]{1,0:T(8,128)(2,1)S(1)}, bf16[1024,256]{1,0:T(8,128)(2,1)S(1)}, u32[]{:S(2)}, u32[]{:S(2)}) collective-permute-start(bf16[1024,256]{1,0:T(8,128)(2,1)S(1)} %mask_ham.1.refs_0_), channel_id=1, source_target_pairs={{0,4},{2,6},{4,0},{6,2},{8,12},{10,14},{12,8},{14,10},{16,20},{18,... | collective-permute-start | bytes 1572872 | tf_op jit(solution)/shard_map/ppermute | solution.py:39
  7.2 1.3 %collective-permute-start.7 = (bf16[1024,256]{1,0:T(8,128)(2,1)S(1)}, bf16[1024,256]{1,0:T(8,128)(2,1)S(1)}, u32[]{:S(2)}, u32[]{:S(2)}) collective-permute-start(bf16[1024,256]{1,0:T(8,128)(2,1)S(1)} %mask_ham.1.refs_0_), channel_id=1, source_target_pairs={{0,8},{2,10},{4,12},{6,14},{8,16},{10,18},{12,20},{14,22},{16,24},... | collective-permute-start | bytes 1572872 | tf_op jit(solution)/shard_map/ppermute | solution.py:35
  8.5 4.4 %collective-permute-start.16 = (bf16[512,256]{1,0:T(8,128)(2,1)S(1)}, bf16[512,256]{1,0:T(8,128)(2,1)S(1)}, u32[]{:S(2)}, u32[]{:S(2)}) collective-permute-start(bf16[512,256]{1,0:T(8,128)(2,1)S(1)} %get-tuple-element.9.refs_17_), channel_id=1, source_target_pairs={{0,224},{32,0},{64,32},{96,64},{128,96},{160,128},{192,160},{224,1... | collective-permute-start | bytes 786440 | tf_op jit(solution)/shard_map/ppermute | solution.py:24
  12.9 1.0 collective-permute-start.15
  13.9 1.5 %collective-permute-done.21.refs_30_ = bf16[512,256]{1,0:T(8,128)(2,1)S(1)} collective-permute-done((bf16[512,256]{1,0:T(8,128)(2,1)S(1)}, bf16[512,256]{1,0:T(8,128)(2,1)S(1)}, u32[]{:S(2)}, u32[]{:S(2)}) %collective-permute-start.21) | collective-permute-done | bytes 262176 | tf_op jit(solution)/shard_map/ppermute | solution.py:24
  15.3 1.9 %collective-permute-done.16.refs_19_ = bf16[512,256]{1,0:T(8,128)(2,1)S(1)} collective-permute-done((bf16[512,256]{1,0:T(8,128)(2,1)S(1)}, bf16[512,256]{1,0:T(8,128)(2,1)S(1)}, u32[]{:S(2)}, u32[]{:S(2)}) %collective-permute-start.16) | collective-permute-done | bytes 262176 | tf_op jit(solution)/shard_map/ppermute | solution.py:24
  17.3 5.6 %collective-permute-done.15.refs_18_ = bf16[512,256]{1,0:T(8,128)(2,1)S(1)} collective-permute-done((bf16[512,256]{1,0:T(8,128)(2,1)S(1)}, bf16[512,256]{1,0:T(8,128)(2,1)S(1)}, u32[]{:S(2)}, u32[]{:S(2)}) %collective-permute-start.15) | collective-permute-done | bytes 262176 | tf_op jit(solution)/shard_map/ppermute | solution.py:24
  22.9 1.5 %collective-permute-start.3 = (bf16[1024,256]{1,0:T(8,128)(2,1)S(1)}, bf16[1024,256]{1,0:T(8,128)(2,1)S(1)}, u32[]{:S(2)}, u32[]{:S(2)}) collective-permute-start(bf16[1024,256]{1,0:T(8,128)(2,1)S(1)} %mask_ham.1.refs_0_), channel_id=1, source_target_pairs={{0,24},{2,26},{4,28},{6,30},{8,0},{10,2},{12,4},{14,6},{16,8},{18,... | collective-permute-start | bytes 1572872 | tf_op jit(solution)/shard_map/ppermute | solution.py:35
  24.4 2.6 %collective-permute-start = (bf16[1024,256]{1,0:T(8,128)(2,1)S(1)}, bf16[1024,256]{1,0:T(8,128)(2,1)S(1)}, u32[]{:S(2)}, u32[]{:S(2)}) collective-permute-start(bf16[1024,256]{1,0:T(8,128)(2,1)S(1)} %mask_ham.1.refs_0_), channel_id=1, source_target_pairs={{0,2},{2,0},{4,6},{6,4},{8,10},{10,8},{12,14},{14,12},{16,18},{18,... | collective-permute-start | bytes 1572872 | tf_op jit(solution)/shard_map/ppermute | solution.py:39
  27.0 3.2 %collective-permute-start.18 = (bf16[512,256]{1,0:T(8,128)(2,1)S(1)}, bf16[512,256]{1,0:T(8,128)(2,1)S(1)}, u32[]{:S(2)}, u32[]{:S(2)}) collective-permute-start(bf16[512,256]{1,0:T(8,128)(2,1)S(1)} %collective-permute-done.16.refs_19_), channel_id=1, source_target_pairs={{0,224},{32,0},{64,32},{96,64},{128,96},{160,128},{192,160},{224,1... | collective-permute-start | bytes 786440 | tf_op jit(solution)/shard_map/ppermute | solution.py:24
  30.3 1.4 %collective-permute-start.27 = (bf16[512,256]{1,0:T(8,128)(2,1)S(1)}, bf16[512,256]{1,0:T(8,128)(2,1)S(1)}, u32[]{:S(2)}, u32[]{:S(2)}) collective-permute-start(bf16[512,256]{1,0:T(8,128)(2,1)S(1)} %collective-permute-done.26.refs_31_), channel_id=1, source_target_pairs={{0,32},{32,64},{64,96},{96,128},{128,160},{160,192},{192,224},{224... | collective-permute-start | bytes 786440 | tf_op jit(solution)/shard_map/ppermute | solution.py:24
  31.7 4.2 %collective-permute-done.18.refs_21_ = bf16[512,256]{1,0:T(8,128)(2,1)S(1)} collective-permute-done((bf16[512,256]{1,0:T(8,128)(2,1)S(1)}, bf16[512,256]{1,0:T(8,128)(2,1)S(1)}, u32[]{:S(2)}, u32[]{:S(2)}) %collective-permute-start.18) | collective-permute-done | bytes 262176 | tf_op jit(solution)/shard_map/ppermute | solution.py:24
  35.9 5.6 %collective-permute-done.17.refs_20_ = bf16[512,256]{1,0:T(8,128)(2,1)S(1)} collective-permute-done((bf16[512,256]{1,0:T(8,128)(2,1)S(1)}, bf16[512,256]{1,0:T(8,128)(2,1)S(1)}, u32[]{:S(2)}, u32[]{:S(2)}) %collective-permute-start.17) | collective-permute-done | bytes 262176 | tf_op jit(solution)/shard_map/ppermute | solution.py:24
  41.5 3.4 %collective-permute-start.20 = (bf16[512,256]{1,0:T(8,128)(2,1)S(1)}, bf16[512,256]{1,0:T(8,128)(2,1)S(1)}, u32[]{:S(2)}, u32[]{:S(2)}) collective-permute-start(bf16[512,256]{1,0:T(8,128)(2,1)S(1)} %collective-permute-done.18.refs_21_), channel_id=1, source_target_pairs={{0,224},{32,0},{64,32},{96,64},{128,96},{160,128},{192,160},{224,1... | collective-permute-start | bytes 786440 | tf_op jit(solution)/shard_map/ppermute | solution.py:24
  44.9 1.5 %collective-permute-start.5 = (bf16[1024,256]{1,0:T(8,128)(2,1)S(1)}, bf16[1024,256]{1,0:T(8,128)(2,1)S(1)}, u32[]{:S(2)}, u32[]{:S(2)}) collective-permute-start(bf16[1024,256]{1,0:T(8,128)(2,1)S(1)} %collective-permute-done.1.refs_2_), channel_id=1, source_target_pairs={{0,24},{2,26},{4,28},{6,30},{8,0},{10,2},{12,4},{14,6},{16,8},{18,... | collective-permute-start | bytes 1572872 | tf_op jit(solution)/shard_map/ppermute | solution.py:35
  46.6 3.1 %collective-permute-done.20.refs_23_ = bf16[512,256]{1,0:T(8,128)(2,1)S(1)} collective-permute-done((bf16[512,256]{1,0:T(8,128)(2,1)S(1)}, bf16[512,256]{1,0:T(8,128)(2,1)S(1)}, u32[]{:S(2)}, u32[]{:S(2)}) %collective-permute-start.20) | collective-permute-done | bytes 262176 | tf_op jit(solution)/shard_map/ppermute | solution.py:24
  49.7 0.5 collective-permute-start.28
  50.1 5.2 %collective-permute-done.19.refs_22_ = bf16[512,256]{1,0:T(8,128)(2,1)S(1)} collective-permute-done((bf16[512,256]{1,0:T(8,128)(2,1)S(1)}, bf16[512,256]{1,0:T(8,128)(2,1)S(1)}, u32[]{:S(2)}, u32[]{:S(2)}) %collective-permute-start.19) | collective-permute-done | bytes 262176 | tf_op jit(solution)/shard_map/ppermute | solution.py:24
  55.3 1.7 %collective-permute-start.2 = (bf16[1024,256]{1,0:T(8,128)(2,1)S(1)}, bf16[1024,256]{1,0:T(8,128)(2,1)S(1)}, u32[]{:S(2)}, u32[]{:S(2)}) collective-permute-start(bf16[1024,256]{1,0:T(8,128)(2,1)S(1)} %collective-permute-done.1.refs_2_), channel_id=1, source_target_pairs={{0,2},{2,0},{4,6},{6,4},{8,10},{10,8},{12,14},{14,12},{16,18},{18,... | collective-permute-start | bytes 1572872 | tf_op jit(solution)/shard_map/ppermute | solution.py:39
  57.1 3.7 %collective-permute-start.12 = (bf16[1024,256]{1,0:T(8,128)(2,1)S(1)}, bf16[1024,256]{1,0:T(8,128)(2,1)S(1)}, u32[]{:S(2)}, u32[]{:S(2)}) collective-permute-start(bf16[1024,256]{1,0:T(8,128)(2,1)S(1)} %collective-permute-done.7.refs_12_), channel_id=1, source_target_pairs={{0,2},{2,0},{4,6},{6,4},{8,10},{10,8},{12,14},{14,12},{16,18},{18,... | collective-permute-start | bytes 1572872 | tf_op jit(solution)/shard_map/ppermute | solution.py:39
  60.8 1.5 %collective-permute-start.10 = (bf16[1024,256]{1,0:T(8,128)(2,1)S(1)}, bf16[1024,256]{1,0:T(8,128)(2,1)S(1)}, u32[]{:S(2)}, u32[]{:S(2)}) collective-permute-start(bf16[1024,256]{1,0:T(8,128)(2,1)S(1)} %collective-permute-done.5.refs_6_), channel_id=1, source_target_pairs={{0,24},{2,26},{4,28},{6,30},{8,0},{10,2},{12,4},{14,6},{16,8},{18,... | collective-permute-start | bytes 1572872 | tf_op jit(solution)/shard_map/ppermute | solution.py:35
  62.3 8.5 %collective-permute-done.8.refs_8_ = bf16[1024,256]{1,0:T(8,128)(2,1)S(1)} collective-permute-done((bf16[1024,256]{1,0:T(8,128)(2,1)S(1)}, bf16[1024,256]{1,0:T(8,128)(2,1)S(1)}, u32[]{:S(2)}, u32[]{:S(2)}) %collective-permute-start.8) | collective-permute-done | bytes 524320 | tf_op jit(solution)/shard_map/ppermute | solution.py:35
  71.1 2.3 %collective-permute-start.4 = (bf16[1024,256]{1,0:T(8,128)(2,1)S(1)}, bf16[1024,256]{1,0:T(8,128)(2,1)S(1)}, u32[]{:S(2)}, u32[]{:S(2)}) collective-permute-start(bf16[1024,256]{1,0:T(8,128)(2,1)S(1)} %collective-permute-done.3.refs_4_), channel_id=1, source_target_pairs={{0,2},{2,0},{4,6},{6,4},{8,10},{10,8},{12,14},{14,12},{16,18},{18,... | collective-permute-start | bytes 1572872 | tf_op jit(solution)/shard_map/ppermute | solution.py:39
  73.4 2.6 %collective-permute-done.25.refs_25_ = bf16[512,256]{1,0:T(8,128)(2,1)S(1)} collective-permute-done((bf16[512,256]{1,0:T(8,128)(2,1)S(1)}, bf16[512,256]{1,0:T(8,128)(2,1)S(1)}, u32[]{:S(2)}, u32[]{:S(2)}) %collective-permute-start.25) | collective-permute-done | bytes 262176 | tf_op jit(solution)/shard_map/ppermute | solution.py:24
  76.0 3.5 %collective-permute-start.6 = (bf16[1024,256]{1,0:T(8,128)(2,1)S(1)}, bf16[1024,256]{1,0:T(8,128)(2,1)S(1)}, u32[]{:S(2)}, u32[]{:S(2)}) collective-permute-start(bf16[1024,256]{1,0:T(8,128)(2,1)S(1)} %collective-permute-done.5.refs_6_), channel_id=1, source_target_pairs={{0,2},{2,0},{4,6},{6,4},{8,10},{10,8},{12,14},{14,12},{16,18},{18,... | collective-permute-start | bytes 1572872 | tf_op jit(solution)/shard_map/ppermute | solution.py:39
  79.5 0.5 collective-permute-start.9
  80.1 0.9 collective-permute-done.6.refs_7_
  81.1 0.7 collective-permute-done.14.refs_15_
  81.8 0.7 collective-permute-done.9.refs_9_
  82.6 0.7 collective-permute-done.11.refs_11_
  83.3 2.8 %rows_other.1 = (f32[512,512]{1,0:T(8,128)S(1)}, f32[8,512]{1,0:T(8,128)S(1)}) custom-call(bf16[1024,256]{1,0:T(8,128)(2,1)S(1)} %mask_ham.1.refs_0_, bf16[1024,256]{1,0:T(8,128)(2,1)S(1)} %collective-permute-done.refs_1_, bf16[1024,256]{1,0:T(8,128)(2,1)S(1)} %collective-permute-done.1.refs_2_, bf16[1024,256]{1,0:T(8,128)(2,1)S(1)} %collective-permute-done.2.refs_3_, ...), custom_call_target="tpu_custom_call" | custom-call | flops 2147483648 | bytes 8388608 | tf_op jit(solution)/shard_map/rows_other/pallas_call | solution.py:146
  86.2 2.5 %collective-permute-start.30 = (f32[8,512]{1,0:T(8,128)S(1)}, f32[8,512]{1,0:T(8,128)S(1)}, u32[]{:S(2)}, u32[]{:S(2)}) collective-permute-start(f32[8,512]{1,0:T(8,128)S(1)} %get-tuple-element.13), channel_id=1, source_target_pairs={{0,1},{1,0},{2,3},{3,2},{4,5},{5,4},{6,7},{7,6},{8,9},{9,8},{10,11... | collective-permute-start | bytes 49160 | tf_op jit(solution)/shard_map/ppermute | solution.py:43
  88.6 2.8 %rows_own.1 = (f32[512,512]{1,0:T(8,128)S(1)}, f32[8,512]{1,0:T(8,128)S(1)}) custom-call(bf16[1024,256]{1,0:T(8,128)(2,1)S(1)} %mask_ham.1.refs_0_, bf16[1024,256]{1,0:T(8,128)(2,1)S(1)} %collective-permute-done.refs_1_, bf16[1024,256]{1,0:T(8,128)(2,1)S(1)} %collective-permute-done.1.refs_2_, bf16[1024,256]{1,0:T(8,128)(2,1)S(1)} %collective-permute-done.2.refs_3_, ...), custom_call_target="tpu_custom_call" | custom-call | flops 2147483648 | bytes 8388608 | tf_op jit(solution)/shard_map/rows_own/pallas_call | solution.py:146
  91.5 1.0 collective-permute-start.31
  92.5 0.8 collective-permute-done.31
  93.3 2.3 %collective-permute-start.29 = (f32[512,512]{1,0:T(8,128)S(1)}, f32[512,512]{1,0:T(8,128)}, u32[]{:S(2)}, u32[]{:S(2)}) collective-permute-start(f32[512,512]{1,0:T(8,128)S(1)} %get-tuple-element.11), channel_id=1, source_target_pairs={{0,1},{1,0},{2,3},{3,2},{4,5},{5,4},{6,7},{7,6},{8,9},{9,8},{10,11... | collective-permute-start | bytes 3145736 | tf_op jit(solution)/shard_map/ppermute | solution.py:43
  96.0 3.0 %collective-permute-done.33 = f32[8,512]{1,0:T(8,128)S(1)} collective-permute-done((f32[8,512]{1,0:T(8,128)S(1)}, f32[8,512]{1,0:T(8,128)S(1)}, u32[]{:S(2)}, u32[]{:S(2)}) %collective-permute-start.33) | collective-permute-done | bytes 16416 | tf_op jit(solution)/shard_map/ppermute | solution.py:39
  99.0 4.4 %collective-permute-done.34 = f32[8,512]{1,0:T(8,128)S(1)} collective-permute-done((f32[8,512]{1,0:T(8,128)S(1)}, f32[8,512]{1,0:T(8,128)S(1)}, u32[]{:S(2)}, u32[]{:S(2)}) %collective-permute-start.34) | collective-permute-done | bytes 16416 | tf_op jit(solution)/shard_map/ppermute | solution.py:39
  104.1 1.0 collective-permute-start.35
  105.1 12.6 %collective-permute-done.35 = f32[16,128]{1,0:T(8,128)S(1)} collective-permute-done((f32[16,128]{1,0:T(8,128)S(1)}, f32[16,128]{1,0:T(8,128)S(1)}, u32[]{:S(2)}, u32[]{:S(2)}) %collective-permute-start.35) | collective-permute-done | bytes 8224 | tf_op jit(solution)/shard_map/ppermute | solution.py:224
  117.7 0.6 pad_maximum_fusion
  118.3 1.4 %collective-permute-done.29 = f32[512,512]{1,0:T(8,128)} collective-permute-done((f32[512,512]{1,0:T(8,128)S(1)}, f32[512,512]{1,0:T(8,128)}, u32[]{:S(2)}, u32[]{:S(2)}) %collective-permute-start.29) | collective-permute-done | bytes 1048608 | tf_op jit(solution)/shard_map/ppermute | solution.py:43
  119.7 2.2 %add_convert_fusion = bf16[512,512]{1,0:T(8,128)(2,1)} fusion(f32[512,512]{1,0:T(8,128)S(1)} %get-tuple-element.10, f32[512,512]{1,0:T(8,128)} %collective-permute-done.29), kind=kLoop, calls=%fused_computation.1 | loop fusion | flops 524288 | bytes 2621440 | tf_op jit(solution)/shard_map/convert_element_type | solution.py:207
  (54 shorter events, 1.9 us)
Async XLA Ops:
  0.6 102.9 %copy-start = (bf16[64,16,128]{2,1,0:T(8,128)(2,1)S(1)}, bf16[64,16,128]{2,1,0:T(8,128)(2,1)}, u32[]{:S(2)}) copy-start(bf16[64,16,128]{2,1,0:T(8,128)(2,1)} %param.10) | copy-start | bytes 786436
  0.6 1.1 copy-start.1
  1.7 0.7 copy-start.3
  2.4 2.9 %copy-start.4 = (s32[16,4]{0,1:T(4,128)S(1)}, s32[16,4]{0,1:T(4,128)}, u32[]{:S(2)}) copy-start(s32[16,4]{0,1:T(4,128)} %param.8) | copy-start | bytes 772
  2.4 3.0 %copy-start.2 = (bf16[1024,256]{1,0:T(8,128)(2,1)S(1)}, bf16[1024,256]{1,0:T(8,128)(2,1)}, u32[]{:S(2)}) copy-start(bf16[1024,256]{1,0:T(8,128)(2,1)} %ham_ref.1) | copy-start | bytes 1572868
  2.8 12.5 %collective-permute-start.21 = (bf16[512,256]{1,0:T(8,128)(2,1)S(1)}, bf16[512,256]{1,0:T(8,128)(2,1)S(1)}, u32[]{:S(2)}, u32[]{:S(2)}) collective-permute-start(bf16[512,256]{1,0:T(8,128)(2,1)S(1)} %get-tuple-element.8.refs_16_), channel_id=1, source_target_pairs={{0,32},{32,64},{64,96},{96,128},{128,160},{160,192},{192,224},{224... | collective-permute-start | bytes 786440 | tf_op jit(solution)/shard_map/ppermute | solution.py:24
  5.9 21.2 %collective-permute-start.1 = (bf16[1024,256]{1,0:T(8,128)(2,1)S(1)}, bf16[1024,256]{1,0:T(8,128)(2,1)S(1)}, u32[]{:S(2)}, u32[]{:S(2)}) collective-permute-start(bf16[1024,256]{1,0:T(8,128)(2,1)S(1)} %mask_ham.1.refs_0_), channel_id=1, source_target_pairs={{0,4},{2,6},{4,0},{6,2},{8,12},{10,14},{12,8},{14,10},{16,20},{18,... | collective-permute-start | bytes 1572872 | tf_op jit(solution)/shard_map/ppermute | solution.py:39
  7.2 23.0 %collective-permute-start.7 = (bf16[1024,256]{1,0:T(8,128)(2,1)S(1)}, bf16[1024,256]{1,0:T(8,128)(2,1)S(1)}, u32[]{:S(2)}, u32[]{:S(2)}) collective-permute-start(bf16[1024,256]{1,0:T(8,128)(2,1)S(1)} %mask_ham.1.refs_0_), channel_id=1, source_target_pairs={{0,8},{2,10},{4,12},{6,14},{8,16},{10,18},{12,20},{14,22},{16,24},... | collective-permute-start | bytes 1572872 | tf_op jit(solution)/shard_map/ppermute | solution.py:35
  8.5 8.8 %collective-permute-start.16 = (bf16[512,256]{1,0:T(8,128)(2,1)S(1)}, bf16[512,256]{1,0:T(8,128)(2,1)S(1)}, u32[]{:S(2)}, u32[]{:S(2)}) collective-permute-start(bf16[512,256]{1,0:T(8,128)(2,1)S(1)} %get-tuple-element.9.refs_17_), channel_id=1, source_target_pairs={{0,224},{32,0},{64,32},{96,64},{128,96},{160,128},{192,160},{224,1... | collective-permute-start | bytes 786440 | tf_op jit(solution)/shard_map/ppermute | solution.py:24
  12.9 10.0 %collective-permute-start.15 = (bf16[512,256]{1,0:T(8,128)(2,1)S(1)}, bf16[512,256]{1,0:T(8,128)(2,1)S(1)}, u32[]{:S(2)}, u32[]{:S(2)}) collective-permute-start(bf16[512,256]{1,0:T(8,128)(2,1)S(1)} %get-tuple-element.8.refs_16_), channel_id=1, source_target_pairs={{0,224},{32,0},{64,32},{96,64},{128,96},{160,128},{192,160},{224,1... | collective-permute-start | bytes 786440 | tf_op jit(solution)/shard_map/ppermute | solution.py:24
  15.3 9.0 %collective-permute-start.26 = (bf16[512,256]{1,0:T(8,128)(2,1)S(1)}, bf16[512,256]{1,0:T(8,128)(2,1)S(1)}, u32[]{:S(2)}, u32[]{:S(2)}) collective-permute-start(bf16[512,256]{1,0:T(8,128)(2,1)S(1)} %get-tuple-element.9.refs_17_), channel_id=1, source_target_pairs={{0,32},{32,64},{64,96},{96,128},{128,160},{160,192},{192,224},{224... | collective-permute-start | bytes 786440 | tf_op jit(solution)/shard_map/ppermute | solution.py:24
  17.2 13.0 %collective-permute-start.22 = (bf16[512,256]{1,0:T(8,128)(2,1)S(1)}, bf16[512,256]{1,0:T(8,128)(2,1)S(1)}, u32[]{:S(2)}, u32[]{:S(2)}) collective-permute-start(bf16[512,256]{1,0:T(8,128)(2,1)S(1)} %collective-permute-done.21.refs_30_), channel_id=1, source_target_pairs={{0,32},{32,64},{64,96},{96,128},{128,160},{160,192},{192,224},{224... | collective-permute-start | bytes 786440 | tf_op jit(solution)/shard_map/ppermute | solution.py:24
  22.9 23.5 %collective-permute-start.3 = (bf16[1024,256]{1,0:T(8,128)(2,1)S(1)}, bf16[1024,256]{1,0:T(8,128)(2,1)S(1)}, u32[]{:S(2)}, u32[]{:S(2)}) collective-permute-start(bf16[1024,256]{1,0:T(8,128)(2,1)S(1)} %mask_ham.1.refs_0_), channel_id=1, source_target_pairs={{0,24},{2,26},{4,28},{6,30},{8,0},{10,2},{12,4},{14,6},{16,8},{18,... | collective-permute-start | bytes 1572872 | tf_op jit(solution)/shard_map/ppermute | solution.py:35
  24.4 22.0 %collective-permute-start = (bf16[1024,256]{1,0:T(8,128)(2,1)S(1)}, bf16[1024,256]{1,0:T(8,128)(2,1)S(1)}, u32[]{:S(2)}, u32[]{:S(2)}) collective-permute-start(bf16[1024,256]{1,0:T(8,128)(2,1)S(1)} %mask_ham.1.refs_0_), channel_id=1, source_target_pairs={{0,2},{2,0},{4,6},{6,4},{8,10},{10,8},{12,14},{14,12},{16,18},{18,... | collective-permute-start | bytes 1572872 | tf_op jit(solution)/shard_map/ppermute | solution.py:39
  27.0 8.8 %collective-permute-start.18 = (bf16[512,256]{1,0:T(8,128)(2,1)S(1)}, bf16[512,256]{1,0:T(8,128)(2,1)S(1)}, u32[]{:S(2)}, u32[]{:S(2)}) collective-permute-start(bf16[512,256]{1,0:T(8,128)(2,1)S(1)} %collective-permute-done.16.refs_19_), channel_id=1, source_target_pairs={{0,224},{32,0},{64,32},{96,64},{128,96},{160,128},{192,160},{224,1... | collective-permute-start | bytes 786440 | tf_op jit(solution)/shard_map/ppermute | solution.py:24
  30.2 11.3 %collective-permute-start.17 = (bf16[512,256]{1,0:T(8,128)(2,1)S(1)}, bf16[512,256]{1,0:T(8,128)(2,1)S(1)}, u32[]{:S(2)}, u32[]{:S(2)}) collective-permute-start(bf16[512,256]{1,0:T(8,128)(2,1)S(1)} %collective-permute-done.15.refs_18_), channel_id=1, source_target_pairs={{0,224},{32,0},{64,32},{96,64},{128,96},{160,128},{192,160},{224,1... | collective-permute-start | bytes 786440 | tf_op jit(solution)/shard_map/ppermute | solution.py:24
  30.3 14.6 %collective-permute-start.27 = (bf16[512,256]{1,0:T(8,128)(2,1)S(1)}, bf16[512,256]{1,0:T(8,128)(2,1)S(1)}, u32[]{:S(2)}, u32[]{:S(2)}) collective-permute-start(bf16[512,256]{1,0:T(8,128)(2,1)S(1)} %collective-permute-done.26.refs_31_), channel_id=1, source_target_pairs={{0,32},{32,64},{64,96},{96,128},{128,160},{160,192},{192,224},{224... | collective-permute-start | bytes 786440 | tf_op jit(solution)/shard_map/ppermute | solution.py:24
  35.9 10.6 %collective-permute-start.23 = (bf16[512,256]{1,0:T(8,128)(2,1)S(1)}, bf16[512,256]{1,0:T(8,128)(2,1)S(1)}, u32[]{:S(2)}, u32[]{:S(2)}) collective-permute-start(bf16[512,256]{1,0:T(8,128)(2,1)S(1)} %collective-permute-done.22.refs_28_), channel_id=1, source_target_pairs={{0,32},{32,64},{64,96},{96,128},{128,160},{160,192},{192,224},{224... | collective-permute-start | bytes 786440 | tf_op jit(solution)/shard_map/ppermute | solution.py:24
  41.5 8.2 %collective-permute-start.20 = (bf16[512,256]{1,0:T(8,128)(2,1)S(1)}, bf16[512,256]{1,0:T(8,128)(2,1)S(1)}, u32[]{:S(2)}, u32[]{:S(2)}) collective-permute-start(bf16[512,256]{1,0:T(8,128)(2,1)S(1)} %collective-permute-done.18.refs_21_), channel_id=1, source_target_pairs={{0,224},{32,0},{64,32},{96,64},{128,96},{160,128},{192,160},{224,1... | collective-permute-start | bytes 786440 | tf_op jit(solution)/shard_map/ppermute | solution.py:24
  44.9 15.9 %collective-permute-start.5 = (bf16[1024,256]{1,0:T(8,128)(2,1)S(1)}, bf16[1024,256]{1,0:T(8,128)(2,1)S(1)}, u32[]{:S(2)}, u32[]{:S(2)}) collective-permute-start(bf16[1024,256]{1,0:T(8,128)(2,1)S(1)} %collective-permute-done.1.refs_2_), channel_id=1, source_target_pairs={{0,24},{2,26},{4,28},{6,30},{8,0},{10,2},{12,4},{14,6},{16,8},{18,... | collective-permute-start | bytes 1572872 | tf_op jit(solution)/shard_map/ppermute | solution.py:35
  46.4 15.9 %collective-permute-start.13 = (bf16[1024,256]{1,0:T(8,128)(2,1)S(1)}, bf16[1024,256]{1,0:T(8,128)(2,1)S(1)}, u32[]{:S(2)}, u32[]{:S(2)}) collective-permute-start(bf16[1024,256]{1,0:T(8,128)(2,1)S(1)} %collective-permute-done.1.refs_2_), channel_id=1, source_target_pairs={{0,8},{2,10},{4,12},{6,14},{8,16},{10,18},{12,20},{14,22},{16,24},... | collective-permute-start | bytes 1572872 | tf_op jit(solution)/shard_map/ppermute | solution.py:35
  46.4 24.4 %collective-permute-start.8 = (bf16[1024,256]{1,0:T(8,128)(2,1)S(1)}, bf16[1024,256]{1,0:T(8,128)(2,1)S(1)}, u32[]{:S(2)}, u32[]{:S(2)}) collective-permute-start(bf16[1024,256]{1,0:T(8,128)(2,1)S(1)} %collective-permute-done.7.refs_12_), channel_id=1, source_target_pairs={{0,8},{2,10},{4,12},{6,14},{8,16},{10,18},{12,20},{14,22},{16,24},... | collective-permute-start | bytes 1572872 | tf_op jit(solution)/shard_map/ppermute | solution.py:35
  46.5 8.8 %collective-permute-start.19 = (bf16[512,256]{1,0:T(8,128)(2,1)S(1)}, bf16[512,256]{1,0:T(8,128)(2,1)S(1)}, u32[]{:S(2)}, u32[]{:S(2)}) collective-permute-start(bf16[512,256]{1,0:T(8,128)(2,1)S(1)} %collective-permute-done.17.refs_20_), channel_id=1, source_target_pairs={{0,224},{32,0},{64,32},{96,64},{128,96},{160,128},{192,160},{224,1... | collective-permute-start | bytes 786440 | tf_op jit(solution)/shard_map/ppermute | solution.py:24
  49.7 7.5 %collective-permute-start.28 = (bf16[512,256]{1,0:T(8,128)(2,1)S(1)}, bf16[512,256]{1,0:T(8,128)(2,1)S(1)}, u32[]{:S(2)}, u32[]{:S(2)}) collective-permute-start(bf16[512,256]{1,0:T(8,128)(2,1)S(1)} %collective-permute-done.27.refs_29_), channel_id=1, source_target_pairs={{0,32},{32,64},{64,96},{96,128},{128,160},{160,192},{192,224},{224... | collective-permute-start | bytes 786440 | tf_op jit(solution)/shard_map/ppermute | solution.py:24
  55.3 24.3 %collective-permute-start.2 = (bf16[1024,256]{1,0:T(8,128)(2,1)S(1)}, bf16[1024,256]{1,0:T(8,128)(2,1)S(1)}, u32[]{:S(2)}, u32[]{:S(2)}) collective-permute-start(bf16[1024,256]{1,0:T(8,128)(2,1)S(1)} %collective-permute-done.1.refs_2_), channel_id=1, source_target_pairs={{0,2},{2,0},{4,6},{6,4},{8,10},{10,8},{12,14},{14,12},{16,18},{18,... | collective-permute-start | bytes 1572872 | tf_op jit(solution)/shard_map/ppermute | solution.py:39
  57.1 22.4 %collective-permute-start.12 = (bf16[1024,256]{1,0:T(8,128)(2,1)S(1)}, bf16[1024,256]{1,0:T(8,128)(2,1)S(1)}, u32[]{:S(2)}, u32[]{:S(2)}) collective-permute-start(bf16[1024,256]{1,0:T(8,128)(2,1)S(1)} %collective-permute-done.7.refs_12_), channel_id=1, source_target_pairs={{0,2},{2,0},{4,6},{6,4},{8,10},{10,8},{12,14},{14,12},{16,18},{18,... | collective-permute-start | bytes 1572872 | tf_op jit(solution)/shard_map/ppermute | solution.py:39
  60.8 19.3 %collective-permute-start.10 = (bf16[1024,256]{1,0:T(8,128)(2,1)S(1)}, bf16[1024,256]{1,0:T(8,128)(2,1)S(1)}, u32[]{:S(2)}, u32[]{:S(2)}) collective-permute-start(bf16[1024,256]{1,0:T(8,128)(2,1)S(1)} %collective-permute-done.5.refs_6_), channel_id=1, source_target_pairs={{0,24},{2,26},{4,28},{6,30},{8,0},{10,2},{12,4},{14,6},{16,8},{18,... | collective-permute-start | bytes 1572872 | tf_op jit(solution)/shard_map/ppermute | solution.py:35
  62.3 8.8 %collective-permute-start.24 = (bf16[512,256]{1,0:T(8,128)(2,1)S(1)}, bf16[512,256]{1,0:T(8,128)(2,1)S(1)}, u32[]{:S(2)}, u32[]{:S(2)}) collective-permute-start(bf16[512,256]{1,0:T(8,128)(2,1)S(1)} %collective-permute-done.23.refs_26_), channel_id=1, source_target_pairs={{0,32},{32,64},{64,96},{96,128},{128,160},{160,192},{192,224},{224... | collective-permute-start | bytes 786440 | tf_op jit(solution)/shard_map/ppermute | solution.py:24
  70.8 5.2 %collective-permute-start.25 = (bf16[512,256]{1,0:T(8,128)(2,1)S(1)}, bf16[512,256]{1,0:T(8,128)(2,1)S(1)}, u32[]{:S(2)}, u32[]{:S(2)}) collective-permute-start(bf16[512,256]{1,0:T(8,128)(2,1)S(1)} %collective-permute-done.20.refs_23_), channel_id=1, source_target_pairs={{0,224},{32,0},{64,32},{96,64},{128,96},{160,128},{192,160},{224,1... | collective-permute-start | bytes 786440 | tf_op jit(solution)/shard_map/ppermute | solution.py:24
  71.1 9.1 %collective-permute-start.4 = (bf16[1024,256]{1,0:T(8,128)(2,1)S(1)}, bf16[1024,256]{1,0:T(8,128)(2,1)S(1)}, u32[]{:S(2)}, u32[]{:S(2)}) collective-permute-start(bf16[1024,256]{1,0:T(8,128)(2,1)S(1)} %collective-permute-done.3.refs_4_), channel_id=1, source_target_pairs={{0,2},{2,0},{4,6},{6,4},{8,10},{10,8},{12,14},{14,12},{16,18},{18,... | collective-permute-start | bytes 1572872 | tf_op jit(solution)/shard_map/ppermute | solution.py:39
  76.0 5.0 %collective-permute-start.6 = (bf16[1024,256]{1,0:T(8,128)(2,1)S(1)}, bf16[1024,256]{1,0:T(8,128)(2,1)S(1)}, u32[]{:S(2)}, u32[]{:S(2)}) collective-permute-start(bf16[1024,256]{1,0:T(8,128)(2,1)S(1)} %collective-permute-done.5.refs_6_), channel_id=1, source_target_pairs={{0,2},{2,0},{4,6},{6,4},{8,10},{10,8},{12,14},{14,12},{16,18},{18,... | collective-permute-start | bytes 1572872 | tf_op jit(solution)/shard_map/ppermute | solution.py:39
  79.5 2.3 %collective-permute-start.14 = (bf16[1024,256]{1,0:T(8,128)(2,1)S(1)}, bf16[1024,256]{1,0:T(8,128)(2,1)S(1)}, u32[]{:S(2)}, u32[]{:S(2)}) collective-permute-start(bf16[1024,256]{1,0:T(8,128)(2,1)S(1)} %collective-permute-done.13.refs_14_), channel_id=1, source_target_pairs={{0,2},{2,0},{4,6},{6,4},{8,10},{10,8},{12,14},{14,12},{16,18},{18,... | collective-permute-start | bytes 1572872 | tf_op jit(solution)/shard_map/ppermute | solution.py:39
  79.5 3.0 %collective-permute-start.9 = (bf16[1024,256]{1,0:T(8,128)(2,1)S(1)}, bf16[1024,256]{1,0:T(8,128)(2,1)S(1)}, u32[]{:S(2)}, u32[]{:S(2)}) collective-permute-start(bf16[1024,256]{1,0:T(8,128)(2,1)S(1)} %collective-permute-done.8.refs_8_), channel_id=1, source_target_pairs={{0,2},{2,0},{4,6},{6,4},{8,10},{10,8},{12,14},{14,12},{16,18},{18,... | collective-permute-start | bytes 1572872 | tf_op jit(solution)/shard_map/ppermute | solution.py:39
  80.1 3.3 %collective-permute-start.11 = (bf16[1024,256]{1,0:T(8,128)(2,1)S(1)}, bf16[1024,256]{1,0:T(8,128)(2,1)S(1)}, u32[]{:S(2)}, u32[]{:S(2)}) collective-permute-start(bf16[1024,256]{1,0:T(8,128)(2,1)S(1)} %collective-permute-done.10.refs_10_), channel_id=1, source_target_pairs={{0,2},{2,0},{4,6},{6,4},{8,10},{10,8},{12,14},{14,12},{16,18},{18,... | collective-permute-start | bytes 1572872 | tf_op jit(solution)/shard_map/ppermute | solution.py:39
  86.2 5.3 %collective-permute-start.30 = (f32[8,512]{1,0:T(8,128)S(1)}, f32[8,512]{1,0:T(8,128)S(1)}, u32[]{:S(2)}, u32[]{:S(2)}) collective-permute-start(f32[8,512]{1,0:T(8,128)S(1)} %get-tuple-element.13), channel_id=1, source_target_pairs={{0,1},{1,0},{2,3},{3,2},{4,5},{5,4},{6,7},{7,6},{8,9},{9,8},{10,11... | collective-permute-start | bytes 49160 | tf_op jit(solution)/shard_map/ppermute | solution.py:43
  91.5 1.8 %collective-permute-start.31 = (f32[8,512]{1,0:T(8,128)S(1)}, f32[8,512]{1,0:T(8,128)S(1)}, u32[]{:S(2)}, u32[]{:S(2)}) collective-permute-start(f32[8,512]{1,0:T(8,128)S(1)} %add.42), channel_id=1, source_target_pairs={{0,2},{2,0},{4,6},{6,4},{8,10},{10,8},{12,14},{14,12},{16,18},{18,... | collective-permute-start | bytes 49160 | tf_op jit(solution)/shard_map/ppermute | solution.py:39
  93.3 2.6 %collective-permute-start.32 = (f32[8,512]{1,0:T(8,128)S(1)}, f32[8,512]{1,0:T(8,128)S(1)}, u32[]{:S(2)}, u32[]{:S(2)}) collective-permute-start(f32[8,512]{1,0:T(8,128)S(1)} %add.43), channel_id=1, source_target_pairs={{0,4},{2,6},{4,0},{6,2},{8,12},{10,14},{12,8},{14,10},{16,20},{18,... | collective-permute-start | bytes 49160 | tf_op jit(solution)/shard_map/ppermute | solution.py:39
  93.3 26.4 %collective-permute-start.29 = (f32[512,512]{1,0:T(8,128)S(1)}, f32[512,512]{1,0:T(8,128)}, u32[]{:S(2)}, u32[]{:S(2)}) collective-permute-start(f32[512,512]{1,0:T(8,128)S(1)} %get-tuple-element.11), channel_id=1, source_target_pairs={{0,1},{1,0},{2,3},{3,2},{4,5},{5,4},{6,7},{7,6},{8,9},{9,8},{10,11... | collective-permute-start | bytes 3145736 | tf_op jit(solution)/shard_map/ppermute | solution.py:43
  95.9 3.0 %copy-start.5 = (s32[8]{0:T(128)S(1)}, s32[8]{0:T(128)}, u32[]{:S(2)}) copy-start(s32[8]{0:T(128)} %param.11) | copy-start | bytes 100
  95.9 3.0 %collective-permute-start.33 = (f32[8,512]{1,0:T(8,128)S(1)}, f32[8,512]{1,0:T(8,128)S(1)}, u32[]{:S(2)}, u32[]{:S(2)}) collective-permute-start(f32[8,512]{1,0:T(8,128)S(1)} %add.44), channel_id=1, source_target_pairs={{0,8},{2,10},{4,12},{6,14},{8,0},{10,2},{12,4},{14,6},{16,24},{18,... | collective-permute-start | bytes 49160 | tf_op jit(solution)/shard_map/ppermute | solution.py:39
  98.9 4.5 %collective-permute-start.34 = (f32[8,512]{1,0:T(8,128)S(1)}, f32[8,512]{1,0:T(8,128)S(1)}, u32[]{:S(2)}, u32[]{:S(2)}) collective-permute-start(f32[8,512]{1,0:T(8,128)S(1)} %add.45), channel_id=1, source_target_pairs={{0,16},{2,18},{4,20},{6,22},{8,24},{10,26},{12,28},{14,30},{16,0},... | collective-permute-start | bytes 49160 | tf_op jit(solution)/shard_map/ppermute | solution.py:39
  104.1 13.6 %collective-permute-start.35 = (f32[16,128]{1,0:T(8,128)S(1)}, f32[16,128]{1,0:T(8,128)S(1)}, u32[]{:S(2)}, u32[]{:S(2)}) collective-permute-start(f32[16,128]{1,0:T(8,128)S(1)} %slice.22), channel_id=1, source_target_pairs={{0,1},{1,32},{32,33},{33,64},{64,65},{65,96},{96,97},{97,128},{128... | collective-permute-start | bytes 24584 | tf_op jit(solution)/shard_map/ppermute | solution.py:224

commit v2 on v0

v2 whole, which is shorter than its diff:
```python
import functools
import math

import jax
import jax.numpy as jnp
from jax import lax
from jax.experimental import pallas as pl
from jax.experimental.pallas import tpu as pltpu
from jax.sharding import PartitionSpec as P

SX = 32
TX = 16
BLK = 64
MIB = 1 << 20

NZ = 8
NY = 4
F32 = jnp.float32
BF16 = jnp.bfloat16
FIRST = 256


def way(core):
    return 1 - 2 * core


def over_row(value, steps):
    pairs = []
    for r in range(NZ):
        for c in range(4 * NY):
            target = (r + way(c % 2) * steps) % NZ
            pairs.append((r * 4 * NY + c, target * 4 * NY + c))
    return lax.ppermute(value, ("row", "col"), pairs)


def over_y(value, steps):
    pairs = []
    for c in range(4 * NY):
        pairs.append((c, ((c // 4 + way(c % 2) * steps) % NY) * 4 + c % 4))
    return lax.ppermute(value, "col", pairs)


def straight_y(value, steps):
    pairs = [(c, ((c // 4 + steps) % NY) * 4 + c % 4) for c in range(4 * NY)]
    return lax.ppermute(value, "col", pairs)


def col_swap(value, bit):
    return lax.ppermute(value, "col", [(c, c ^ bit) for c in range(4 * NY)])


def rep_swap(value):
    return lax.ppermute(value, "rep", [(0, 1), (1, 0)])


def over_x(value, steps):
    pairs = []
    for c in range(4 * NY):
        for p in range(2):
            x = (2 * p + (c // 2) % 2 + steps) % 4
            pairs.append((c * 2 + p, (c + 2 * (x % 2 - (c // 2) % 2)) * 2 + x // 2))
    return lax.ppermute(value, ("col", "rep"), pairs)


def spread(pattern_ref, rows, cols):
    pattern = pattern_ref[...].astype(F32).astype(BF16)
    rows_b, cols_b = pattern.shape
    left = (
        lax.broadcasted_iota(jnp.int32, (rows, rows_b), 0) // BLK
        == lax.broadcasted_iota(jnp.int32, (rows, rows_b), 1)
    )
    right = (
        lax.broadcasted_iota(jnp.int32, (cols_b, cols), 1) // BLK
        == lax.broadcasted_iota(jnp.int32, (cols_b, cols), 0)
    )
    wide = jnp.dot(pattern, right.astype(F32).astype(BF16), preferred_element_type=F32)
    return jnp.dot(
        left.astype(F32).astype(BF16), wide.astype(BF16), preferred_element_type=F32
    ).astype(BF16)


def mask_kernel(pattern_ref, matrix_ref, out_ref, *sums_refs):
    rows, cols = matrix_ref.shape
    masked = matrix_ref[...] * spread(pattern_ref, rows, cols)
    out_ref[...] = masked
    for ref in sums_refs:
        ref[...] = lax.dot_general(
            jnp.ones((8, cols), BF16), masked, (((1,), (1,)), ((), ())), preferred_element_type=F32
        )


def masked(name, pattern, matrix, with_sums=False):
    shapes = [jax.ShapeDtypeStruct(matrix.shape, BF16)]
    if with_sums:
        shapes.append(jax.ShapeDtypeStruct((8, matrix.shape[0]), F32))
    return pl.pallas_call(
        mask_kernel,
        out_shape=shapes,
        compiler_params=pltpu.CompilerParams(vmem_limit_bytes=12 * MIB),
        name=name,
    )(pattern, matrix)


def place():
    row = lax.axis_index("row")
    col = lax.axis_index("col")
    return row, col // 4, (col // 2) % 2, col % 2, lax.axis_index("rep")


def split_dot(wide, narrow):
    total = None
    for _ in range(3):
        piece = wide.astype(BF16)
        wide = wide - piece.astype(F32)
        term = lax.dot_general(
            piece, narrow, (((1,), (1,)), ((), ())), preferred_element_type=F32
        )
        total = term if total is None else total + term
    return total


def row_sums(ref):
    lanes = 128
    folded = ref[:, :lanes]
    for j in range(lanes, ref.shape[1], lanes):
        folded += ref[:, j : j + lanes]
    return lax.dot_general(
        jnp.ones((8, lanes), F32),
        folded,
        (((1,), (1,)), ((), ())),
        precision=lax.Precision.HIGHEST,
        preferred_element_type=F32,
    )


def early_kernel(*refs):
    n_ham, n_den = len(HAM_KEYS), len(DEN_KEYS) - 1
    ham_refs, den_refs, far_ref = refs[:n_ham], refs[n_ham : n_ham + n_den], refs[n_ham + n_den]
    other_ref, own_ref, ham_far_ref, sums_ref, den_buf = refs[n_ham + n_den + 1 :]
    row, y, x, core, rep = place()
    rows = own_ref.shape[0]
    for n in range(n_den):
        den_buf[lax.rem(row + way(core) * DEN_KEYS[n] + NZ, NZ)] = den_refs[n][...]
    far = lax.rem(row + NZ // 2, NZ)
    den_buf[far] = jnp.zeros(den_buf.shape[1:], BF16)
    half_size = den_buf.shape[1] // 2
    starts = [pl.multiple_of((1 - rep) * rows, rows), pl.multiple_of(rep * rows, rows)]
    for n, (dy, dx, dk) in enumerate(HAM_KEYS):
        half = core + dk - 2 * core * dk
        chip = lax.rem(y + way(half) * dy + NY, NY) * 2 + (x + dx - 2 * x * dx)
        block = ham_refs[n]

        @pl.when(chip == far)
        def _():
            ham_far_ref[half] = block[...]

        den = den_buf[chip, pl.ds(pl.multiple_of(half * half_size, half_size), half_size), :]
        for start, out_ref in zip(starts, (other_ref, own_ref)):
            term = jnp.dot(block[pl.ds(start, rows), :], den, preferred_element_type=F32)
            if n == 0:
                out_ref[...] = term
            else:
                out_ref[...] += term
    far_sums = split_dot(far_ref[:, :half_size], ham_far_ref[0])
    far_sums += split_dot(far_ref[:, half_size:], ham_far_ref[1])
    sums_ref[...] = far_sums
    for start, out_ref in zip(starts, (other_ref, own_ref)):
        sums_ref[:, pl.ds(start, rows)] += row_sums(out_ref)


def early(ham_blocks, den_blocks, far_sums):
    rows, half = ham_blocks[0].shape
    depth, cols = den_blocks[0].shape
    n = len(ham_blocks) + len(den_blocks) + 1
    return pl.pallas_call(
        early_kernel,
        out_shape=(
            jax.ShapeDtypeStruct((rows // 2, cols), F32),
            jax.ShapeDtypeStruct((rows // 2, cols), F32),
            jax.ShapeDtypeStruct((2, rows, half), BF16),
            jax.ShapeDtypeStruct((8, rows), F32),
        ),
        in_specs=[pl.BlockSpec(memory_space=pltpu.VMEM)] * n,
        scratch_shapes=[pltpu.VMEM((NZ, depth, cols), BF16)],
        compiler_params=pltpu.CompilerParams(vmem_limit_bytes=12 * MIB),
        cost_estimate=pl.CostEstimate(
            flops=2 * rows * cols * depth * NZ, bytes_accessed=4 * MIB, transcendentals=0
        ),
        name="early",
    )(*ham_blocks, *den_blocks, far_sums)


def late_kernel(other_ref, own_ref, ham_ref, den_ref, first_out, second_out, own_out):
    rep = lax.axis_index("rep")
    rows = own_out.shape[0]
    half = ham_ref.shape[2]
    cut = first_out.shape[0]
    for start, total in (((1 - rep) * rows, other_ref), (rep * rows, own_ref)):
        span = pl.ds(pl.multiple_of(start, rows), rows)
        term = jnp.dot(ham_ref[0, span], den_ref[:half], preferred_element_type=F32)
        term += jnp.dot(ham_ref[1, span], den_ref[half:], preferred_element_type=F32)
        if total is other_ref:
            first_out[...] = total[:cut] + term[:cut]
            second_out[...] = total[cut:] + term[cut:]
        else:
            own_out[...] = total[...] + term


def late(other, own, ham_far, den_far):
    rows, cols = own.shape
    return pl.pallas_call(
        late_kernel,
        out_shape=[jax.ShapeDtypeStruct((n, cols), F32) for n in (FIRST, rows - FIRST, rows)],
        in_specs=[pl.BlockSpec(memory_space=pltpu.VMEM)] * 4,
        compiler_params=pltpu.CompilerParams(vmem_limit_bytes=8 * MIB),
        name="late",
    )(other, own, ham_far, den_far)


def finish_kernel(kept_ref, first_ref, second_ref, out_ref):
    cut = first_ref.shape[0]
    out_ref[:cut] = (kept_ref[:cut] + first_ref[...]).astype(BF16)
    out_ref[cut:] = (kept_ref[cut:] + second_ref[...]).astype(BF16)


def finish(kept, first, second):
    return pl.pallas_call(
        finish_kernel,
        out_shape=jax.ShapeDtypeStruct(kept.shape, BF16),
        compiler_params=pltpu.CompilerParams(vmem_limit_bytes=8 * MIB),
        name="finish",
    )(kept, first, second)


HAM_KEYS = [(dy, dx, dk) for dx in range(2) for dy in (0, -1, 1, 2) for dk in range(2)]
DEN_KEYS = [0, -1, 1, -2, 2, -3, 3, -4]


def after(value, *others):
    return lax.optimization_barrier((value, *others))[0]


def gather(dens, ham, dens_sums):
    den, got, swapped = {0: dens}, {(0, 0): ham}, {}

    def swap(key, *others):
        swapped[key] = col_swap(after(got[key], *others), 1)

    den[-1], den[1] = over_row(dens, 1), over_row(dens, -1)
    got[(-1, 0)], got[(1, 0)] = over_y(ham, 1), over_y(ham, -1)
    got[(0, 1)] = col_swap(ham, 2)

    den[-2], den[2] = over_row(den[-1], 1), over_row(den[1], -1)
    got[(-1, 1)] = over_y(after(got[(0, 1)], got[(-1, 0)]), 1)
    got[(1, 1)] = over_y(after(got[(0, 1)], got[(1, 0)]), -1)
    far_sums = over_row(dens_sums, 4)
    swap((0, 0), den[-1])
    swap((0, 1), swapped[(0, 0)])

    den[-3], den[3] = over_row(den[-2], 1), over_row(den[2], -1)
    got[(2, 1)] = over_y(got[(-1, 1)], 1)
    got[(2, 0)] = over_y(after(got[(1, 0)], got[(1, 1)]), -1)
    swap((-1, 0), den[-2], swapped[(0, 1)], far_sums)
    swap((1, 0), swapped[(-1, 0)])

    den[-4] = over_row(den[-3], 1)
    swap((-1, 1), den[-3])
    swap((1, 1), swapped[(-1, 1)])
    swap((2, 0), den[3])
    swap((2, 1), swapped[(2, 0)])
    ham_blocks = [(swapped if dk else got)[(dy, dx)] for dy, dx, dk in HAM_KEYS]
    return [den[key] for key in DEN_KEYS], ham_blocks, far_sums


def shards(hamiltonian, density, ham_pattern, den_pattern, tile_basis, offsets):
    dens, dens_sums = masked("mask_dens", den_pattern, density, with_sums=True)
    (ham,) = masked("mask_ham", ham_pattern, hamiltonian)
    (*den_blocks, den_far), ham_blocks, far_sums = gather(dens, ham, dens_sums)
    other, own, ham_far, sums = early(ham_blocks, den_blocks, far_sums)

    sums = sums + over_x(sums, 1) + over_x(sums, -1) + over_x(sums, 2)
    first, second, kept = late(other, own, ham_far, den_far)
    first = rep_swap(first)
    second = rep_swap(after(second, sums))
    product = finish(kept, first, second)
    sums = sums + straight_y(sums, 1) + straight_y(sums, -1) + straight_y(sums, 2)
    sums = after(sums + col_swap(sums, 1), first)

    total_order = density.shape[1] * lax.axis_size("col")
    atoms = offsets.shape[0]
    amplitudes = (sums[0] * (1.0 / math.sqrt(total_order))).reshape(2 * atoms, -1)
    tiles = jnp.einsum(
        "am,mtp->atp", amplitudes, tile_basis.astype(F32), precision=lax.Precision.HIGHEST
    )
    rep = lax.axis_index("rep")
    theirs = rep_swap(offsets)
    both = jnp.where(rep == 0, jnp.stack([offsets, theirs]), jnp.stack([theirs, offsets]))
    planes = both[:, :, None] + jnp.arange(TX, dtype=jnp.int32)[None, None, :]
    onehot = (planes[..., None] == jnp.arange(SX + TX, dtype=jnp.int32)).astype(F32)
    extended = jnp.einsum(
        "satx,satp->sxp",
        onehot,
        tiles.reshape(2, atoms, *tiles.shape[1:]),
        precision=lax.Precision.HIGHEST,
    )
    across = lax.ppermute(extended[1, SX:], "row", [(i, (i + 1) % NZ) for i in range(NZ)])
    incoming = jnp.where(rep == 0, across, extended[0, SX:])
    own_planes = jnp.where(rep == 0, extended[0, :SX], extended[1, :SX])
    grid_density = jnp.concatenate([own_planes[:TX] + incoming, own_planes[TX:]], axis=0)

    return (product, grid_density)


def solution(mesh):
    in_specs = (
        P("row", ("rep", "col")),
        P(("rep", "row"), "col"),
        P("row", ("rep", "col")),
        P(("rep", "row"), "col"),
        P(None, None, "col"),
        P(("row", "rep")),
    )
    out_specs = (P(("row", "rep"), "col"), P(("row", "rep"), "col"))
    return jax.shard_map(shards, mesh=mesh, in_specs=in_specs, out_specs=out_specs, check_vma=False)
```

time: 227 us -> 107 us (0.47)
  waiting for transfers between devices: 164 us -> 20.6 us
  starting transfers between devices: 0.99 us -> 68.7 us
  blocking collectives: 27.1 us -> 0 us
  between operations: 13.8 us -> 0.75 us
  Pallas kernels: 0 us -> 12 us
  matrix products: 10.9 us -> 0.56 us
  other arithmetic: 6.89 us -> 0.74 us
    all_gather x2 -> x0, waiting for transfers between devices: 123 us -> none  [the longest x1 66.5 us: shards(): lax.all_gather(ham, 'col', axis=1, tiled=True)]
    ppermute x1 -> x34, starting transfers between devices: 0.87 us -> 68.7 us  [the longest x10 31.1 us: col_swap(): return lax.ppermute(value, 'col', [(c, c ^ bit) for c in range(4 * NY)])]
    reduce_scatter x1 -> x0, waiting for transfers between devices: 35.7 us -> none  [shards(): lax.psum_scatter(partial_terms, 'rep', scatter_dimension=0, tiled=True)]
    psum x1 -> x0, blocking collectives: 27.1 us -> none  [row_charges(): return lax.psum(jnp.sum(full_rows, axis=1), 'col')]
    ppermute x1 -> x34, waiting for transfers between devices: 5.33 us -> 20.6 us  [the longest x3 8.11 us: rep_swap(): return lax.ppermute(value, 'rep', [(0, 1), (1, 0)])]
    pallas_call x0 -> x5, Pallas kernels: none -> 12 us  [the longest x1 7.85 us: early(): pl.pallas_call(early_kernel, out_shape=(jax.ShapeDtypeStruct((rows // 2,...]
    dot_general x3 -> x2, matrix products: 10.9 us -> 0.56 us  [the longest x1 0.33 us: shards(): jnp.einsum('satx,satp->sxp', onehot, tiles.reshape(2, atoms, *tiles.shape...]
    mul x3 -> x1, other arithmetic: 2.94 us -> 0.02 us  [shards(): sums[0] * (1.0 / math.sqrt(total_order))]
  transfers between devices with their start and end apart: 4 -> 34, of which waited for: 4 -> 10; matrix products, arithmetic and copies ran while one was open for 1% -> 1% of each run, Pallas kernels for 0% -> 10%
where the time goes in v2:
time: 107 us; the launch traced here: 106 us
  starting transfers between devices  68.7 us (64%)
  waiting for transfers between devices  20.6 us (19%)
  Pallas kernels  12 us (11%)
  local copies, waits for them, and re-layouts  2.93 us (3%)
    ppermute x10, starting transfers between devices, col_swap(): return lax.ppermute(value, 'col', [(c, c ^ bit) for c in range(4 * NY)])  31.1 us
    ppermute x8, starting transfers between devices, over_row(): return lax.ppermute(value, ('row', 'col'), pairs)  18.1 us
    ppermute x3, waiting for transfers between devices, rep_swap(): return lax.ppermute(value, 'rep', [(0, 1), (1, 0)])  8.11 us
    pallas_call x1, Pallas kernels, early(): pl.pallas_call(early_kernel, out_shape=(jax.ShapeDtypeStruct((rows // 2,...  7.85 us
    ppermute x6, starting transfers between devices, over_y(): return lax.ppermute(value, 'col', pairs)  7.08 us
    ppermute x3, starting transfers between devices, rep_swap(): return lax.ppermute(value, 'rep', [(0, 1), (1, 0)])  4.68 us
    ppermute x3, waiting for transfers between devices, straight_y(): return lax.ppermute(value, 'col', pairs)  4.55 us
    ppermute x3, starting transfers between devices, over_x(): return lax.ppermute(value, ('col', 'rep'), pairs)  3.98 us
  transfers between devices with their start and end apart: 34, of which 10 were waited for; matrix products, arithmetic and copies ran while one was open for 1% of the time, Pallas kernels for 10%

profile of v2, /device:TPU:1, one launch (start us, length us, event | category | flops | bytes accessed | tf_op | source)
XLA Modules:
  0.0 106.2 jit_solution(5641406984183699268)
XLA Ops:
  0.6 0.8 copy.8.pattern_ref
  1.4 1.0 copy-done.3
  2.5 0.4 mask_ham.1.refs_0_
  2.9 2.1 %collective-permute-start.4 = (bf16[1024,256]{1,0:T(8,128)(2,1)S(1)}, bf16[1024,256]{1,0:T(8,128)(2,1)S(1)}, u32[]{:S(2)}, u32[]{:S(2)}) collective-permute-start(bf16[1024,256]{1,0:T(8,128)(2,1)S(1)} %mask_ham.1.refs_0_), channel_id=1, source_target_pairs={{0,4},{2,6},{4,0},{6,2},{8,12},{10,14},{12,8},{14,10},{16,20},{18,... | collective-permute-start | bytes 1572872 | tf_op jit(solution)/shard_map/ppermute | solution.py:49
  5.0 1.3 %collective-permute-start.8 = (bf16[1024,256]{1,0:T(8,128)(2,1)S(1)}, bf16[1024,256]{1,0:T(8,128)(2,1)S(1)}, u32[]{:S(2)}, u32[]{:S(2)}) collective-permute-start(bf16[1024,256]{1,0:T(8,128)(2,1)S(1)} %mask_ham.1.refs_0_), channel_id=1, source_target_pairs={{0,24},{2,10},{4,28},{6,14},{8,0},{10,18},{12,4},{14,22},{16,8},{1... | collective-permute-start | bytes 1572872 | tf_op jit(solution)/shard_map/ppermute | solution.py:40
  6.3 0.5 mask_dens.1
  6.9 1.7 %collective-permute-start.12 = (bf16[512,512]{1,0:T(8,128)(2,1)S(1)}, bf16[512,512]{1,0:T(8,128)(2,1)S(1)}, u32[]{:S(2)}, u32[]{:S(2)}) collective-permute-start(bf16[512,512]{1,0:T(8,128)(2,1)S(1)} %get-tuple-element.24.refs_16_), channel_id=1, source_target_pairs={{0,224},{2,34},{4,228},{6,38},{8,232},{10,42},{12,236},{14,46},{16... | collective-permute-start | bytes 1572872 | tf_op jit(solution)/shard_map/ppermute | solution.py:33
  8.6 4.0 %collective-permute-start = (bf16[512,512]{1,0:T(8,128)(2,1)S(1)}, bf16[512,512]{1,0:T(8,128)(2,1)S(1)}, u32[]{:S(2)}, u32[]{:S(2)}) collective-permute-start(bf16[512,512]{1,0:T(8,128)(2,1)S(1)} %get-tuple-element.24.refs_16_), channel_id=1, source_target_pairs={{0,32},{2,226},{4,36},{6,230},{8,40},{10,234},{12,44},{14,238},{16... | collective-permute-start | bytes 1572872 | tf_op jit(solution)/shard_map/ppermute | solution.py:33
  12.5 1.4 %collective-permute-start.2 = (bf16[1024,256]{1,0:T(8,128)(2,1)S(1)}, bf16[1024,256]{1,0:T(8,128)(2,1)S(1)}, u32[]{:S(2)}, u32[]{:S(2)}) collective-permute-start(bf16[1024,256]{1,0:T(8,128)(2,1)S(1)} %mask_ham.1.refs_0_), channel_id=1, source_target_pairs={{0,8},{2,26},{4,12},{6,30},{8,16},{10,2},{12,20},{14,6},{16,24},{1... | collective-permute-start | bytes 1572872 | tf_op jit(solution)/shard_map/ppermute | solution.py:40
  14.0 1.4 %collective-permute-done.4.refs_8_ = bf16[1024,256]{1,0:T(8,128)(2,1)S(1)} collective-permute-done((bf16[1024,256]{1,0:T(8,128)(2,1)S(1)}, bf16[1024,256]{1,0:T(8,128)(2,1)S(1)}, u32[]{:S(2)}, u32[]{:S(2)}) %collective-permute-start.4) | collective-permute-done | bytes 524320 | tf_op jit(solution)/shard_map/ppermute | solution.py:49
  15.3 2.6 %collective-permute-start.10 = (bf16[1024,256]{1,0:T(8,128)(2,1)S(1)}, bf16[1024,256]{1,0:T(8,128)(2,1)S(1)}, u32[]{:S(2)}, u32[]{:S(2)}) collective-permute-start(bf16[1024,256]{1,0:T(8,128)(2,1)S(1)} %collective-permute-done.4.refs_8_), channel_id=1, source_target_pairs={{0,24},{2,10},{4,28},{6,14},{8,0},{10,18},{12,4},{14,22},{16,8},{1... | collective-permute-start | bytes 1572872 | tf_op jit(solution)/shard_map/ppermute | solution.py:40
  17.9 1.1 %collective-permute-done.12.refs_18_ = bf16[512,512]{1,0:T(8,128)(2,1)S(1)} collective-permute-done((bf16[512,512]{1,0:T(8,128)(2,1)S(1)}, bf16[512,512]{1,0:T(8,128)(2,1)S(1)}, u32[]{:S(2)}, u32[]{:S(2)}) %collective-permute-start.12) | collective-permute-done | bytes 524320 | tf_op jit(solution)/shard_map/ppermute | solution.py:33
  19.1 0.5 collective-permute-start.13
  19.5 1.8 %collective-permute-done.refs_17_ = bf16[512,512]{1,0:T(8,128)(2,1)S(1)} collective-permute-done((bf16[512,512]{1,0:T(8,128)(2,1)S(1)}, bf16[512,512]{1,0:T(8,128)(2,1)S(1)}, u32[]{:S(2)}, u32[]{:S(2)}) %collective-permute-start) | collective-permute-done | bytes 524320 | tf_op jit(solution)/shard_map/ppermute | solution.py:33
  21.3 3.2 %collective-permute-start.3 = (bf16[512,512]{1,0:T(8,128)(2,1)S(1)}, bf16[512,512]{1,0:T(8,128)(2,1)S(1)}, u32[]{:S(2)}, u32[]{:S(2)}) collective-permute-start(bf16[512,512]{1,0:T(8,128)(2,1)S(1)} %collective-permute-done.refs_17_), channel_id=1, source_target_pairs={{0,32},{2,226},{4,36},{6,230},{8,40},{10,234},{12,44},{14,238},{16... | collective-permute-start | bytes 1572872 | tf_op jit(solution)/shard_map/ppermute | solution.py:33
  24.5 5.8 %collective-permute-start.1 = (bf16[1024,256]{1,0:T(8,128)(2,1)S(1)}, bf16[1024,256]{1,0:T(8,128)(2,1)S(1)}, u32[]{:S(2)}, u32[]{:S(2)}) collective-permute-start(bf16[1024,256]{1,0:T(8,128)(2,1)S(1)} %mask_ham.1.refs_0_), channel_id=1, source_target_pairs={{0,2},{2,0},{4,6},{6,4},{8,10},{10,8},{12,14},{14,12},{16,18},{18,... | collective-permute-start | bytes 1572872 | tf_op jit(solution)/shard_map/ppermute | solution.py:49
  30.3 0.5 collective-permute-done.10.refs_12_
  30.8 1.0 collective-permute-start.11
  31.8 3.0 %collective-permute-start.17 = (bf16[512,512]{1,0:T(8,128)(2,1)S(1)}, bf16[512,512]{1,0:T(8,128)(2,1)}, u32[]{:S(2)}, u32[]{:S(2)}) collective-permute-start(bf16[512,512]{1,0:T(8,128)(2,1)S(1)} %collective-permute-done.3.refs_19_), channel_id=1, source_target_pairs={{0,32},{2,226},{4,36},{6,230},{8,40},{10,234},{12,44},{14,238},{16... | collective-permute-start | bytes 1572872 | tf_op jit(solution)/shard_map/ppermute | solution.py:33
  34.8 10.2 %collective-permute-start.5 = (bf16[1024,256]{1,0:T(8,128)(2,1)S(1)}, bf16[1024,256]{1,0:T(8,128)(2,1)S(1)}, u32[]{:S(2)}, u32[]{:S(2)}) collective-permute-start(bf16[1024,256]{1,0:T(8,128)(2,1)S(1)} %collective-permute-done.4.refs_8_), channel_id=1, source_target_pairs={{0,2},{2,0},{4,6},{6,4},{8,10},{10,8},{12,14},{14,12},{16,18},{18,... | collective-permute-start | bytes 1572872 | tf_op jit(solution)/shard_map/ppermute | solution.py:49
  45.0 2.3 %collective-permute-start.6 = (f32[8,512]{1,0:T(8,128)S(1)}, f32[8,512]{1,0:T(8,128)S(1)}, u32[]{:S(2)}, u32[]{:S(2)}) collective-permute-start(f32[8,512]{1,0:T(8,128)S(1)} %get-tuple-element.27), channel_id=1, source_target_pairs={{0,128},{2,130},{4,132},{6,134},{8,136},{10,138},{12,140},{14,142}... | collective-permute-start | bytes 49160 | tf_op jit(solution)/shard_map/ppermute | solution.py:33
  47.3 0.8 collective-permute-start.20
  48.1 3.8 %collective-permute-start.15 = (bf16[1024,256]{1,0:T(8,128)(2,1)S(1)}, bf16[1024,256]{1,0:T(8,128)(2,1)S(1)}, u32[]{:S(2)}, u32[]{:S(2)}) collective-permute-start(bf16[1024,256]{1,0:T(8,128)(2,1)S(1)} %collective-permute-done.11.refs_6_), channel_id=1, source_target_pairs={{0,2},{2,0},{4,6},{6,4},{8,10},{10,8},{12,14},{14,12},{16,18},{18,... | collective-permute-start | bytes 1572872 | tf_op jit(solution)/shard_map/ppermute | solution.py:49
  51.9 4.3 %collective-permute-start.18 = (bf16[1024,256]{1,0:T(8,128)(2,1)S(1)}, bf16[1024,256]{1,0:T(8,128)(2,1)S(1)}, u32[]{:S(2)}, u32[]{:S(2)}) collective-permute-start(bf16[1024,256]{1,0:T(8,128)(2,1)S(1)} %collective-permute-done.16.refs_10_), channel_id=1, source_target_pairs={{0,2},{2,0},{4,6},{6,4},{8,10},{10,8},{12,14},{14,12},{16,18},{18,... | collective-permute-start | bytes 1572872 | tf_op jit(solution)/shard_map/ppermute | solution.py:49
  56.3 2.0 %collective-permute-start.21 = (bf16[1024,256]{1,0:T(8,128)(2,1)S(1)}, bf16[1024,256]{1,0:T(8,128)(2,1)S(1)}, u32[]{:S(2)}, u32[]{:S(2)}) collective-permute-start(bf16[1024,256]{1,0:T(8,128)(2,1)S(1)} %collective-permute-done.20.refs_14_), channel_id=1, source_target_pairs={{0,2},{2,0},{4,6},{6,4},{8,10},{10,8},{12,14},{14,12},{16,18},{18,... | collective-permute-start | bytes 1572872 | tf_op jit(solution)/shard_map/ppermute | solution.py:49
  58.4 0.4 collective-permute-start.9
  58.8 3.3 %collective-permute-start.22 = (bf16[512,512]{1,0:T(8,128)(2,1)}, bf16[512,512]{1,0:T(8,128)(2,1)}, u32[]{:S(2)}, u32[]{:S(2)}) collective-permute-start(bf16[512,512]{1,0:T(8,128)(2,1)} %collective-permute-done.17.refs_21_), channel_id=1, source_target_pairs={{0,32},{2,226},{4,36},{6,230},{8,40},{10,234},{12,44},{14,238},{16... | collective-permute-start | bytes 1572872 | tf_op jit(solution)/shard_map/ppermute | solution.py:33
  62.1 7.8 %early.1 = (f32[512,512]{1,0:T(8,128)S(1)}, f32[512,512]{1,0:T(8,128)S(1)}, bf16[2,1024,256]{2,1,0:T(8,128)(2,1)S(1)}, f32[8,1024]{1,0:T(8,128)S(1)}) custom-call(bf16[1024,256]{1,0:T(8,128)(2,1)S(1)} %mask_ham.1.refs_0_, bf16[1024,256]{1,0:T(8,128)(2,1)S(1)} %collective-permute-done.1.refs_1_, bf16[1024,256]{1,0:T(8,128)(2,1)S(1)} %collective-permute-done.2.refs_2_, ...), custom_call_target="tpu_custom_call" | custom-call | flops 4294967296 | bytes 4194304 | tf_op jit(solution)/shard_map/early/pallas_call | solution.py:175
  70.0 0.3 collective-permute-start.24
  70.3 2.4 %collective-permute-start.25 = (f32[8,1024]{1,0:T(8,128)S(1)}, f32[8,1024]{1,0:T(8,128)S(1)}, u32[]{:S(2)}, u32[]{:S(2)}) collective-permute-start(f32[8,1024]{1,0:T(8,128)S(1)} %get-tuple-element.43), channel_id=1, source_target_pairs={{0,5},{1,4},{2,7},{3,6},{4,0},{5,1},{6,2},{7,3},{8,13},{9,12},{10,... | collective-permute-start | bytes 98312 | tf_op jit(solution)/shard_map/ppermute | solution.py:62
  72.7 1.3 %collective-permute-start.26 = (f32[8,1024]{1,0:T(8,128)S(1)}, f32[8,1024]{1,0:T(8,128)S(1)}, u32[]{:S(2)}, u32[]{:S(2)}) collective-permute-start(f32[8,1024]{1,0:T(8,128)S(1)} %get-tuple-element.43), channel_id=1, source_target_pairs={{0,1},{1,0},{2,3},{3,2},{4,5},{5,4},{6,7},{7,6},{8,9},{9,8},{10,11... | collective-permute-start | bytes 98312 | tf_op jit(solution)/shard_map/ppermute | solution.py:62
  74.0 1.7 %collective-permute-start.28 = (s32[8]{0:T(128)S(1)}, s32[8]{0:T(128)S(1)}, u32[]{:S(2)}, u32[]{:S(2)}) collective-permute-start(s32[8]{0:T(128)S(1)} %copy-done.6), channel_id=1, source_target_pairs={{0,1},{1,0},{2,3},{3,2},{4,5},{5,4},{6,7},{7,6},{8,9},{9,8},{10,11... | collective-permute-start | bytes 104 | tf_op jit(solution)/shard_map/ppermute | solution.py:53
  75.7 2.3 %late.1 = (f32[256,512]{1,0:T(8,128)S(1)}, f32[256,512]{1,0:T(8,128)}, f32[512,512]{1,0:T(8,128)S(1)}) custom-call(f32[512,512]{1,0:T(8,128)S(1)} %get-tuple-element.37.other_ref, f32[512,512]{1,0:T(8,128)S(1)} %get-tuple-element.38.own_ref, bf16[2,1024,256]{2,1,0:T(8,128)(2,1)S(1)} %get-tuple-element.39.ham_ref, ...), custom_call_target="tpu_custom_call" | custom-call | tf_op jit(solution)/shard_map/late/pallas_call | solution.py:211
  78.0 1.0 copy-done.1
  79.0 1.3 %collective-permute-start.23 = (f32[256,512]{1,0:T(8,128)S(1)}, f32[256,512]{1,0:T(8,128)S(1)}, u32[]{:S(2)}, u32[]{:S(2)}) collective-permute-start(f32[256,512]{1,0:T(8,128)S(1)} %get-tuple-element.41), channel_id=1, source_target_pairs={{0,1},{1,0},{2,3},{3,2},{4,5},{5,4},{6,7},{7,6},{8,9},{9,8},{10,11... | collective-permute-start | bytes 1572872 | tf_op jit(solution)/shard_map/ppermute | solution.py:53
  80.3 2.7 %collective-permute-start.30 = (f32[8,1024]{1,0:T(8,128)S(1)}, f32[8,1024]{1,0:T(8,128)S(1)}, u32[]{:S(2)}, u32[]{:S(2)}) collective-permute-start(f32[8,1024]{1,0:T(8,128)S(1)} %add_add_fusion.1), channel_id=1, source_target_pairs={{0,24},{2,26},{4,28},{6,30},{8,0},{10,2},{12,4},{14,6},{16,8},{18,... | collective-permute-start | bytes 98312 | tf_op jit(solution)/shard_map/ppermute | solution.py:45
  83.0 1.6 %collective-permute-done.29 = f32[8,1024]{1,0:T(8,128)S(1)} collective-permute-done((f32[8,1024]{1,0:T(8,128)S(1)}, f32[8,1024]{1,0:T(8,128)S(1)}, u32[]{:S(2)}, u32[]{:S(2)}) %collective-permute-start.29) | collective-permute-done | bytes 32800 | tf_op jit(solution)/shard_map/ppermute | solution.py:45
  84.6 3.0 %collective-permute-done.31 = f32[8,1024]{1,0:T(8,128)S(1)} collective-permute-done((f32[8,1024]{1,0:T(8,128)S(1)}, f32[8,1024]{1,0:T(8,128)S(1)}, u32[]{:S(2)}, u32[]{:S(2)}) %collective-permute-start.31) | collective-permute-done | bytes 32800 | tf_op jit(solution)/shard_map/ppermute | solution.py:45
  87.6 2.4 %collective-permute-start.32 = (f32[8,1024]{1,0:T(8,128)S(1)}, f32[8,1024]{1,0:T(8,128)S(1)}, u32[]{:S(2)}, u32[]{:S(2)}) collective-permute-start(f32[8,1024]{1,0:T(8,128)S(1)} %add_add_fusion), channel_id=1, source_target_pairs={{0,2},{2,0},{4,6},{6,4},{8,10},{10,8},{12,14},{14,12},{16,18},{18,... | collective-permute-start | bytes 98312 | tf_op jit(solution)/shard_map/ppermute | solution.py:49
  90.1 1.7 %collective-permute-start.27 = (f32[256,512]{1,0:T(8,128)}, f32[256,512]{1,0:T(8,128)S(1)}, u32[]{:S(2)}, u32[]{:S(2)}) collective-permute-start(f32[256,512]{1,0:T(8,128)} %get-tuple-element.44), channel_id=1, source_target_pairs={{0,1},{1,0},{2,3},{3,2},{4,5},{5,4},{6,7},{7,6},{8,9},{9,8},{10,11... | collective-permute-start | bytes 1572872 | tf_op jit(solution)/shard_map/ppermute | solution.py:53
  91.8 1.5 %collective-permute-done.23.first_ref = f32[256,512]{1,0:T(8,128)S(1)} collective-permute-done((f32[256,512]{1,0:T(8,128)S(1)}, f32[256,512]{1,0:T(8,128)S(1)}, u32[]{:S(2)}, u32[]{:S(2)}) %collective-permute-start.23) | collective-permute-done | bytes 524320 | tf_op jit(solution)/shard_map/ppermute | solution.py:53
  93.4 0.2 fusion
  93.6 0.3 convolution_bitcast_fusion
  94.0 1.1 %collective-permute-start.33 = (f32[16,128]{1,0:T(8,128)S(1)}, f32[16,128]{1,0:T(8,128)S(1)}, u32[]{:S(2)}, u32[]{:S(2)}) collective-permute-start(f32[16,128]{1,0:T(8,128)S(1)} %slice_bitcast_fusion.2), channel_id=1, source_target_pairs={{0,32},{32,64},{64,96},{96,128},{128,160},{160,192},{192,224},{224... | collective-permute-start | bytes 24584 | tf_op jit(solution)/shard_map/ppermute | solution.py:306
  95.1 3.0 %collective-permute-done.33 = f32[16,128]{1,0:T(8,128)S(1)} collective-permute-done((f32[16,128]{1,0:T(8,128)S(1)}, f32[16,128]{1,0:T(8,128)S(1)}, u32[]{:S(2)}, u32[]{:S(2)}) %collective-permute-start.33) | collective-permute-done | bytes 8224 | tf_op jit(solution)/shard_map/ppermute | solution.py:306
  98.1 0.6 pad_maximum_fusion
  98.7 6.6 %collective-permute-done.27.second_ref = f32[256,512]{1,0:T(8,128)S(1)} collective-permute-done((f32[256,512]{1,0:T(8,128)}, f32[256,512]{1,0:T(8,128)S(1)}, u32[]{:S(2)}, u32[]{:S(2)}) %collective-permute-start.27) | collective-permute-done | bytes 524320 | tf_op jit(solution)/shard_map/ppermute | solution.py:53
  105.3 0.9 finish.1
  (54 shorter events, 0.7 us)
Async XLA Ops:
  0.6 92.8 %copy-start = (bf16[64,16,128]{2,1,0:T(8,128)(2,1)S(1)}, bf16[64,16,128]{2,1,0:T(8,128)(2,1)}, u32[]{:S(2)}) copy-start(bf16[64,16,128]{2,1,0:T(8,128)(2,1)} %param.10) | copy-start | bytes 786436
  1.4 1.0 copy-start.3
  2.5 3.8 %copy-start.4 = (bf16[512,512]{1,0:T(8,128)(2,1)S(1)}, bf16[512,512]{1,0:T(8,128)(2,1)}, u32[]{:S(2)}) copy-start(bf16[512,512]{1,0:T(8,128)(2,1)} %matrix_ref.3) | copy-start | bytes 1572868
  2.5 3.8 %copy-start.5 = (s32[8,8]{1,0:T(8,128)S(1)}, s32[8,8]{1,0:T(8,128)}, u32[]{:S(2)}) copy-start(s32[8,8]{1,0:T(8,128)} %pattern_ref.2) | copy-start | bytes 772
  2.9 12.4 %collective-permute-start.4 = (bf16[1024,256]{1,0:T(8,128)(2,1)S(1)}, bf16[1024,256]{1,0:T(8,128)(2,1)S(1)}, u32[]{:S(2)}, u32[]{:S(2)}) collective-permute-start(bf16[1024,256]{1,0:T(8,128)(2,1)S(1)} %mask_ham.1.refs_0_), channel_id=1, source_target_pairs={{0,4},{2,6},{4,0},{6,2},{8,12},{10,14},{12,8},{14,10},{16,20},{18,... | collective-permute-start | bytes 1572872 | tf_op jit(solution)/shard_map/ppermute | solution.py:49
  5.0 10.3 %collective-permute-start.8 = (bf16[1024,256]{1,0:T(8,128)(2,1)S(1)}, bf16[1024,256]{1,0:T(8,128)(2,1)S(1)}, u32[]{:S(2)}, u32[]{:S(2)}) collective-permute-start(bf16[1024,256]{1,0:T(8,128)(2,1)S(1)} %mask_ham.1.refs_0_), channel_id=1, source_target_pairs={{0,24},{2,10},{4,28},{6,14},{8,0},{10,18},{12,4},{14,22},{16,8},{1... | collective-permute-start | bytes 1572872 | tf_op jit(solution)/shard_map/ppermute | solution.py:40
  6.9 12.2 %collective-permute-start.12 = (bf16[512,512]{1,0:T(8,128)(2,1)S(1)}, bf16[512,512]{1,0:T(8,128)(2,1)S(1)}, u32[]{:S(2)}, u32[]{:S(2)}) collective-permute-start(bf16[512,512]{1,0:T(8,128)(2,1)S(1)} %get-tuple-element.24.refs_16_), channel_id=1, source_target_pairs={{0,224},{2,34},{4,228},{6,38},{8,232},{10,42},{12,236},{14,46},{16... | collective-permute-start | bytes 1572872 | tf_op jit(solution)/shard_map/ppermute | solution.py:33
  8.6 12.8 %collective-permute-start = (bf16[512,512]{1,0:T(8,128)(2,1)S(1)}, bf16[512,512]{1,0:T(8,128)(2,1)S(1)}, u32[]{:S(2)}, u32[]{:S(2)}) collective-permute-start(bf16[512,512]{1,0:T(8,128)(2,1)S(1)} %get-tuple-element.24.refs_16_), channel_id=1, source_target_pairs={{0,32},{2,226},{4,36},{6,230},{8,40},{10,234},{12,44},{14,238},{16... | collective-permute-start | bytes 1572872 | tf_op jit(solution)/shard_map/ppermute | solution.py:33
  12.5 17.8 %collective-permute-start.2 = (bf16[1024,256]{1,0:T(8,128)(2,1)S(1)}, bf16[1024,256]{1,0:T(8,128)(2,1)S(1)}, u32[]{:S(2)}, u32[]{:S(2)}) collective-permute-start(bf16[1024,256]{1,0:T(8,128)(2,1)S(1)} %mask_ham.1.refs_0_), channel_id=1, source_target_pairs={{0,8},{2,26},{4,12},{6,30},{8,16},{10,2},{12,20},{14,6},{16,24},{1... | collective-permute-start | bytes 1572872 | tf_op jit(solution)/shard_map/ppermute | solution.py:40
  15.3 15.4 %collective-permute-start.10 = (bf16[1024,256]{1,0:T(8,128)(2,1)S(1)}, bf16[1024,256]{1,0:T(8,128)(2,1)S(1)}, u32[]{:S(2)}, u32[]{:S(2)}) collective-permute-start(bf16[1024,256]{1,0:T(8,128)(2,1)S(1)} %collective-permute-done.4.refs_8_), channel_id=1, source_target_pairs={{0,24},{2,10},{4,28},{6,14},{8,0},{10,18},{12,4},{14,22},{16,8},{1... | collective-permute-start | bytes 1572872 | tf_op jit(solution)/shard_map/ppermute | solution.py:40
  19.1 12.7 %collective-permute-start.13 = (bf16[512,512]{1,0:T(8,128)(2,1)S(1)}, bf16[512,512]{1,0:T(8,128)(2,1)S(1)}, u32[]{:S(2)}, u32[]{:S(2)}) collective-permute-start(bf16[512,512]{1,0:T(8,128)(2,1)S(1)} %collective-permute-done.12.refs_18_), channel_id=1, source_target_pairs={{0,224},{2,34},{4,228},{6,38},{8,232},{10,42},{12,236},{14,46},{16... | collective-permute-start | bytes 1572872 | tf_op jit(solution)/shard_map/ppermute | solution.py:33
  21.3 10.5 %collective-permute-start.3 = (bf16[512,512]{1,0:T(8,128)(2,1)S(1)}, bf16[512,512]{1,0:T(8,128)(2,1)S(1)}, u32[]{:S(2)}, u32[]{:S(2)}) collective-permute-start(bf16[512,512]{1,0:T(8,128)(2,1)S(1)} %collective-permute-done.refs_17_), channel_id=1, source_target_pairs={{0,32},{2,226},{4,36},{6,230},{8,40},{10,234},{12,44},{14,238},{16... | collective-permute-start | bytes 1572872 | tf_op jit(solution)/shard_map/ppermute | solution.py:33
  24.5 10.3 %collective-permute-start.1 = (bf16[1024,256]{1,0:T(8,128)(2,1)S(1)}, bf16[1024,256]{1,0:T(8,128)(2,1)S(1)}, u32[]{:S(2)}, u32[]{:S(2)}) collective-permute-start(bf16[1024,256]{1,0:T(8,128)(2,1)S(1)} %mask_ham.1.refs_0_), channel_id=1, source_target_pairs={{0,2},{2,0},{4,6},{6,4},{8,10},{10,8},{12,14},{14,12},{16,18},{18,... | collective-permute-start | bytes 1572872 | tf_op jit(solution)/shard_map/ppermute | solution.py:49
  30.3 14.7 %collective-permute-start.16 = (bf16[1024,256]{1,0:T(8,128)(2,1)S(1)}, bf16[1024,256]{1,0:T(8,128)(2,1)S(1)}, u32[]{:S(2)}, u32[]{:S(2)}) collective-permute-start(bf16[1024,256]{1,0:T(8,128)(2,1)S(1)} %collective-permute-done.4.refs_8_), channel_id=1, source_target_pairs={{0,8},{2,26},{4,12},{6,30},{8,16},{10,2},{12,20},{14,6},{16,24},{1... | collective-permute-start | bytes 1572872 | tf_op jit(solution)/shard_map/ppermute | solution.py:40
  30.8 16.5 %collective-permute-start.11 = (bf16[1024,256]{1,0:T(8,128)(2,1)S(1)}, bf16[1024,256]{1,0:T(8,128)(2,1)S(1)}, u32[]{:S(2)}, u32[]{:S(2)}) collective-permute-start(bf16[1024,256]{1,0:T(8,128)(2,1)S(1)} %collective-permute-done.8.refs_4_), channel_id=1, source_target_pairs={{0,24},{2,10},{4,28},{6,14},{8,0},{10,18},{12,4},{14,22},{16,8},{1... | collective-permute-start | bytes 1572872 | tf_op jit(solution)/shard_map/ppermute | solution.py:40
  31.8 16.3 %collective-permute-start.14 = (bf16[512,512]{1,0:T(8,128)(2,1)S(1)}, bf16[512,512]{1,0:T(8,128)(2,1)S(1)}, u32[]{:S(2)}, u32[]{:S(2)}) collective-permute-start(bf16[512,512]{1,0:T(8,128)(2,1)S(1)} %collective-permute-done.13.refs_20_), channel_id=1, source_target_pairs={{0,224},{2,34},{4,228},{6,38},{8,232},{10,42},{12,236},{14,46},{16... | collective-permute-start | bytes 1572872 | tf_op jit(solution)/shard_map/ppermute | solution.py:33
  31.8 20.1 %collective-permute-start.17 = (bf16[512,512]{1,0:T(8,128)(2,1)S(1)}, bf16[512,512]{1,0:T(8,128)(2,1)}, u32[]{:S(2)}, u32[]{:S(2)}) collective-permute-start(bf16[512,512]{1,0:T(8,128)(2,1)S(1)} %collective-permute-done.3.refs_19_), channel_id=1, source_target_pairs={{0,32},{2,226},{4,36},{6,230},{8,40},{10,234},{12,44},{14,238},{16... | collective-permute-start | bytes 1572872 | tf_op jit(solution)/shard_map/ppermute | solution.py:33
  34.8 21.3 %collective-permute-start.5 = (bf16[1024,256]{1,0:T(8,128)(2,1)S(1)}, bf16[1024,256]{1,0:T(8,128)(2,1)S(1)}, u32[]{:S(2)}, u32[]{:S(2)}) collective-permute-start(bf16[1024,256]{1,0:T(8,128)(2,1)S(1)} %collective-permute-done.4.refs_8_), channel_id=1, source_target_pairs={{0,2},{2,0},{4,6},{6,4},{8,10},{10,8},{12,14},{14,12},{16,18},{18,... | collective-permute-start | bytes 1572872 | tf_op jit(solution)/shard_map/ppermute | solution.py:49
  45.0 11.2 %collective-permute-start.6 = (f32[8,512]{1,0:T(8,128)S(1)}, f32[8,512]{1,0:T(8,128)S(1)}, u32[]{:S(2)}, u32[]{:S(2)}) collective-permute-start(f32[8,512]{1,0:T(8,128)S(1)} %get-tuple-element.27), channel_id=1, source_target_pairs={{0,128},{2,130},{4,132},{6,134},{8,136},{10,138},{12,140},{14,142}... | collective-permute-start | bytes 49160 | tf_op jit(solution)/shard_map/ppermute | solution.py:33
  47.3 8.9 %collective-permute-start.20 = (bf16[1024,256]{1,0:T(8,128)(2,1)S(1)}, bf16[1024,256]{1,0:T(8,128)(2,1)S(1)}, u32[]{:S(2)}, u32[]{:S(2)}) collective-permute-start(bf16[1024,256]{1,0:T(8,128)(2,1)S(1)} %collective-permute-done.16.refs_10_), channel_id=1, source_target_pairs={{0,8},{2,26},{4,12},{6,30},{8,16},{10,2},{12,20},{14,6},{16,24},{1... | collective-permute-start | bytes 1572872 | tf_op jit(solution)/shard_map/ppermute | solution.py:40
  48.1 8.2 %collective-permute-start.15 = (bf16[1024,256]{1,0:T(8,128)(2,1)S(1)}, bf16[1024,256]{1,0:T(8,128)(2,1)S(1)}, u32[]{:S(2)}, u32[]{:S(2)}) collective-permute-start(bf16[1024,256]{1,0:T(8,128)(2,1)S(1)} %collective-permute-done.11.refs_6_), channel_id=1, source_target_pairs={{0,2},{2,0},{4,6},{6,4},{8,10},{10,8},{12,14},{14,12},{16,18},{18,... | collective-permute-start | bytes 1572872 | tf_op jit(solution)/shard_map/ppermute | solution.py:49
  51.9 6.3 %collective-permute-start.18 = (bf16[1024,256]{1,0:T(8,128)(2,1)S(1)}, bf16[1024,256]{1,0:T(8,128)(2,1)S(1)}, u32[]{:S(2)}, u32[]{:S(2)}) collective-permute-start(bf16[1024,256]{1,0:T(8,128)(2,1)S(1)} %collective-permute-done.16.refs_10_), channel_id=1, source_target_pairs={{0,2},{2,0},{4,6},{6,4},{8,10},{10,8},{12,14},{14,12},{16,18},{18,... | collective-permute-start | bytes 1572872 | tf_op jit(solution)/shard_map/ppermute | solution.py:49
  56.2 2.3 %collective-permute-start.7 = (bf16[1024,256]{1,0:T(8,128)(2,1)S(1)}, bf16[1024,256]{1,0:T(8,128)(2,1)S(1)}, u32[]{:S(2)}, u32[]{:S(2)}) collective-permute-start(bf16[1024,256]{1,0:T(8,128)(2,1)S(1)} %collective-permute-done.2.refs_2_), channel_id=1, source_target_pairs={{0,2},{2,0},{4,6},{6,4},{8,10},{10,8},{12,14},{14,12},{16,18},{18,... | collective-permute-start | bytes 1572872 | tf_op jit(solution)/shard_map/ppermute | solution.py:49
  56.3 5.9 %collective-permute-start.21 = (bf16[1024,256]{1,0:T(8,128)(2,1)S(1)}, bf16[1024,256]{1,0:T(8,128)(2,1)S(1)}, u32[]{:S(2)}, u32[]{:S(2)}) collective-permute-start(bf16[1024,256]{1,0:T(8,128)(2,1)S(1)} %collective-permute-done.20.refs_14_), channel_id=1, source_target_pairs={{0,2},{2,0},{4,6},{6,4},{8,10},{10,8},{12,14},{14,12},{16,18},{18,... | collective-permute-start | bytes 1572872 | tf_op jit(solution)/shard_map/ppermute | solution.py:49
  58.2 3.9 %collective-permute-start.19 = (bf16[1024,256]{1,0:T(8,128)(2,1)S(1)}, bf16[1024,256]{1,0:T(8,128)(2,1)S(1)}, u32[]{:S(2)}, u32[]{:S(2)}) collective-permute-start(bf16[1024,256]{1,0:T(8,128)(2,1)S(1)} %collective-permute-done.10.refs_12_), channel_id=1, source_target_pairs={{0,2},{2,0},{4,6},{6,4},{8,10},{10,8},{12,14},{14,12},{16,18},{18,... | collective-permute-start | bytes 1572872 | tf_op jit(solution)/shard_map/ppermute | solution.py:49
  58.4 3.7 %collective-permute-start.9 = (bf16[1024,256]{1,0:T(8,128)(2,1)S(1)}, bf16[1024,256]{1,0:T(8,128)(2,1)S(1)}, u32[]{:S(2)}, u32[]{:S(2)}) collective-permute-start(bf16[1024,256]{1,0:T(8,128)(2,1)S(1)} %collective-permute-done.8.refs_4_), channel_id=1, source_target_pairs={{0,2},{2,0},{4,6},{6,4},{8,10},{10,8},{12,14},{14,12},{16,18},{18,... | collective-permute-start | bytes 1572872 | tf_op jit(solution)/shard_map/ppermute | solution.py:49
  58.8 16.9 %collective-permute-start.22 = (bf16[512,512]{1,0:T(8,128)(2,1)}, bf16[512,512]{1,0:T(8,128)(2,1)}, u32[]{:S(2)}, u32[]{:S(2)}) collective-permute-start(bf16[512,512]{1,0:T(8,128)(2,1)} %collective-permute-done.17.refs_21_), channel_id=1, source_target_pairs={{0,32},{2,226},{4,36},{6,230},{8,40},{10,234},{12,44},{14,238},{16... | collective-permute-start | bytes 1572872 | tf_op jit(solution)/shard_map/ppermute | solution.py:33
  70.0 4.0 %copy-start.6 = (s32[8]{0:T(128)S(1)}, s32[8]{0:T(128)}, u32[]{:S(2)}) copy-start(s32[8]{0:T(128)} %param.11) | copy-start | bytes 100
  70.0 10.2 %collective-permute-start.24 = (f32[8,1024]{1,0:T(8,128)S(1)}, f32[8,1024]{1,0:T(8,128)S(1)}, u32[]{:S(2)}, u32[]{:S(2)}) collective-permute-start(f32[8,1024]{1,0:T(8,128)S(1)} %get-tuple-element.43), channel_id=1, source_target_pairs={{0,4},{1,5},{2,6},{3,7},{4,1},{5,0},{6,3},{7,2},{8,12},{9,13},{10,... | collective-permute-start | bytes 98312 | tf_op jit(solution)/shard_map/ppermute | solution.py:62
  70.3 10.0 %collective-permute-start.25 = (f32[8,1024]{1,0:T(8,128)S(1)}, f32[8,1024]{1,0:T(8,128)S(1)}, u32[]{:S(2)}, u32[]{:S(2)}) collective-permute-start(f32[8,1024]{1,0:T(8,128)S(1)} %get-tuple-element.43), channel_id=1, source_target_pairs={{0,5},{1,4},{2,7},{3,6},{4,0},{5,1},{6,2},{7,3},{8,13},{9,12},{10,... | collective-permute-start | bytes 98312 | tf_op jit(solution)/shard_map/ppermute | solution.py:62
  72.7 7.5 %collective-permute-start.26 = (f32[8,1024]{1,0:T(8,128)S(1)}, f32[8,1024]{1,0:T(8,128)S(1)}, u32[]{:S(2)}, u32[]{:S(2)}) collective-permute-start(f32[8,1024]{1,0:T(8,128)S(1)} %get-tuple-element.43), channel_id=1, source_target_pairs={{0,1},{1,0},{2,3},{3,2},{4,5},{5,4},{6,7},{7,6},{8,9},{9,8},{10,11... | collective-permute-start | bytes 98312 | tf_op jit(solution)/shard_map/ppermute | solution.py:62
  74.0 9.0 %collective-permute-start.28 = (s32[8]{0:T(128)S(1)}, s32[8]{0:T(128)S(1)}, u32[]{:S(2)}, u32[]{:S(2)}) collective-permute-start(s32[8]{0:T(128)S(1)} %copy-done.6), channel_id=1, source_target_pairs={{0,1},{1,0},{2,3},{3,2},{4,5},{5,4},{6,7},{7,6},{8,9},{9,8},{10,11... | collective-permute-start | bytes 104 | tf_op jit(solution)/shard_map/ppermute | solution.py:53
  78.0 1.0 copy-start.1
  79.0 26.3 %copy-start.2 = (f32[512,512]{1,0:T(8,128)S(1)}, f32[512,512]{1,0:T(8,128)}, u32[]{:S(2)}) copy-start(f32[512,512]{1,0:T(8,128)} %copy-done.1) | copy-start | bytes 3145732
  79.0 14.3 %collective-permute-start.23 = (f32[256,512]{1,0:T(8,128)S(1)}, f32[256,512]{1,0:T(8,128)S(1)}, u32[]{:S(2)}, u32[]{:S(2)}) collective-permute-start(f32[256,512]{1,0:T(8,128)S(1)} %get-tuple-element.41), channel_id=1, source_target_pairs={{0,1},{1,0},{2,3},{3,2},{4,5},{5,4},{6,7},{7,6},{8,9},{9,8},{10,11... | collective-permute-start | bytes 1572872 | tf_op jit(solution)/shard_map/ppermute | solution.py:53
  80.3 4.3 %collective-permute-start.29 = (f32[8,1024]{1,0:T(8,128)S(1)}, f32[8,1024]{1,0:T(8,128)S(1)}, u32[]{:S(2)}, u32[]{:S(2)}) collective-permute-start(f32[8,1024]{1,0:T(8,128)S(1)} %add_add_fusion.1), channel_id=1, source_target_pairs={{0,8},{2,10},{4,12},{6,14},{8,16},{10,18},{12,20},{14,22},{16,24},... | collective-permute-start | bytes 98312 | tf_op jit(solution)/shard_map/ppermute | solution.py:45
  80.3 4.3 %collective-permute-start.30 = (f32[8,1024]{1,0:T(8,128)S(1)}, f32[8,1024]{1,0:T(8,128)S(1)}, u32[]{:S(2)}, u32[]{:S(2)}) collective-permute-start(f32[8,1024]{1,0:T(8,128)S(1)} %add_add_fusion.1), channel_id=1, source_target_pairs={{0,24},{2,26},{4,28},{6,30},{8,0},{10,2},{12,4},{14,6},{16,8},{18,... | collective-permute-start | bytes 98312 | tf_op jit(solution)/shard_map/ppermute | solution.py:45
  83.0 4.6 %collective-permute-start.31 = (f32[8,1024]{1,0:T(8,128)S(1)}, f32[8,1024]{1,0:T(8,128)S(1)}, u32[]{:S(2)}, u32[]{:S(2)}) collective-permute-start(f32[8,1024]{1,0:T(8,128)S(1)} %add_add_fusion.1), channel_id=1, source_target_pairs={{0,16},{2,18},{4,20},{6,22},{8,24},{10,26},{12,28},{14,30},{16,0},... | collective-permute-start | bytes 98312 | tf_op jit(solution)/shard_map/ppermute | solution.py:45
  87.6 4.2 %collective-permute-start.32 = (f32[8,1024]{1,0:T(8,128)S(1)}, f32[8,1024]{1,0:T(8,128)S(1)}, u32[]{:S(2)}, u32[]{:S(2)}) collective-permute-start(f32[8,1024]{1,0:T(8,128)S(1)} %add_add_fusion), channel_id=1, source_target_pairs={{0,2},{2,0},{4,6},{6,4},{8,10},{10,8},{12,14},{14,12},{16,18},{18,... | collective-permute-start | bytes 98312 | tf_op jit(solution)/shard_map/ppermute | solution.py:49
  90.1 15.2 %collective-permute-start.27 = (f32[256,512]{1,0:T(8,128)}, f32[256,512]{1,0:T(8,128)S(1)}, u32[]{:S(2)}, u32[]{:S(2)}) collective-permute-start(f32[256,512]{1,0:T(8,128)} %get-tuple-element.44), channel_id=1, source_target_pairs={{0,1},{1,0},{2,3},{3,2},{4,5},{5,4},{6,7},{7,6},{8,9},{9,8},{10,11... | collective-permute-start | bytes 1572872 | tf_op jit(solution)/shard_map/ppermute | solution.py:53
  94.0 4.1 %collective-permute-start.33 = (f32[16,128]{1,0:T(8,128)S(1)}, f32[16,128]{1,0:T(8,128)S(1)}, u32[]{:S(2)}, u32[]{:S(2)}) collective-permute-start(f32[16,128]{1,0:T(8,128)S(1)} %slice_bitcast_fusion.2), channel_id=1, source_target_pairs={{0,32},{32,64},{64,96},{96,128},{128,160},{160,192},{192,224},{224... | collective-permute-start | bytes 24584 | tf_op jit(solution)/shard_map/ppermute | solution.py:306

commit v3 on v2

--- a/solution.py
+++ b/solution.py
@@ -107,16 +107,18 @@
     return row, col // 4, (col // 2) % 2, col % 2, lax.axis_index("rep")
 
 
+def dot_transposed(left, right):
+    return lax.dot_general(left, right, (((1,), (1,)), ((), ())), preferred_element_type=F32)
+
+
 def split_dot(wide, narrow):
-    total = None
+    rows = wide.shape[0]
+    terms = []
     for _ in range(3):
-        piece = wide.astype(BF16)
-        wide = wide - piece.astype(F32)
-        term = lax.dot_general(
-            piece, narrow, (((1,), (1,)), ((), ())), preferred_element_type=F32
-        )
-        total = term if total is None else total + term
-    return total
+        terms.append(wide.astype(BF16))
+        wide = wide - terms[-1].astype(F32)
+    result = dot_transposed(jnp.concatenate(terms, axis=0), narrow)
+    return result[:rows] + (result[rows : 2 * rows] + result[2 * rows :])
 
 
 def row_sums(ref):
@@ -136,7 +138,9 @@
 def early_kernel(*refs):
     n_ham, n_den = len(HAM_KEYS), len(DEN_KEYS) - 1
     ham_refs, den_refs, far_ref = refs[:n_ham], refs[n_ham : n_ham + n_den], refs[n_ham + n_den]
-    other_ref, own_ref, ham_far_ref, sums_ref, den_buf = refs[n_ham + n_den + 1 :]
+    other_out, own_out, ham_far_out, sums_ref, other_ref, own_ref, ham_far_ref, den_buf, sems = refs[
+        n_ham + n_den + 1 :
+    ]
     row, y, x, core, rep = place()
     rows = own_ref.shape[0]
     for n in range(n_den):
@@ -144,45 +148,52 @@
     far = lax.rem(row + NZ // 2, NZ)
     den_buf[far] = jnp.zeros(den_buf.shape[1:], BF16)
     half_size = den_buf.shape[1] // 2
-    starts = [pl.multiple_of((1 - rep) * rows, rows), pl.multiple_of(rep * rows, rows)]
+    places = []
     for n, (dy, dx, dk) in enumerate(HAM_KEYS):
         half = core + dk - 2 * core * dk
         chip = lax.rem(y + way(half) * dy + NY, NY) * 2 + (x + dx - 2 * x * dx)
-        block = ham_refs[n]
+        places.append((chip, half))
 
         @pl.when(chip == far)
         def _():
-            ham_far_ref[half] = block[...]
-
-        den = den_buf[chip, pl.ds(pl.multiple_of(half * half_size, half_size), half_size), :]
-        for start, out_ref in zip(starts, (other_ref, own_ref)):
-            term = jnp.dot(block[pl.ds(start, rows), :], den, preferred_element_type=F32)
+            ham_far_ref[half] = ham_refs[n][...]
+
+    out = pltpu.make_async_copy(ham_far_ref, ham_far_out, sems.at[0])
+    out.start()
+    outs = [out]
+    sums_ref[...] = split_dot(far_ref[:, :half_size], ham_far_ref[0]) + split_dot(
+        far_ref[:, half_size:], ham_far_ref[1]
+    )
+    for i, (part, total, total_out) in enumerate(((1 - rep, other_ref, other_out), (rep, own_ref, own_out))):
+        span = pl.ds(pl.multiple_of(part * rows, rows), rows)
+        for n, (chip, half) in enumerate(places):
+            den = den_buf[chip, pl.ds(pl.multiple_of(half * half_size, half_size), half_size), :]
+            term = jnp.dot(ham_refs[n][span, :], den, preferred_element_type=F32)
             if n == 0:
-                out_ref[...] = term
+                total[...] = term
             else:
-                out_ref[...] += term
-    far_sums = split_dot(far_ref[:, :half_size], ham_far_ref[0])
-    far_sums += split_dot(far_ref[:, half_size:], ham_far_ref[1])
-    sums_ref[...] = far_sums
-    for start, out_ref in zip(starts, (other_ref, own_ref)):
-        sums_ref[:, pl.ds(start, rows)] += row_sums(out_ref)
+                total[...] += term
+        out = pltpu.make_async_copy(total, total_out, sems.at[1 + i])
+        out.start()
+        outs.append(out)
+        sums_ref[:, span] += row_sums(total)
+    for out in outs:
+        out.wait()
 
 
 def early(ham_blocks, den_blocks, far_sums):
     rows, half = ham_blocks[0].shape
     depth, cols = den_blocks[0].shape
     n = len(ham_blocks) + len(den_blocks) + 1
+    shapes = [((rows // 2, cols), F32), ((rows // 2, cols), F32), ((2, rows, half), BF16)]
     return pl.pallas_call(
         early_kernel,
-        out_shape=(
-            jax.ShapeDtypeStruct((rows // 2, cols), F32),
-            jax.ShapeDtypeStruct((rows // 2, cols), F32),
-            jax.ShapeDtypeStruct((2, rows, half), BF16),
-            jax.ShapeDtypeStruct((8, rows), F32),
-        ),
+        out_shape=[jax.ShapeDtypeStruct(*shape) for shape in shapes] + [jax.ShapeDtypeStruct((8, rows), F32)],
         in_specs=[pl.BlockSpec(memory_space=pltpu.VMEM)] * n,
-        scratch_shapes=[pltpu.VMEM((NZ, depth, cols), BF16)],
-        compiler_params=pltpu.CompilerParams(vmem_limit_bytes=12 * MIB),
+        out_specs=[pl.BlockSpec(memory_space=pltpu.HBM)] * 3 + [pl.BlockSpec(memory_space=pltpu.VMEM)],
+        scratch_shapes=[pltpu.VMEM(*shape) for shape in shapes]
+        + [pltpu.VMEM((NZ, depth, cols), BF16), pltpu.SemaphoreType.DMA((3,))],
+        compiler_params=pltpu.CompilerParams(vmem_limit_bytes=16 * MIB),
         cost_estimate=pl.CostEstimate(
             flops=2 * rows * cols * depth * NZ, bytes_accessed=4 * MIB, transcendentals=0
         ),
@@ -190,31 +201,44 @@
     )(*ham_blocks, *den_blocks, far_sums)
 
 
-def late_kernel(other_ref, own_ref, ham_ref, den_ref, first_out, second_out, own_out):
-    rep = lax.axis_index("rep")
-    rows = own_out.shape[0]
+def far_term(start, rows, ham_ref, den_ref):
     half = ham_ref.shape[2]
-    cut = first_out.shape[0]
-    for start, total in (((1 - rep) * rows, other_ref), (rep * rows, own_ref)):
-        span = pl.ds(pl.multiple_of(start, rows), rows)
-        term = jnp.dot(ham_ref[0, span], den_ref[:half], preferred_element_type=F32)
-        term += jnp.dot(ham_ref[1, span], den_ref[half:], preferred_element_type=F32)
-        if total is other_ref:
-            first_out[...] = total[:cut] + term[:cut]
-            second_out[...] = total[cut:] + term[cut:]
-        else:
-            own_out[...] = total[...] + term
-
-
-def late(other, own, ham_far, den_far):
-    rows, cols = own.shape
+    span = pl.ds(pl.multiple_of(start, rows), rows)
+    term = jnp.dot(ham_ref[0, span], den_ref[:half], preferred_element_type=F32)
+    return term + jnp.dot(ham_ref[1, span], den_ref[half:], preferred_element_type=F32)
+
+
+def late_kernel(other_ref, ham_ref, den_ref, first_out, second_out):
+    rows, cut = other_ref.shape[0], first_out.shape[0]
+    term = far_term((1 - lax.axis_index("rep")) * rows, rows, ham_ref, den_ref)
+    first_out[...] = other_ref[:cut] + term[:cut]
+    second_out[...] = other_ref[cut:] + term[cut:]
+
+
+def late(other, ham_far, den_far):
+    rows, cols = other.shape
     return pl.pallas_call(
         late_kernel,
-        out_shape=[jax.ShapeDtypeStruct((n, cols), F32) for n in (FIRST, rows - FIRST, rows)],
-        in_specs=[pl.BlockSpec(memory_space=pltpu.VMEM)] * 4,
+        out_shape=[jax.ShapeDtypeStruct((n, cols), F32) for n in (FIRST, rows - FIRST)],
+        in_specs=[pl.BlockSpec(memory_space=pltpu.VMEM)] * 3,
         compiler_params=pltpu.CompilerParams(vmem_limit_bytes=8 * MIB),
         name="late",
-    )(other, own, ham_far, den_far)
+    )(other, ham_far, den_far)
+
+
+def kept_kernel(own_ref, ham_ref, den_ref, out_ref):
+    rows = own_ref.shape[0]
+    out_ref[...] = own_ref[...] + far_term(lax.axis_index("rep") * rows, rows, ham_ref, den_ref)
+
+
+def kept_rows(own, ham_far, den_far):
+    return pl.pallas_call(
+        kept_kernel,
+        out_shape=jax.ShapeDtypeStruct(own.shape, F32),
+        in_specs=[pl.BlockSpec(memory_space=pltpu.VMEM)] * 3,
+        compiler_params=pltpu.CompilerParams(vmem_limit_bytes=8 * MIB),
+        name="kept",
+    )(own, ham_far, den_far)
 
 
 def finish_kernel(kept_ref, first_ref, second_ref, out_ref):
@@ -278,22 +302,24 @@
     (*den_blocks, den_far), ham_blocks, far_sums = gather(dens, ham, dens_sums)
     other, own, ham_far, sums = early(ham_blocks, den_blocks, far_sums)
 
-    sums = sums + over_x(sums, 1) + over_x(sums, -1) + over_x(sums, 2)
-    first, second, kept = late(other, own, ham_far, den_far)
+    atoms = offsets.shape[0]
+    sums = sums.at[1, :atoms].set(offsets.astype(F32))
+    hops = [over_x(sums, steps) for steps in (1, -1, 2)]
+    theirs = hops[2][1, :atoms].astype(jnp.int32)
+    sums = sums + hops[0] + hops[1] + hops[2]
+    first, second = late(other, ham_far, den_far)
     first = rep_swap(first)
     second = rep_swap(after(second, sums))
-    product = finish(kept, first, second)
+    product = finish(kept_rows(after(own, first), ham_far, den_far), first, second)
     sums = sums + straight_y(sums, 1) + straight_y(sums, -1) + straight_y(sums, 2)
     sums = after(sums + col_swap(sums, 1), first)
 
     total_order = density.shape[1] * lax.axis_size("col")
-    atoms = offsets.shape[0]
     amplitudes = (sums[0] * (1.0 / math.sqrt(total_order))).reshape(2 * atoms, -1)
     tiles = jnp.einsum(
         "am,mtp->atp", amplitudes, tile_basis.astype(F32), precision=lax.Precision.HIGHEST
     )
     rep = lax.axis_index("rep")
-    theirs = rep_swap(offsets)
     both = jnp.where(rep == 0, jnp.stack([offsets, theirs]), jnp.stack([theirs, offsets]))
     planes = both[:, :, None] + jnp.arange(TX, dtype=jnp.int32)[None, None, :]
     onehot = (planes[..., None] == jnp.arange(SX + TX, dtype=jnp.int32)).astype(F32)

time: 107 us -> 105 us (0.981)
  starting transfers between devices: 68.7 us -> 66.5 us
  local copies, waits for them, and re-layouts: 2.93 us -> 4.24 us
  Pallas kernels: 12 us -> 10.8 us
    ppermute x3 -> x2, starting transfers between devices: 4.68 us -> 2.98 us  [rep_swap(): return lax.ppermute(value, 'rep', [(0, 1), (1, 0)])]
    unnamed x15, local copies, waits for them, and re-layouts: 2.85 us -> 4.06 us
    pallas_call x1 -> x2, Pallas kernels: 7.85 us -> 6.7 us  [the longest x1 6.27 us: early(): pl.pallas_call(early_kernel, out_shape=[jax.ShapeDtypeStruct(*shape) for...]
    ppermute x3 -> x2, waiting for transfers between devices: 8.11 us -> 8.56 us  [rep_swap(): return lax.ppermute(value, 'rep', [(0, 1), (1, 0)])]
  transfers between devices with their start and end apart: 34 -> 33, of which waited for: 10 -> 9; matrix products, arithmetic and copies ran while one was open for 1% -> 1% of each run, Pallas kernels for 10% -> 8%
where the time goes in v3:
time: 105 us
  starting transfers between devices  66.5 us (63%)
  waiting for transfers between devices  20.9 us (20%)
  Pallas kernels  10.8 us (10%)
  local copies, waits for them, and re-layouts  4.24 us (4%)
    ppermute x10, starting transfers between devices, col_swap(): return lax.ppermute(value, 'col', [(c, c ^ bit) for c in range(4 * NY)])  30.8 us
    ppermute x8, starting transfers between devices, over_row(): return lax.ppermute(value, ('row', 'col'), pairs)  18.2 us
    ppermute x2, waiting for transfers between devices, rep_swap(): return lax.ppermute(value, 'rep', [(0, 1), (1, 0)])  8.56 us
    ppermute x6, starting transfers between devices, over_y(): return lax.ppermute(value, 'col', pairs)  7.07 us
    pallas_call x1, Pallas kernels, early(): pl.pallas_call(early_kernel, out_shape=[jax.ShapeDtypeStruct(*shape) for...  6.27 us
    ppermute x3, waiting for transfers between devices, straight_y(): return lax.ppermute(value, 'col', pairs)  4.54 us
    unnamed x15, local copies, waits for them, and re-layouts  4.06 us
    ppermute x3, starting transfers between devices, over_x(): return lax.ppermute(value, ('col', 'rep'), pairs)  4.02 us
  transfers between devices with their start and end apart: 33, of which 9 were waited for; matrix products, arithmetic and copies ran while one was open for 1% of the time, Pallas kernels for 8%

profile of v3, /device:TPU:1, one launch (start us, length us, event | category | flops | bytes accessed | tf_op | source)
XLA Modules:
  0.0 104.6 jit_solution(4592142054672729126)
XLA Ops:
  0.6 0.8 copy.8.pattern_ref
  1.4 1.0 copy-done.3
  2.5 0.4 mask_ham.1.refs_0_
  2.9 2.1 %collective-permute-start.4 = (bf16[1024,256]{1,0:T(8,128)(2,1)S(1)}, bf16[1024,256]{1,0:T(8,128)(2,1)S(1)}, u32[]{:S(2)}, u32[]{:S(2)}) collective-permute-start(bf16[1024,256]{1,0:T(8,128)(2,1)S(1)} %mask_ham.1.refs_0_), channel_id=1, source_target_pairs={{0,4},{2,6},{4,0},{6,2},{8,12},{10,14},{12,8},{14,10},{16,20},{18,... | collective-permute-start | bytes 1572872 | tf_op jit(solution)/shard_map/ppermute | solution.py:49
  5.0 1.3 %collective-permute-start.8 = (bf16[1024,256]{1,0:T(8,128)(2,1)S(1)}, bf16[1024,256]{1,0:T(8,128)(2,1)S(1)}, u32[]{:S(2)}, u32[]{:S(2)}) collective-permute-start(bf16[1024,256]{1,0:T(8,128)(2,1)S(1)} %mask_ham.1.refs_0_), channel_id=1, source_target_pairs={{0,24},{2,10},{4,28},{6,14},{8,0},{10,18},{12,4},{14,22},{16,8},{1... | collective-permute-start | bytes 1572872 | tf_op jit(solution)/shard_map/ppermute | solution.py:40
  6.3 0.5 mask_dens.1
  6.9 1.7 %collective-permute-start.12 = (bf16[512,512]{1,0:T(8,128)(2,1)S(1)}, bf16[512,512]{1,0:T(8,128)(2,1)S(1)}, u32[]{:S(2)}, u32[]{:S(2)}) collective-permute-start(bf16[512,512]{1,0:T(8,128)(2,1)S(1)} %get-tuple-element.36.refs_16_), channel_id=1, source_target_pairs={{0,224},{2,34},{4,228},{6,38},{8,232},{10,42},{12,236},{14,46},{16... | collective-permute-start | bytes 1572872 | tf_op jit(solution)/shard_map/ppermute | solution.py:33
  8.6 4.0 %collective-permute-start = (bf16[512,512]{1,0:T(8,128)(2,1)S(1)}, bf16[512,512]{1,0:T(8,128)(2,1)S(1)}, u32[]{:S(2)}, u32[]{:S(2)}) collective-permute-start(bf16[512,512]{1,0:T(8,128)(2,1)S(1)} %get-tuple-element.36.refs_16_), channel_id=1, source_target_pairs={{0,32},{2,226},{4,36},{6,230},{8,40},{10,234},{12,44},{14,238},{16... | collective-permute-start | bytes 1572872 | tf_op jit(solution)/shard_map/ppermute | solution.py:33
  12.5 1.4 %collective-permute-start.2 = (bf16[1024,256]{1,0:T(8,128)(2,1)S(1)}, bf16[1024,256]{1,0:T(8,128)(2,1)S(1)}, u32[]{:S(2)}, u32[]{:S(2)}) collective-permute-start(bf16[1024,256]{1,0:T(8,128)(2,1)S(1)} %mask_ham.1.refs_0_), channel_id=1, source_target_pairs={{0,8},{2,26},{4,12},{6,30},{8,16},{10,2},{12,20},{14,6},{16,24},{1... | collective-permute-start | bytes 1572872 | tf_op jit(solution)/shard_map/ppermute | solution.py:40
  14.0 1.4 %collective-permute-done.4.refs_8_ = bf16[1024,256]{1,0:T(8,128)(2,1)S(1)} collective-permute-done((bf16[1024,256]{1,0:T(8,128)(2,1)S(1)}, bf16[1024,256]{1,0:T(8,128)(2,1)S(1)}, u32[]{:S(2)}, u32[]{:S(2)}) %collective-permute-start.4) | collective-permute-done | bytes 524320 | tf_op jit(solution)/shard_map/ppermute | solution.py:49
  15.3 2.6 %collective-permute-start.10 = (bf16[1024,256]{1,0:T(8,128)(2,1)S(1)}, bf16[1024,256]{1,0:T(8,128)(2,1)S(1)}, u32[]{:S(2)}, u32[]{:S(2)}) collective-permute-start(bf16[1024,256]{1,0:T(8,128)(2,1)S(1)} %collective-permute-done.4.refs_8_), channel_id=1, source_target_pairs={{0,24},{2,10},{4,28},{6,14},{8,0},{10,18},{12,4},{14,22},{16,8},{1... | collective-permute-start | bytes 1572872 | tf_op jit(solution)/shard_map/ppermute | solution.py:40
  17.9 1.1 %collective-permute-done.12.refs_18_ = bf16[512,512]{1,0:T(8,128)(2,1)S(1)} collective-permute-done((bf16[512,512]{1,0:T(8,128)(2,1)S(1)}, bf16[512,512]{1,0:T(8,128)(2,1)S(1)}, u32[]{:S(2)}, u32[]{:S(2)}) %collective-permute-start.12) | collective-permute-done | bytes 524320 | tf_op jit(solution)/shard_map/ppermute | solution.py:33
  19.1 0.5 collective-permute-start.13
  19.5 1.8 %collective-permute-done.refs_17_ = bf16[512,512]{1,0:T(8,128)(2,1)S(1)} collective-permute-done((bf16[512,512]{1,0:T(8,128)(2,1)S(1)}, bf16[512,512]{1,0:T(8,128)(2,1)S(1)}, u32[]{:S(2)}, u32[]{:S(2)}) %collective-permute-start) | collective-permute-done | bytes 524320 | tf_op jit(solution)/shard_map/ppermute | solution.py:33
  21.3 3.2 %collective-permute-start.3 = (bf16[512,512]{1,0:T(8,128)(2,1)S(1)}, bf16[512,512]{1,0:T(8,128)(2,1)S(1)}, u32[]{:S(2)}, u32[]{:S(2)}) collective-permute-start(bf16[512,512]{1,0:T(8,128)(2,1)S(1)} %collective-permute-done.refs_17_), channel_id=1, source_target_pairs={{0,32},{2,226},{4,36},{6,230},{8,40},{10,234},{12,44},{14,238},{16... | collective-permute-start | bytes 1572872 | tf_op jit(solution)/shard_map/ppermute | solution.py:33
  24.5 5.7 %collective-permute-start.1 = (bf16[1024,256]{1,0:T(8,128)(2,1)S(1)}, bf16[1024,256]{1,0:T(8,128)(2,1)S(1)}, u32[]{:S(2)}, u32[]{:S(2)}) collective-permute-start(bf16[1024,256]{1,0:T(8,128)(2,1)S(1)} %mask_ham.1.refs_0_), channel_id=1, source_target_pairs={{0,2},{2,0},{4,6},{6,4},{8,10},{10,8},{12,14},{14,12},{16,18},{18,... | collective-permute-start | bytes 1572872 | tf_op jit(solution)/shard_map/ppermute | solution.py:49
  30.3 0.5 collective-permute-done.10.refs_12_
  30.8 1.0 collective-permute-start.11
  31.8 3.0 %collective-permute-start.17 = (bf16[512,512]{1,0:T(8,128)(2,1)S(1)}, bf16[512,512]{1,0:T(8,128)(2,1)S(1)}, u32[]{:S(2)}, u32[]{:S(2)}) collective-permute-start(bf16[512,512]{1,0:T(8,128)(2,1)S(1)} %collective-permute-done.3.refs_19_), channel_id=1, source_target_pairs={{0,32},{2,226},{4,36},{6,230},{8,40},{10,234},{12,44},{14,238},{16... | collective-permute-start | bytes 1572872 | tf_op jit(solution)/shard_map/ppermute | solution.py:33
  34.8 10.2 %collective-permute-start.5 = (bf16[1024,256]{1,0:T(8,128)(2,1)S(1)}, bf16[1024,256]{1,0:T(8,128)(2,1)S(1)}, u32[]{:S(2)}, u32[]{:S(2)}) collective-permute-start(bf16[1024,256]{1,0:T(8,128)(2,1)S(1)} %collective-permute-done.4.refs_8_), channel_id=1, source_target_pairs={{0,2},{2,0},{4,6},{6,4},{8,10},{10,8},{12,14},{14,12},{16,18},{18,... | collective-permute-start | bytes 1572872 | tf_op jit(solution)/shard_map/ppermute | solution.py:49
  45.0 2.3 %collective-permute-start.6 = (f32[8,512]{1,0:T(8,128)S(1)}, f32[8,512]{1,0:T(8,128)S(1)}, u32[]{:S(2)}, u32[]{:S(2)}) collective-permute-start(f32[8,512]{1,0:T(8,128)S(1)} %get-tuple-element.39), channel_id=1, source_target_pairs={{0,128},{2,130},{4,132},{6,134},{8,136},{10,138},{12,140},{14,142}... | collective-permute-start | bytes 49160 | tf_op jit(solution)/shard_map/ppermute | solution.py:33
  47.3 0.8 collective-permute-start.20
  48.1 3.8 %collective-permute-start.15 = (bf16[1024,256]{1,0:T(8,128)(2,1)S(1)}, bf16[1024,256]{1,0:T(8,128)(2,1)S(1)}, u32[]{:S(2)}, u32[]{:S(2)}) collective-permute-start(bf16[1024,256]{1,0:T(8,128)(2,1)S(1)} %collective-permute-done.11.refs_6_), channel_id=1, source_target_pairs={{0,2},{2,0},{4,6},{6,4},{8,10},{10,8},{12,14},{14,12},{16,18},{18,... | collective-permute-start | bytes 1572872 | tf_op jit(solution)/shard_map/ppermute | solution.py:49
  51.9 4.2 %collective-permute-start.18 = (bf16[1024,256]{1,0:T(8,128)(2,1)S(1)}, bf16[1024,256]{1,0:T(8,128)(2,1)S(1)}, u32[]{:S(2)}, u32[]{:S(2)}) collective-permute-start(bf16[1024,256]{1,0:T(8,128)(2,1)S(1)} %collective-permute-done.16.refs_10_), channel_id=1, source_target_pairs={{0,2},{2,0},{4,6},{6,4},{8,10},{10,8},{12,14},{14,12},{16,18},{18,... | collective-permute-start | bytes 1572872 | tf_op jit(solution)/shard_map/ppermute | solution.py:49
  56.1 2.1 %collective-permute-start.21 = (bf16[1024,256]{1,0:T(8,128)(2,1)S(1)}, bf16[1024,256]{1,0:T(8,128)(2,1)S(1)}, u32[]{:S(2)}, u32[]{:S(2)}) collective-permute-start(bf16[1024,256]{1,0:T(8,128)(2,1)S(1)} %collective-permute-done.20.refs_14_), channel_id=1, source_target_pairs={{0,2},{2,0},{4,6},{6,4},{8,10},{10,8},{12,14},{14,12},{16,18},{18,... | collective-permute-start | bytes 1572872 | tf_op jit(solution)/shard_map/ppermute | solution.py:49
  58.3 0.4 collective-permute-start.9
  58.7 3.4 %collective-permute-start.22 = (bf16[512,512]{1,0:T(8,128)(2,1)S(1)}, bf16[512,512]{1,0:T(8,128)(2,1)S(1)}, u32[]{:S(2)}, u32[]{:S(2)}) collective-permute-start(bf16[512,512]{1,0:T(8,128)(2,1)S(1)} %collective-permute-done.17.refs_21_), channel_id=1, source_target_pairs={{0,32},{2,226},{4,36},{6,230},{8,40},{10,234},{12,44},{14,238},{16... | collective-permute-start | bytes 1572872 | tf_op jit(solution)/shard_map/ppermute | solution.py:33
  62.2 6.3 %early.1 = (f32[512,512]{1,0:T(8,128)S(1)}, f32[512,512]{1,0:T(8,128)S(1)}, bf16[2,1024,256]{2,1,0:T(8,128)(2,1)S(1)}, f32[8,1024]{1,0:T(8,128)S(1)}) custom-call(bf16[1024,256]{1,0:T(8,128)(2,1)S(1)} %mask_ham.1.refs_0_, bf16[1024,256]{1,0:T(8,128)(2,1)S(1)} %collective-permute-done.1.refs_1_, bf16[1024,256]{1,0:T(8,128)(2,1)S(1)} %collective-permute-done.2.refs_2_, ...), custom_call_target="tpu_custom_call" | custom-call | flops 4294967296 | bytes 4194304 | tf_op jit(solution)/shard_map/early/pallas_call | solution.py:189
  68.5 1.0 copy-done.1
  69.5 0.3 collective-permute-start.24
  69.9 2.4 %collective-permute-start.25 = (f32[8,1024]{1,0:T(8,128)S(1)}, f32[8,1024]{1,0:T(8,128)S(1)}, u32[]{:S(2)}, u32[]{:S(2)}) collective-permute-start(f32[8,1024]{1,0:T(8,128)S(1)} %scatter.4), channel_id=1, source_target_pairs={{0,5},{1,4},{2,7},{3,6},{4,0},{5,1},{6,2},{7,3},{8,13},{9,12},{10,... | collective-permute-start | bytes 98312 | tf_op jit(solution)/shard_map/ppermute | solution.py:62
  72.3 1.3 %collective-permute-start.26 = (f32[8,1024]{1,0:T(8,128)S(1)}, f32[8,1024]{1,0:T(8,128)S(1)}, u32[]{:S(2)}, u32[]{:S(2)}) collective-permute-start(f32[8,1024]{1,0:T(8,128)S(1)} %scatter.4), channel_id=1, source_target_pairs={{0,1},{1,0},{2,3},{3,2},{4,5},{5,4},{6,7},{7,6},{8,9},{9,8},{10,11... | collective-permute-start | bytes 98312 | tf_op jit(solution)/shard_map/ppermute | solution.py:62
  73.6 1.2 %copy-done.2 = f32[512,512]{1,0:T(8,128)S(1)} copy-done((f32[512,512]{1,0:T(8,128)S(1)}, f32[512,512]{1,0:T(8,128)}, u32[]{:S(2)}) %copy-start.2) | copy-done | bytes 1048600
  74.8 1.2 %late.1 = (f32[256,512]{1,0:T(8,128)S(1)}, f32[256,512]{1,0:T(8,128)}) custom-call(f32[512,512]{1,0:T(8,128)S(1)} %copy-done.2, bf16[2,1024,256]{2,1,0:T(8,128)(2,1)S(1)} %get-tuple-element.51.ham_ref, bf16[512,512]{1,0:T(8,128)(2,1)S(1)} %collective-permute-done.22.den_ref), custom_call_target="tpu_custom_call" | custom-call | tf_op jit(solution)/shard_map/late/pallas_call | solution.py:220
  76.0 1.7 %collective-permute-start.23 = (f32[256,512]{1,0:T(8,128)S(1)}, f32[256,512]{1,0:T(8,128)S(1)}, u32[]{:S(2)}, u32[]{:S(2)}) collective-permute-start(f32[256,512]{1,0:T(8,128)S(1)} %get-tuple-element.52), channel_id=1, source_target_pairs={{0,1},{1,0},{2,3},{3,2},{4,5},{5,4},{6,7},{7,6},{8,9},{9,8},{10,11... | collective-permute-start | bytes 1572872 | tf_op jit(solution)/shard_map/ppermute | solution.py:53
  77.9 2.7 %collective-permute-start.29 = (f32[8,1024]{1,0:T(8,128)S(1)}, f32[8,1024]{1,0:T(8,128)S(1)}, u32[]{:S(2)}, u32[]{:S(2)}) collective-permute-start(f32[8,1024]{1,0:T(8,128)S(1)} %add_add_fusion.1), channel_id=1, source_target_pairs={{0,24},{2,26},{4,28},{6,30},{8,0},{10,2},{12,4},{14,6},{16,8},{18,... | collective-permute-start | bytes 98312 | tf_op jit(solution)/shard_map/ppermute | solution.py:45
  80.5 1.6 %collective-permute-done.28 = f32[8,1024]{1,0:T(8,128)S(1)} collective-permute-done((f32[8,1024]{1,0:T(8,128)S(1)}, f32[8,1024]{1,0:T(8,128)S(1)}, u32[]{:S(2)}, u32[]{:S(2)}) %collective-permute-start.28) | collective-permute-done | bytes 32800 | tf_op jit(solution)/shard_map/ppermute | solution.py:45
  82.1 3.0 %collective-permute-done.30 = f32[8,1024]{1,0:T(8,128)S(1)} collective-permute-done((f32[8,1024]{1,0:T(8,128)S(1)}, f32[8,1024]{1,0:T(8,128)S(1)}, u32[]{:S(2)}, u32[]{:S(2)}) %collective-permute-start.30) | collective-permute-done | bytes 32800 | tf_op jit(solution)/shard_map/ppermute | solution.py:45
  85.1 2.1 %collective-permute-start.31 = (f32[8,1024]{1,0:T(8,128)S(1)}, f32[8,1024]{1,0:T(8,128)S(1)}, u32[]{:S(2)}, u32[]{:S(2)}) collective-permute-start(f32[8,1024]{1,0:T(8,128)S(1)} %add_add_fusion), channel_id=1, source_target_pairs={{0,2},{2,0},{4,6},{6,4},{8,10},{10,8},{12,14},{14,12},{16,18},{18,... | collective-permute-start | bytes 98312 | tf_op jit(solution)/shard_map/ppermute | solution.py:49
  87.3 1.3 %collective-permute-start.27 = (f32[256,512]{1,0:T(8,128)}, f32[256,512]{1,0:T(8,128)}, u32[]{:S(2)}, u32[]{:S(2)}) collective-permute-start(f32[256,512]{1,0:T(8,128)} %get-tuple-element.56), channel_id=1, source_target_pairs={{0,1},{1,0},{2,3},{3,2},{4,5},{5,4},{6,7},{7,6},{8,9},{9,8},{10,11... | collective-permute-start | bytes 1572872 | tf_op jit(solution)/shard_map/ppermute | solution.py:53
  88.6 2.1 %collective-permute-done.23.first_ref = f32[256,512]{1,0:T(8,128)S(1)} collective-permute-done((f32[256,512]{1,0:T(8,128)S(1)}, f32[256,512]{1,0:T(8,128)S(1)}, u32[]{:S(2)}, u32[]{:S(2)}) %collective-permute-start.23) | collective-permute-done | bytes 524320 | tf_op jit(solution)/shard_map/ppermute | solution.py:53
  91.0 0.3 convolution_bitcast_fusion
  91.4 0.8 collective-permute-start.32
  92.1 0.4 kept.1.kept_ref
  92.6 3.0 %collective-permute-done.32 = f32[16,128]{1,0:T(8,128)S(1)} collective-permute-done((f32[16,128]{1,0:T(8,128)S(1)}, f32[16,128]{1,0:T(8,128)S(1)}, u32[]{:S(2)}, u32[]{:S(2)}) %collective-permute-start.32) | collective-permute-done | bytes 8224 | tf_op jit(solution)/shard_map/ppermute | solution.py:332
  95.6 0.6 pad_maximum_fusion
  96.2 6.5 %collective-permute-done.27.second_ref = f32[256,512]{1,0:T(8,128)} collective-permute-done((f32[256,512]{1,0:T(8,128)}, f32[256,512]{1,0:T(8,128)}, u32[]{:S(2)}, u32[]{:S(2)}) %collective-permute-start.27) | collective-permute-done | bytes 524320 | tf_op jit(solution)/shard_map/ppermute | solution.py:53
  102.6 1.9 %finish.1 = bf16[512,512]{1,0:T(8,128)(2,1)} custom-call(f32[512,512]{1,0:T(8,128)S(1)} %kept.1.kept_ref, f32[256,512]{1,0:T(8,128)S(1)} %collective-permute-done.23.first_ref, f32[256,512]{1,0:T(8,128)} %collective-permute-done.27.second_ref), custom_call_target="tpu_custom_call" | custom-call | tf_op jit(solution)/shard_map/finish/pallas_call | solution.py:251
  (56 shorter events, 0.9 us)
Async XLA Ops:
  0.6 90.1 %copy-start = (bf16[64,16,128]{2,1,0:T(8,128)(2,1)S(1)}, bf16[64,16,128]{2,1,0:T(8,128)(2,1)}, u32[]{:S(2)}) copy-start(bf16[64,16,128]{2,1,0:T(8,128)(2,1)} %param.12) | copy-start | bytes 786436
  1.4 1.0 copy-start.3
  2.5 3.8 %copy-start.4 = (bf16[512,512]{1,0:T(8,128)(2,1)S(1)}, bf16[512,512]{1,0:T(8,128)(2,1)}, u32[]{:S(2)}) copy-start(bf16[512,512]{1,0:T(8,128)(2,1)} %matrix_ref.3) | copy-start | bytes 1572868
  2.5 3.8 %copy-start.5 = (s32[8,8]{1,0:T(8,128)S(1)}, s32[8,8]{1,0:T(8,128)}, u32[]{:S(2)}) copy-start(s32[8,8]{1,0:T(8,128)} %pattern_ref.2) | copy-start | bytes 772
  2.9 12.4 %collective-permute-start.4 = (bf16[1024,256]{1,0:T(8,128)(2,1)S(1)}, bf16[1024,256]{1,0:T(8,128)(2,1)S(1)}, u32[]{:S(2)}, u32[]{:S(2)}) collective-permute-start(bf16[1024,256]{1,0:T(8,128)(2,1)S(1)} %mask_ham.1.refs_0_), channel_id=1, source_target_pairs={{0,4},{2,6},{4,0},{6,2},{8,12},{10,14},{12,8},{14,10},{16,20},{18,... | collective-permute-start | bytes 1572872 | tf_op jit(solution)/shard_map/ppermute | solution.py:49
  5.0 10.3 %collective-permute-start.8 = (bf16[1024,256]{1,0:T(8,128)(2,1)S(1)}, bf16[1024,256]{1,0:T(8,128)(2,1)S(1)}, u32[]{:S(2)}, u32[]{:S(2)}) collective-permute-start(bf16[1024,256]{1,0:T(8,128)(2,1)S(1)} %mask_ham.1.refs_0_), channel_id=1, source_target_pairs={{0,24},{2,10},{4,28},{6,14},{8,0},{10,18},{12,4},{14,22},{16,8},{1... | collective-permute-start | bytes 1572872 | tf_op jit(solution)/shard_map/ppermute | solution.py:40
  6.9 55.3 %copy-start.6 = (s32[8]{0:T(128)S(1)}, s32[8]{0:T(128)}, u32[]{:S(2)}) copy-start(s32[8]{0:T(128)} %param.13) | copy-start | bytes 100
  6.9 12.2 %collective-permute-start.12 = (bf16[512,512]{1,0:T(8,128)(2,1)S(1)}, bf16[512,512]{1,0:T(8,128)(2,1)S(1)}, u32[]{:S(2)}, u32[]{:S(2)}) collective-permute-start(bf16[512,512]{1,0:T(8,128)(2,1)S(1)} %get-tuple-element.36.refs_16_), channel_id=1, source_target_pairs={{0,224},{2,34},{4,228},{6,38},{8,232},{10,42},{12,236},{14,46},{16... | collective-permute-start | bytes 1572872 | tf_op jit(solution)/shard_map/ppermute | solution.py:33
  8.6 12.8 %collective-permute-start = (bf16[512,512]{1,0:T(8,128)(2,1)S(1)}, bf16[512,512]{1,0:T(8,128)(2,1)S(1)}, u32[]{:S(2)}, u32[]{:S(2)}) collective-permute-start(bf16[512,512]{1,0:T(8,128)(2,1)S(1)} %get-tuple-element.36.refs_16_), channel_id=1, source_target_pairs={{0,32},{2,226},{4,36},{6,230},{8,40},{10,234},{12,44},{14,238},{16... | collective-permute-start | bytes 1572872 | tf_op jit(solution)/shard_map/ppermute | solution.py:33
  12.5 17.7 %collective-permute-start.2 = (bf16[1024,256]{1,0:T(8,128)(2,1)S(1)}, bf16[1024,256]{1,0:T(8,128)(2,1)S(1)}, u32[]{:S(2)}, u32[]{:S(2)}) collective-permute-start(bf16[1024,256]{1,0:T(8,128)(2,1)S(1)} %mask_ham.1.refs_0_), channel_id=1, source_target_pairs={{0,8},{2,26},{4,12},{6,30},{8,16},{10,2},{12,20},{14,6},{16,24},{1... | collective-permute-start | bytes 1572872 | tf_op jit(solution)/shard_map/ppermute | solution.py:40
  15.3 15.4 %collective-permute-start.10 = (bf16[1024,256]{1,0:T(8,128)(2,1)S(1)}, bf16[1024,256]{1,0:T(8,128)(2,1)S(1)}, u32[]{:S(2)}, u32[]{:S(2)}) collective-permute-start(bf16[1024,256]{1,0:T(8,128)(2,1)S(1)} %collective-permute-done.4.refs_8_), channel_id=1, source_target_pairs={{0,24},{2,10},{4,28},{6,14},{8,0},{10,18},{12,4},{14,22},{16,8},{1... | collective-permute-start | bytes 1572872 | tf_op jit(solution)/shard_map/ppermute | solution.py:40
  19.1 12.7 %collective-permute-start.13 = (bf16[512,512]{1,0:T(8,128)(2,1)S(1)}, bf16[512,512]{1,0:T(8,128)(2,1)S(1)}, u32[]{:S(2)}, u32[]{:S(2)}) collective-permute-start(bf16[512,512]{1,0:T(8,128)(2,1)S(1)} %collective-permute-done.12.refs_18_), channel_id=1, source_target_pairs={{0,224},{2,34},{4,228},{6,38},{8,232},{10,42},{12,236},{14,46},{16... | collective-permute-start | bytes 1572872 | tf_op jit(solution)/shard_map/ppermute | solution.py:33
  21.3 10.5 %collective-permute-start.3 = (bf16[512,512]{1,0:T(8,128)(2,1)S(1)}, bf16[512,512]{1,0:T(8,128)(2,1)S(1)}, u32[]{:S(2)}, u32[]{:S(2)}) collective-permute-start(bf16[512,512]{1,0:T(8,128)(2,1)S(1)} %collective-permute-done.refs_17_), channel_id=1, source_target_pairs={{0,32},{2,226},{4,36},{6,230},{8,40},{10,234},{12,44},{14,238},{16... | collective-permute-start | bytes 1572872 | tf_op jit(solution)/shard_map/ppermute | solution.py:33
  24.5 10.3 %collective-permute-start.1 = (bf16[1024,256]{1,0:T(8,128)(2,1)S(1)}, bf16[1024,256]{1,0:T(8,128)(2,1)S(1)}, u32[]{:S(2)}, u32[]{:S(2)}) collective-permute-start(bf16[1024,256]{1,0:T(8,128)(2,1)S(1)} %mask_ham.1.refs_0_), channel_id=1, source_target_pairs={{0,2},{2,0},{4,6},{6,4},{8,10},{10,8},{12,14},{14,12},{16,18},{18,... | collective-permute-start | bytes 1572872 | tf_op jit(solution)/shard_map/ppermute | solution.py:49
  30.3 14.7 %collective-permute-start.16 = (bf16[1024,256]{1,0:T(8,128)(2,1)S(1)}, bf16[1024,256]{1,0:T(8,128)(2,1)S(1)}, u32[]{:S(2)}, u32[]{:S(2)}) collective-permute-start(bf16[1024,256]{1,0:T(8,128)(2,1)S(1)} %collective-permute-done.4.refs_8_), channel_id=1, source_target_pairs={{0,8},{2,26},{4,12},{6,30},{8,16},{10,2},{12,20},{14,6},{16,24},{1... | collective-permute-start | bytes 1572872 | tf_op jit(solution)/shard_map/ppermute | solution.py:40
  30.8 16.5 %collective-permute-start.11 = (bf16[1024,256]{1,0:T(8,128)(2,1)S(1)}, bf16[1024,256]{1,0:T(8,128)(2,1)S(1)}, u32[]{:S(2)}, u32[]{:S(2)}) collective-permute-start(bf16[1024,256]{1,0:T(8,128)(2,1)S(1)} %collective-permute-done.8.refs_4_), channel_id=1, source_target_pairs={{0,24},{2,10},{4,28},{6,14},{8,0},{10,18},{12,4},{14,22},{16,8},{1... | collective-permute-start | bytes 1572872 | tf_op jit(solution)/shard_map/ppermute | solution.py:40
  31.8 16.3 %collective-permute-start.14 = (bf16[512,512]{1,0:T(8,128)(2,1)S(1)}, bf16[512,512]{1,0:T(8,128)(2,1)S(1)}, u32[]{:S(2)}, u32[]{:S(2)}) collective-permute-start(bf16[512,512]{1,0:T(8,128)(2,1)S(1)} %collective-permute-done.13.refs_20_), channel_id=1, source_target_pairs={{0,224},{2,34},{4,228},{6,38},{8,232},{10,42},{12,236},{14,46},{16... | collective-permute-start | bytes 1572872 | tf_op jit(solution)/shard_map/ppermute | solution.py:33
  31.8 20.1 %collective-permute-start.17 = (bf16[512,512]{1,0:T(8,128)(2,1)S(1)}, bf16[512,512]{1,0:T(8,128)(2,1)S(1)}, u32[]{:S(2)}, u32[]{:S(2)}) collective-permute-start(bf16[512,512]{1,0:T(8,128)(2,1)S(1)} %collective-permute-done.3.refs_19_), channel_id=1, source_target_pairs={{0,32},{2,226},{4,36},{6,230},{8,40},{10,234},{12,44},{14,238},{16... | collective-permute-start | bytes 1572872 | tf_op jit(solution)/shard_map/ppermute | solution.py:33
  34.8 21.2 %collective-permute-start.5 = (bf16[1024,256]{1,0:T(8,128)(2,1)S(1)}, bf16[1024,256]{1,0:T(8,128)(2,1)S(1)}, u32[]{:S(2)}, u32[]{:S(2)}) collective-permute-start(bf16[1024,256]{1,0:T(8,128)(2,1)S(1)} %collective-permute-done.4.refs_8_), channel_id=1, source_target_pairs={{0,2},{2,0},{4,6},{6,4},{8,10},{10,8},{12,14},{14,12},{16,18},{18,... | collective-permute-start | bytes 1572872 | tf_op jit(solution)/shard_map/ppermute | solution.py:49
  45.0 11.1 %collective-permute-start.6 = (f32[8,512]{1,0:T(8,128)S(1)}, f32[8,512]{1,0:T(8,128)S(1)}, u32[]{:S(2)}, u32[]{:S(2)}) collective-permute-start(f32[8,512]{1,0:T(8,128)S(1)} %get-tuple-element.39), channel_id=1, source_target_pairs={{0,128},{2,130},{4,132},{6,134},{8,136},{10,138},{12,140},{14,142}... | collective-permute-start | bytes 49160 | tf_op jit(solution)/shard_map/ppermute | solution.py:33
  47.3 8.8 %collective-permute-start.20 = (bf16[1024,256]{1,0:T(8,128)(2,1)S(1)}, bf16[1024,256]{1,0:T(8,128)(2,1)S(1)}, u32[]{:S(2)}, u32[]{:S(2)}) collective-permute-start(bf16[1024,256]{1,0:T(8,128)(2,1)S(1)} %collective-permute-done.16.refs_10_), channel_id=1, source_target_pairs={{0,8},{2,26},{4,12},{6,30},{8,16},{10,2},{12,20},{14,6},{16,24},{1... | collective-permute-start | bytes 1572872 | tf_op jit(solution)/shard_map/ppermute | solution.py:40
  48.1 8.1 %collective-permute-start.15 = (bf16[1024,256]{1,0:T(8,128)(2,1)S(1)}, bf16[1024,256]{1,0:T(8,128)(2,1)S(1)}, u32[]{:S(2)}, u32[]{:S(2)}) collective-permute-start(bf16[1024,256]{1,0:T(8,128)(2,1)S(1)} %collective-permute-done.11.refs_6_), channel_id=1, source_target_pairs={{0,2},{2,0},{4,6},{6,4},{8,10},{10,8},{12,14},{14,12},{16,18},{18,... | collective-permute-start | bytes 1572872 | tf_op jit(solution)/shard_map/ppermute | solution.py:49
  51.9 6.3 %collective-permute-start.18 = (bf16[1024,256]{1,0:T(8,128)(2,1)S(1)}, bf16[1024,256]{1,0:T(8,128)(2,1)S(1)}, u32[]{:S(2)}, u32[]{:S(2)}) collective-permute-start(bf16[1024,256]{1,0:T(8,128)(2,1)S(1)} %collective-permute-done.16.refs_10_), channel_id=1, source_target_pairs={{0,2},{2,0},{4,6},{6,4},{8,10},{10,8},{12,14},{14,12},{16,18},{18,... | collective-permute-start | bytes 1572872 | tf_op jit(solution)/shard_map/ppermute | solution.py:49
  56.0 2.3 %collective-permute-start.7 = (bf16[1024,256]{1,0:T(8,128)(2,1)S(1)}, bf16[1024,256]{1,0:T(8,128)(2,1)S(1)}, u32[]{:S(2)}, u32[]{:S(2)}) collective-permute-start(bf16[1024,256]{1,0:T(8,128)(2,1)S(1)} %collective-permute-done.2.refs_2_), channel_id=1, source_target_pairs={{0,2},{2,0},{4,6},{6,4},{8,10},{10,8},{12,14},{14,12},{16,18},{18,... | collective-permute-start | bytes 1572872 | tf_op jit(solution)/shard_map/ppermute | solution.py:49
  56.1 6.0 %collective-permute-start.21 = (bf16[1024,256]{1,0:T(8,128)(2,1)S(1)}, bf16[1024,256]{1,0:T(8,128)(2,1)S(1)}, u32[]{:S(2)}, u32[]{:S(2)}) collective-permute-start(bf16[1024,256]{1,0:T(8,128)(2,1)S(1)} %collective-permute-done.20.refs_14_), channel_id=1, source_target_pairs={{0,2},{2,0},{4,6},{6,4},{8,10},{10,8},{12,14},{14,12},{16,18},{18,... | collective-permute-start | bytes 1572872 | tf_op jit(solution)/shard_map/ppermute | solution.py:49
  58.2 3.9 %collective-permute-start.19 = (bf16[1024,256]{1,0:T(8,128)(2,1)S(1)}, bf16[1024,256]{1,0:T(8,128)(2,1)S(1)}, u32[]{:S(2)}, u32[]{:S(2)}) collective-permute-start(bf16[1024,256]{1,0:T(8,128)(2,1)S(1)} %collective-permute-done.10.refs_12_), channel_id=1, source_target_pairs={{0,2},{2,0},{4,6},{6,4},{8,10},{10,8},{12,14},{14,12},{16,18},{18,... | collective-permute-start | bytes 1572872 | tf_op jit(solution)/shard_map/ppermute | solution.py:49
  58.3 3.8 %collective-permute-start.9 = (bf16[1024,256]{1,0:T(8,128)(2,1)S(1)}, bf16[1024,256]{1,0:T(8,128)(2,1)S(1)}, u32[]{:S(2)}, u32[]{:S(2)}) collective-permute-start(bf16[1024,256]{1,0:T(8,128)(2,1)S(1)} %collective-permute-done.8.refs_4_), channel_id=1, source_target_pairs={{0,2},{2,0},{4,6},{6,4},{8,10},{10,8},{12,14},{14,12},{16,18},{18,... | collective-permute-start | bytes 1572872 | tf_op jit(solution)/shard_map/ppermute | solution.py:49
  58.7 14.8 %collective-permute-start.22 = (bf16[512,512]{1,0:T(8,128)(2,1)S(1)}, bf16[512,512]{1,0:T(8,128)(2,1)S(1)}, u32[]{:S(2)}, u32[]{:S(2)}) collective-permute-start(bf16[512,512]{1,0:T(8,128)(2,1)S(1)} %collective-permute-done.17.refs_21_), channel_id=1, source_target_pairs={{0,32},{2,226},{4,36},{6,230},{8,40},{10,234},{12,44},{14,238},{16... | collective-permute-start | bytes 1572872 | tf_op jit(solution)/shard_map/ppermute | solution.py:33
  68.4 1.0 copy-start.1
  69.5 8.2 %collective-permute-start.24 = (f32[8,1024]{1,0:T(8,128)S(1)}, f32[8,1024]{1,0:T(8,128)S(1)}, u32[]{:S(2)}, u32[]{:S(2)}) collective-permute-start(f32[8,1024]{1,0:T(8,128)S(1)} %scatter.4), channel_id=1, source_target_pairs={{0,4},{1,5},{2,6},{3,7},{4,1},{5,0},{6,3},{7,2},{8,12},{9,13},{10,... | collective-permute-start | bytes 98312 | tf_op jit(solution)/shard_map/ppermute | solution.py:62
  69.9 7.9 %collective-permute-start.25 = (f32[8,1024]{1,0:T(8,128)S(1)}, f32[8,1024]{1,0:T(8,128)S(1)}, u32[]{:S(2)}, u32[]{:S(2)}) collective-permute-start(f32[8,1024]{1,0:T(8,128)S(1)} %scatter.4), channel_id=1, source_target_pairs={{0,5},{1,4},{2,7},{3,6},{4,0},{5,1},{6,2},{7,3},{8,13},{9,12},{10,... | collective-permute-start | bytes 98312 | tf_op jit(solution)/shard_map/ppermute | solution.py:62
  72.3 5.5 %collective-permute-start.26 = (f32[8,1024]{1,0:T(8,128)S(1)}, f32[8,1024]{1,0:T(8,128)S(1)}, u32[]{:S(2)}, u32[]{:S(2)}) collective-permute-start(f32[8,1024]{1,0:T(8,128)S(1)} %scatter.4), channel_id=1, source_target_pairs={{0,1},{1,0},{2,3},{3,2},{4,5},{5,4},{6,7},{7,6},{8,9},{9,8},{10,11... | collective-permute-start | bytes 98312 | tf_op jit(solution)/shard_map/ppermute | solution.py:62
  73.6 1.2 %copy-start.2 = (f32[512,512]{1,0:T(8,128)S(1)}, f32[512,512]{1,0:T(8,128)}, u32[]{:S(2)}) copy-start(f32[512,512]{1,0:T(8,128)} %copy-done.1) | copy-start | bytes 3145732
  76.0 14.7 %collective-permute-start.23 = (f32[256,512]{1,0:T(8,128)S(1)}, f32[256,512]{1,0:T(8,128)S(1)}, u32[]{:S(2)}, u32[]{:S(2)}) collective-permute-start(f32[256,512]{1,0:T(8,128)S(1)} %get-tuple-element.52), channel_id=1, source_target_pairs={{0,1},{1,0},{2,3},{3,2},{4,5},{5,4},{6,7},{7,6},{8,9},{9,8},{10,11... | collective-permute-start | bytes 1572872 | tf_op jit(solution)/shard_map/ppermute | solution.py:53
  77.8 4.3 %collective-permute-start.28 = (f32[8,1024]{1,0:T(8,128)S(1)}, f32[8,1024]{1,0:T(8,128)S(1)}, u32[]{:S(2)}, u32[]{:S(2)}) collective-permute-start(f32[8,1024]{1,0:T(8,128)S(1)} %add_add_fusion.1), channel_id=1, source_target_pairs={{0,8},{2,10},{4,12},{6,14},{8,16},{10,18},{12,20},{14,22},{16,24},... | collective-permute-start | bytes 98312 | tf_op jit(solution)/shard_map/ppermute | solution.py:45
  77.9 4.3 %collective-permute-start.29 = (f32[8,1024]{1,0:T(8,128)S(1)}, f32[8,1024]{1,0:T(8,128)S(1)}, u32[]{:S(2)}, u32[]{:S(2)}) collective-permute-start(f32[8,1024]{1,0:T(8,128)S(1)} %add_add_fusion.1), channel_id=1, source_target_pairs={{0,24},{2,26},{4,28},{6,30},{8,0},{10,2},{12,4},{14,6},{16,8},{18,... | collective-permute-start | bytes 98312 | tf_op jit(solution)/shard_map/ppermute | solution.py:45
  80.5 4.6 %collective-permute-start.30 = (f32[8,1024]{1,0:T(8,128)S(1)}, f32[8,1024]{1,0:T(8,128)S(1)}, u32[]{:S(2)}, u32[]{:S(2)}) collective-permute-start(f32[8,1024]{1,0:T(8,128)S(1)} %add_add_fusion.1), channel_id=1, source_target_pairs={{0,16},{2,18},{4,20},{6,22},{8,24},{10,26},{12,28},{14,30},{16,0},... | collective-permute-start | bytes 98312 | tf_op jit(solution)/shard_map/ppermute | solution.py:45
  85.1 3.5 %collective-permute-start.31 = (f32[8,1024]{1,0:T(8,128)S(1)}, f32[8,1024]{1,0:T(8,128)S(1)}, u32[]{:S(2)}, u32[]{:S(2)}) collective-permute-start(f32[8,1024]{1,0:T(8,128)S(1)} %add_add_fusion), channel_id=1, source_target_pairs={{0,2},{2,0},{4,6},{6,4},{8,10},{10,8},{12,14},{14,12},{16,18},{18,... | collective-permute-start | bytes 98312 | tf_op jit(solution)/shard_map/ppermute | solution.py:49
  87.3 15.3 %collective-permute-start.27 = (f32[256,512]{1,0:T(8,128)}, f32[256,512]{1,0:T(8,128)}, u32[]{:S(2)}, u32[]{:S(2)}) collective-permute-start(f32[256,512]{1,0:T(8,128)} %get-tuple-element.56), channel_id=1, source_target_pairs={{0,1},{1,0},{2,3},{3,2},{4,5},{5,4},{6,7},{7,6},{8,9},{9,8},{10,11... | collective-permute-start | bytes 1572872 | tf_op jit(solution)/shard_map/ppermute | solution.py:53
  91.4 4.2 %collective-permute-start.32 = (f32[16,128]{1,0:T(8,128)S(1)}, f32[16,128]{1,0:T(8,128)S(1)}, u32[]{:S(2)}, u32[]{:S(2)}) collective-permute-start(f32[16,128]{1,0:T(8,128)S(1)} %slice_bitcast_fusion.2), channel_id=1, source_target_pairs={{0,32},{32,64},{64,96},{96,128},{128,160},{160,192},{192,224},{224... | collective-permute-start | bytes 24584 | tf_op jit(solution)/shard_map/ppermute | solution.py:332

commit v4 on v3

--- a/solution.py
+++ b/solution.py
@@ -138,9 +138,7 @@
 def early_kernel(*refs):
     n_ham, n_den = len(HAM_KEYS), len(DEN_KEYS) - 1
     ham_refs, den_refs, far_ref = refs[:n_ham], refs[n_ham : n_ham + n_den], refs[n_ham + n_den]
-    other_out, own_out, ham_far_out, sums_ref, other_ref, own_ref, ham_far_ref, den_buf, sems = refs[
-        n_ham + n_den + 1 :
-    ]
+    other_out, own_ref, ham_far_ref, sums_ref, other_ref, den_buf, sem = refs[n_ham + n_den + 1 :]
     row, y, x, core, rep = place()
     rows = own_ref.shape[0]
     for n in range(n_den):
@@ -158,13 +156,11 @@
         def _():
             ham_far_ref[half] = ham_refs[n][...]
 
-    out = pltpu.make_async_copy(ham_far_ref, ham_far_out, sems.at[0])
-    out.start()
-    outs = [out]
     sums_ref[...] = split_dot(far_ref[:, :half_size], ham_far_ref[0]) + split_dot(
         far_ref[:, half_size:], ham_far_ref[1]
     )
-    for i, (part, total, total_out) in enumerate(((1 - rep, other_ref, other_out), (rep, own_ref, own_out))):
+    out = pltpu.make_async_copy(other_ref, other_out, sem)
+    for part, total in ((1 - rep, other_ref), (rep, own_ref)):
         span = pl.ds(pl.multiple_of(part * rows, rows), rows)
         for n, (chip, half) in enumerate(places):
             den = den_buf[chip, pl.ds(pl.multiple_of(half * half_size, half_size), half_size), :]
@@ -173,12 +169,10 @@
                 total[...] = term
             else:
                 total[...] += term
-        out = pltpu.make_async_copy(total, total_out, sems.at[1 + i])
-        out.start()
-        outs.append(out)
+        if total is other_ref:
+            out.start()
         sums_ref[:, span] += row_sums(total)
-    for out in outs:
-        out.wait()
+    out.wait()
 
 
 def early(ham_blocks, den_blocks, far_sums):
@@ -188,11 +182,16 @@
     shapes = [((rows // 2, cols), F32), ((rows // 2, cols), F32), ((2, rows, half), BF16)]
     return pl.pallas_call(
         early_kernel,
-        out_shape=[jax.ShapeDtypeStruct(*shape) for shape in shapes] + [jax.ShapeDtypeStruct((8, rows), F32)],
+        out_shape=[pltpu.HBM(*shapes[0])]
+        + [jax.ShapeDtypeStruct(*shape) for shape in shapes[1:]]
+        + [jax.ShapeDtypeStruct((8, rows), F32)],
         in_specs=[pl.BlockSpec(memory_space=pltpu.VMEM)] * n,
-        out_specs=[pl.BlockSpec(memory_space=pltpu.HBM)] * 3 + [pl.BlockSpec(memory_space=pltpu.VMEM)],
-        scratch_shapes=[pltpu.VMEM(*shape) for shape in shapes]
-        + [pltpu.VMEM((NZ, depth, cols), BF16), pltpu.SemaphoreType.DMA((3,))],
+        out_specs=[pl.BlockSpec(memory_space=pltpu.HBM)] + [pl.BlockSpec(memory_space=pltpu.VMEM)] * 3,
+        scratch_shapes=[
+            pltpu.VMEM(*shapes[0]),
+            pltpu.VMEM((NZ, depth, cols), BF16),
+            pltpu.SemaphoreType.DMA,
+        ],
         compiler_params=pltpu.CompilerParams(vmem_limit_bytes=16 * MIB),
         cost_estimate=pl.CostEstimate(
             flops=2 * rows * cols * depth * NZ, bytes_accessed=4 * MIB, transcendentals=0
@@ -208,11 +207,14 @@
     return term + jnp.dot(ham_ref[1, span], den_ref[half:], preferred_element_type=F32)
 
 
-def late_kernel(other_ref, ham_ref, den_ref, first_out, second_out):
+def late_kernel(other_ref, ham_ref, den_ref, first_out, second_out, other_buf, sem):
     rows, cut = other_ref.shape[0], first_out.shape[0]
+    copy = pltpu.make_async_copy(other_ref, other_buf, sem)
+    copy.start()
     term = far_term((1 - lax.axis_index("rep")) * rows, rows, ham_ref, den_ref)
-    first_out[...] = other_ref[:cut] + term[:cut]
-    second_out[...] = other_ref[cut:] + term[cut:]
+    copy.wait()
+    first_out[...] = other_buf[:cut] + term[:cut]
+    second_out[...] = other_buf[cut:] + term[cut:]
 
 
 def late(other, ham_far, den_far):
@@ -220,10 +222,11 @@
     return pl.pallas_call(
         late_kernel,
         out_shape=[jax.ShapeDtypeStruct((n, cols), F32) for n in (FIRST, rows - FIRST)],
-        in_specs=[pl.BlockSpec(memory_space=pltpu.VMEM)] * 3,
+        in_specs=[pl.BlockSpec(memory_space=pltpu.HBM)] + [pl.BlockSpec(memory_space=pltpu.VMEM)] * 2,
+        scratch_shapes=[pltpu.VMEM((rows, cols), F32), pltpu.SemaphoreType.DMA],
         compiler_params=pltpu.CompilerParams(vmem_limit_bytes=8 * MIB),
         name="late",
-    )(other, ham_far, den_far)
+    )(pltpu.with_memory_space_constraint(other, pltpu.HBM), ham_far, den_far)
 
 
 def kept_kernel(own_ref, ham_ref, den_ref, out_ref):

time: 105 us -> 104 us (level)
  local copies, waits for them, and re-layouts: 4.24 us -> 2.17 us
  Pallas kernels: 10.8 us -> 11.9 us
    unnamed x15 -> x11, local copies, waits for them, and re-layouts: 4.06 us -> 1.86 us
    pallas_call x1, Pallas kernels: 1.22 us -> 2.33 us  [late(): pl.pallas_call(late_kernel, out_shape=[jax.ShapeDtypeStruct((n, cols), F3...]
  transfers between devices with their start and end apart: 33 -> 33, of which waited for: 9 -> 9; matrix products, arithmetic and copies ran while one was open for 1% -> 2% of each run, Pallas kernels for 8% -> 9%
where the time goes in v4:
time: 104 us
  starting transfers between devices  66.6 us (64%)
  waiting for transfers between devices  20.9 us (20%)
  Pallas kernels  11.9 us (11%)
  local copies, waits for them, and re-layouts  2.17 us (2%)
    ppermute x10, starting transfers between devices, col_swap(): return lax.ppermute(value, 'col', [(c, c ^ bit) for c in range(4 * NY)])  30.8 us
    ppermute x8, starting transfers between devices, over_row(): return lax.ppermute(value, ('row', 'col'), pairs)  18.2 us
    ppermute x2, waiting for transfers between devices, rep_swap(): return lax.ppermute(value, 'rep', [(0, 1), (1, 0)])  8.55 us
    ppermute x6, starting transfers between devices, over_y(): return lax.ppermute(value, 'col', pairs)  7.07 us
    pallas_call x1, Pallas kernels, early(): pl.pallas_call(early_kernel, out_shape=[pltpu.HBM(*shapes[0])] + [jax.Sha...  6.23 us
    ppermute x3, waiting for transfers between devices, straight_y(): return lax.ppermute(value, 'col', pairs)  4.54 us
    ppermute x3, starting transfers between devices, over_x(): return lax.ppermute(value, ('col', 'rep'), pairs)  4.02 us
    ppermute x2, starting transfers between devices, rep_swap(): return lax.ppermute(value, 'rep', [(0, 1), (1, 0)])  3.07 us
  transfers between devices with their start and end apart: 33, of which 9 were waited for; matrix products, arithmetic and copies ran while one was open for 2% of the time, Pallas kernels for 9%

profile of v4, /device:TPU:1, one launch (start us, length us, event | category | flops | bytes accessed | tf_op | source)
XLA Modules:
  0.0 103.6 jit_solution(16418347529612957901)
XLA Ops:
  0.6 0.8 copy.8.pattern_ref
  1.4 1.0 %copy-done.1 = bf16[1024,256]{1,0:T(8,128)(2,1)S(1)} copy-done((bf16[1024,256]{1,0:T(8,128)(2,1)S(1)}, bf16[1024,256]{1,0:T(8,128)(2,1)}, u32[]{:S(2)}) %copy-start.1) | copy-done | bytes 524312
  2.5 0.4 mask_ham.1.refs_0_
  2.9 2.1 %collective-permute-start.4 = (bf16[1024,256]{1,0:T(8,128)(2,1)S(1)}, bf16[1024,256]{1,0:T(8,128)(2,1)S(1)}, u32[]{:S(2)}, u32[]{:S(2)}) collective-permute-start(bf16[1024,256]{1,0:T(8,128)(2,1)S(1)} %mask_ham.1.refs_0_), channel_id=1, source_target_pairs={{0,4},{2,6},{4,0},{6,2},{8,12},{10,14},{12,8},{14,10},{16,20},{18,... | collective-permute-start | bytes 1572872 | tf_op jit(solution)/shard_map/ppermute | solution.py:49
  5.0 1.3 %collective-permute-start.8 = (bf16[1024,256]{1,0:T(8,128)(2,1)S(1)}, bf16[1024,256]{1,0:T(8,128)(2,1)S(1)}, u32[]{:S(2)}, u32[]{:S(2)}) collective-permute-start(bf16[1024,256]{1,0:T(8,128)(2,1)S(1)} %mask_ham.1.refs_0_), channel_id=1, source_target_pairs={{0,24},{2,10},{4,28},{6,14},{8,0},{10,18},{12,4},{14,22},{16,8},{1... | collective-permute-start | bytes 1572872 | tf_op jit(solution)/shard_map/ppermute | solution.py:40
  6.3 0.5 mask_dens.1
  6.9 1.7 %collective-permute-start.12 = (bf16[512,512]{1,0:T(8,128)(2,1)S(1)}, bf16[512,512]{1,0:T(8,128)(2,1)S(1)}, u32[]{:S(2)}, u32[]{:S(2)}) collective-permute-start(bf16[512,512]{1,0:T(8,128)(2,1)S(1)} %get-tuple-element.36.refs_16_), channel_id=1, source_target_pairs={{0,224},{2,34},{4,228},{6,38},{8,232},{10,42},{12,236},{14,46},{16... | collective-permute-start | bytes 1572872 | tf_op jit(solution)/shard_map/ppermute | solution.py:33
  8.6 4.0 %collective-permute-start = (bf16[512,512]{1,0:T(8,128)(2,1)S(1)}, bf16[512,512]{1,0:T(8,128)(2,1)S(1)}, u32[]{:S(2)}, u32[]{:S(2)}) collective-permute-start(bf16[512,512]{1,0:T(8,128)(2,1)S(1)} %get-tuple-element.36.refs_16_), channel_id=1, source_target_pairs={{0,32},{2,226},{4,36},{6,230},{8,40},{10,234},{12,44},{14,238},{16... | collective-permute-start | bytes 1572872 | tf_op jit(solution)/shard_map/ppermute | solution.py:33
  12.5 1.4 %collective-permute-start.2 = (bf16[1024,256]{1,0:T(8,128)(2,1)S(1)}, bf16[1024,256]{1,0:T(8,128)(2,1)S(1)}, u32[]{:S(2)}, u32[]{:S(2)}) collective-permute-start(bf16[1024,256]{1,0:T(8,128)(2,1)S(1)} %mask_ham.1.refs_0_), channel_id=1, source_target_pairs={{0,8},{2,26},{4,12},{6,30},{8,16},{10,2},{12,20},{14,6},{16,24},{1... | collective-permute-start | bytes 1572872 | tf_op jit(solution)/shard_map/ppermute | solution.py:40
  14.0 1.4 %collective-permute-done.4.refs_8_ = bf16[1024,256]{1,0:T(8,128)(2,1)S(1)} collective-permute-done((bf16[1024,256]{1,0:T(8,128)(2,1)S(1)}, bf16[1024,256]{1,0:T(8,128)(2,1)S(1)}, u32[]{:S(2)}, u32[]{:S(2)}) %collective-permute-start.4) | collective-permute-done | bytes 524320 | tf_op jit(solution)/shard_map/ppermute | solution.py:49
  15.3 2.6 %collective-permute-start.10 = (bf16[1024,256]{1,0:T(8,128)(2,1)S(1)}, bf16[1024,256]{1,0:T(8,128)(2,1)S(1)}, u32[]{:S(2)}, u32[]{:S(2)}) collective-permute-start(bf16[1024,256]{1,0:T(8,128)(2,1)S(1)} %collective-permute-done.4.refs_8_), channel_id=1, source_target_pairs={{0,24},{2,10},{4,28},{6,14},{8,0},{10,18},{12,4},{14,22},{16,8},{1... | collective-permute-start | bytes 1572872 | tf_op jit(solution)/shard_map/ppermute | solution.py:40
  17.9 1.1 %collective-permute-done.12.refs_18_ = bf16[512,512]{1,0:T(8,128)(2,1)S(1)} collective-permute-done((bf16[512,512]{1,0:T(8,128)(2,1)S(1)}, bf16[512,512]{1,0:T(8,128)(2,1)S(1)}, u32[]{:S(2)}, u32[]{:S(2)}) %collective-permute-start.12) | collective-permute-done | bytes 524320 | tf_op jit(solution)/shard_map/ppermute | solution.py:33
  19.1 0.5 collective-permute-start.13
  19.5 1.8 %collective-permute-done.refs_17_ = bf16[512,512]{1,0:T(8,128)(2,1)S(1)} collective-permute-done((bf16[512,512]{1,0:T(8,128)(2,1)S(1)}, bf16[512,512]{1,0:T(8,128)(2,1)S(1)}, u32[]{:S(2)}, u32[]{:S(2)}) %collective-permute-start) | collective-permute-done | bytes 524320 | tf_op jit(solution)/shard_map/ppermute | solution.py:33
  21.3 3.2 %collective-permute-start.3 = (bf16[512,512]{1,0:T(8,128)(2,1)S(1)}, bf16[512,512]{1,0:T(8,128)(2,1)S(1)}, u32[]{:S(2)}, u32[]{:S(2)}) collective-permute-start(bf16[512,512]{1,0:T(8,128)(2,1)S(1)} %collective-permute-done.refs_17_), channel_id=1, source_target_pairs={{0,32},{2,226},{4,36},{6,230},{8,40},{10,234},{12,44},{14,238},{16... | collective-permute-start | bytes 1572872 | tf_op jit(solution)/shard_map/ppermute | solution.py:33
  24.5 5.7 %collective-permute-start.1 = (bf16[1024,256]{1,0:T(8,128)(2,1)S(1)}, bf16[1024,256]{1,0:T(8,128)(2,1)S(1)}, u32[]{:S(2)}, u32[]{:S(2)}) collective-permute-start(bf16[1024,256]{1,0:T(8,128)(2,1)S(1)} %mask_ham.1.refs_0_), channel_id=1, source_target_pairs={{0,2},{2,0},{4,6},{6,4},{8,10},{10,8},{12,14},{14,12},{16,18},{18,... | collective-permute-start | bytes 1572872 | tf_op jit(solution)/shard_map/ppermute | solution.py:49
  30.3 0.5 collective-permute-done.10.refs_12_
  30.8 1.0 collective-permute-start.11
  31.8 3.0 %collective-permute-start.17 = (bf16[512,512]{1,0:T(8,128)(2,1)S(1)}, bf16[512,512]{1,0:T(8,128)(2,1)S(1)}, u32[]{:S(2)}, u32[]{:S(2)}) collective-permute-start(bf16[512,512]{1,0:T(8,128)(2,1)S(1)} %collective-permute-done.3.refs_19_), channel_id=1, source_target_pairs={{0,32},{2,226},{4,36},{6,230},{8,40},{10,234},{12,44},{14,238},{16... | collective-permute-start | bytes 1572872 | tf_op jit(solution)/shard_map/ppermute | solution.py:33
  34.8 10.2 %collective-permute-start.5 = (bf16[1024,256]{1,0:T(8,128)(2,1)S(1)}, bf16[1024,256]{1,0:T(8,128)(2,1)S(1)}, u32[]{:S(2)}, u32[]{:S(2)}) collective-permute-start(bf16[1024,256]{1,0:T(8,128)(2,1)S(1)} %collective-permute-done.4.refs_8_), channel_id=1, source_target_pairs={{0,2},{2,0},{4,6},{6,4},{8,10},{10,8},{12,14},{14,12},{16,18},{18,... | collective-permute-start | bytes 1572872 | tf_op jit(solution)/shard_map/ppermute | solution.py:49
  45.0 2.3 %collective-permute-start.6 = (f32[8,512]{1,0:T(8,128)S(1)}, f32[8,512]{1,0:T(8,128)S(1)}, u32[]{:S(2)}, u32[]{:S(2)}) collective-permute-start(f32[8,512]{1,0:T(8,128)S(1)} %get-tuple-element.39), channel_id=1, source_target_pairs={{0,128},{2,130},{4,132},{6,134},{8,136},{10,138},{12,140},{14,142}... | collective-permute-start | bytes 49160 | tf_op jit(solution)/shard_map/ppermute | solution.py:33
  47.3 0.8 collective-permute-start.20
  48.1 3.8 %collective-permute-start.15 = (bf16[1024,256]{1,0:T(8,128)(2,1)S(1)}, bf16[1024,256]{1,0:T(8,128)(2,1)S(1)}, u32[]{:S(2)}, u32[]{:S(2)}) collective-permute-start(bf16[1024,256]{1,0:T(8,128)(2,1)S(1)} %collective-permute-done.11.refs_6_), channel_id=1, source_target_pairs={{0,2},{2,0},{4,6},{6,4},{8,10},{10,8},{12,14},{14,12},{16,18},{18,... | collective-permute-start | bytes 1572872 | tf_op jit(solution)/shard_map/ppermute | solution.py:49
  51.9 4.2 %collective-permute-start.18 = (bf16[1024,256]{1,0:T(8,128)(2,1)S(1)}, bf16[1024,256]{1,0:T(8,128)(2,1)S(1)}, u32[]{:S(2)}, u32[]{:S(2)}) collective-permute-start(bf16[1024,256]{1,0:T(8,128)(2,1)S(1)} %collective-permute-done.16.refs_10_), channel_id=1, source_target_pairs={{0,2},{2,0},{4,6},{6,4},{8,10},{10,8},{12,14},{14,12},{16,18},{18,... | collective-permute-start | bytes 1572872 | tf_op jit(solution)/shard_map/ppermute | solution.py:49
  56.1 2.1 %collective-permute-start.21 = (bf16[1024,256]{1,0:T(8,128)(2,1)S(1)}, bf16[1024,256]{1,0:T(8,128)(2,1)S(1)}, u32[]{:S(2)}, u32[]{:S(2)}) collective-permute-start(bf16[1024,256]{1,0:T(8,128)(2,1)S(1)} %collective-permute-done.20.refs_14_), channel_id=1, source_target_pairs={{0,2},{2,0},{4,6},{6,4},{8,10},{10,8},{12,14},{14,12},{16,18},{18,... | collective-permute-start | bytes 1572872 | tf_op jit(solution)/shard_map/ppermute | solution.py:49
  58.3 0.4 collective-permute-start.9
  58.7 3.4 %collective-permute-start.22 = (bf16[512,512]{1,0:T(8,128)(2,1)S(1)}, bf16[512,512]{1,0:T(8,128)(2,1)S(1)}, u32[]{:S(2)}, u32[]{:S(2)}) collective-permute-start(bf16[512,512]{1,0:T(8,128)(2,1)S(1)} %collective-permute-done.17.refs_21_), channel_id=1, source_target_pairs={{0,32},{2,226},{4,36},{6,230},{8,40},{10,234},{12,44},{14,238},{16... | collective-permute-start | bytes 1572872 | tf_op jit(solution)/shard_map/ppermute | solution.py:33
  62.2 6.2 %early.1 = (f32[512,512]{1,0:T(8,128)}, f32[512,512]{1,0:T(8,128)S(1)}, bf16[2,1024,256]{2,1,0:T(8,128)(2,1)S(1)}, f32[8,1024]{1,0:T(8,128)S(1)}) custom-call(bf16[1024,256]{1,0:T(8,128)(2,1)S(1)} %mask_ham.1.refs_0_, bf16[1024,256]{1,0:T(8,128)(2,1)S(1)} %collective-permute-done.1.refs_1_, bf16[1024,256]{1,0:T(8,128)(2,1)S(1)} %collective-permute-done.2.refs_2_, ...), custom_call_target="tpu_custom_call" | custom-call | flops 4294967296 | bytes 4194304 | tf_op jit(solution)/shard_map/early/pallas_call | solution.py:183
  68.4 0.2 scatter.4
  68.7 0.3 collective-permute-start.24
  69.0 2.4 %collective-permute-start.25 = (f32[8,1024]{1,0:T(8,128)S(1)}, f32[8,1024]{1,0:T(8,128)S(1)}, u32[]{:S(2)}, u32[]{:S(2)}) collective-permute-start(f32[8,1024]{1,0:T(8,128)S(1)} %scatter.4), channel_id=1, source_target_pairs={{0,5},{1,4},{2,7},{3,6},{4,0},{5,1},{6,2},{7,3},{8,13},{9,12},{10,... | collective-permute-start | bytes 98312 | tf_op jit(solution)/shard_map/ppermute | solution.py:62
  71.4 1.3 %collective-permute-start.26 = (f32[8,1024]{1,0:T(8,128)S(1)}, f32[8,1024]{1,0:T(8,128)S(1)}, u32[]{:S(2)}, u32[]{:S(2)}) collective-permute-start(f32[8,1024]{1,0:T(8,128)S(1)} %scatter.4), channel_id=1, source_target_pairs={{0,1},{1,0},{2,3},{3,2},{4,5},{5,4},{6,7},{7,6},{8,9},{9,8},{10,11... | collective-permute-start | bytes 98312 | tf_op jit(solution)/shard_map/ppermute | solution.py:62
  72.7 2.3 %late.1 = (f32[256,512]{1,0:T(8,128)S(1)}, f32[256,512]{1,0:T(8,128)}) custom-call(f32[512,512]{1,0:T(8,128)} %get-tuple-element.50.other_ref, bf16[2,1024,256]{2,1,0:T(8,128)(2,1)S(1)} %get-tuple-element.51.ham_ref, bf16[512,512]{1,0:T(8,128)(2,1)S(1)} %collective-permute-done.22.den_ref), custom_call_target="tpu_custom_call" | custom-call | tf_op jit(solution)/shard_map/late/pallas_call | solution.py:222
  75.0 1.8 %collective-permute-start.23 = (f32[256,512]{1,0:T(8,128)S(1)}, f32[256,512]{1,0:T(8,128)S(1)}, u32[]{:S(2)}, u32[]{:S(2)}) collective-permute-start(f32[256,512]{1,0:T(8,128)S(1)} %get-tuple-element.52), channel_id=1, source_target_pairs={{0,1},{1,0},{2,3},{3,2},{4,5},{5,4},{6,7},{7,6},{8,9},{9,8},{10,11... | collective-permute-start | bytes 1572872 | tf_op jit(solution)/shard_map/ppermute | solution.py:53
  76.9 2.7 %collective-permute-start.29 = (f32[8,1024]{1,0:T(8,128)S(1)}, f32[8,1024]{1,0:T(8,128)S(1)}, u32[]{:S(2)}, u32[]{:S(2)}) collective-permute-start(f32[8,1024]{1,0:T(8,128)S(1)} %add_add_fusion.1), channel_id=1, source_target_pairs={{0,24},{2,26},{4,28},{6,30},{8,0},{10,2},{12,4},{14,6},{16,8},{18,... | collective-permute-start | bytes 98312 | tf_op jit(solution)/shard_map/ppermute | solution.py:45
  79.6 1.6 %collective-permute-done.28 = f32[8,1024]{1,0:T(8,128)S(1)} collective-permute-done((f32[8,1024]{1,0:T(8,128)S(1)}, f32[8,1024]{1,0:T(8,128)S(1)}, u32[]{:S(2)}, u32[]{:S(2)}) %collective-permute-start.28) | collective-permute-done | bytes 32800 | tf_op jit(solution)/shard_map/ppermute | solution.py:45
  81.2 3.0 %collective-permute-done.30 = f32[8,1024]{1,0:T(8,128)S(1)} collective-permute-done((f32[8,1024]{1,0:T(8,128)S(1)}, f32[8,1024]{1,0:T(8,128)S(1)}, u32[]{:S(2)}, u32[]{:S(2)}) %collective-permute-start.30) | collective-permute-done | bytes 32800 | tf_op jit(solution)/shard_map/ppermute | solution.py:45
  84.2 2.1 %collective-permute-start.31 = (f32[8,1024]{1,0:T(8,128)S(1)}, f32[8,1024]{1,0:T(8,128)S(1)}, u32[]{:S(2)}, u32[]{:S(2)}) collective-permute-start(f32[8,1024]{1,0:T(8,128)S(1)} %add_add_fusion), channel_id=1, source_target_pairs={{0,2},{2,0},{4,6},{6,4},{8,10},{10,8},{12,14},{14,12},{16,18},{18,... | collective-permute-start | bytes 98312 | tf_op jit(solution)/shard_map/ppermute | solution.py:49
  86.4 1.3 %collective-permute-start.27 = (f32[256,512]{1,0:T(8,128)}, f32[256,512]{1,0:T(8,128)}, u32[]{:S(2)}, u32[]{:S(2)}) collective-permute-start(f32[256,512]{1,0:T(8,128)} %get-tuple-element.56), channel_id=1, source_target_pairs={{0,1},{1,0},{2,3},{3,2},{4,5},{5,4},{6,7},{7,6},{8,9},{9,8},{10,11... | collective-permute-start | bytes 1572872 | tf_op jit(solution)/shard_map/ppermute | solution.py:53
  87.7 2.1 %collective-permute-done.23.first_ref = f32[256,512]{1,0:T(8,128)S(1)} collective-permute-done((f32[256,512]{1,0:T(8,128)S(1)}, f32[256,512]{1,0:T(8,128)S(1)}, u32[]{:S(2)}, u32[]{:S(2)}) %collective-permute-start.23) | collective-permute-done | bytes 524320 | tf_op jit(solution)/shard_map/ppermute | solution.py:53
  89.8 0.2 fusion
  90.1 0.3 convolution_bitcast_fusion
  90.4 0.8 collective-permute-start.32
  91.2 0.4 kept.1.kept_ref
  91.6 3.0 %collective-permute-done.32 = f32[16,128]{1,0:T(8,128)S(1)} collective-permute-done((f32[16,128]{1,0:T(8,128)S(1)}, f32[16,128]{1,0:T(8,128)S(1)}, u32[]{:S(2)}, u32[]{:S(2)}) %collective-permute-start.32) | collective-permute-done | bytes 8224 | tf_op jit(solution)/shard_map/ppermute | solution.py:335
  94.6 0.6 pad_maximum_fusion
  95.3 6.5 %collective-permute-done.27.second_ref = f32[256,512]{1,0:T(8,128)} collective-permute-done((f32[256,512]{1,0:T(8,128)}, f32[256,512]{1,0:T(8,128)}, u32[]{:S(2)}, u32[]{:S(2)}) %collective-permute-start.27) | collective-permute-done | bytes 524320 | tf_op jit(solution)/shard_map/ppermute | solution.py:53
  101.7 1.9 %finish.1 = bf16[512,512]{1,0:T(8,128)(2,1)} custom-call(f32[512,512]{1,0:T(8,128)S(1)} %kept.1.kept_ref, f32[256,512]{1,0:T(8,128)S(1)} %collective-permute-done.23.first_ref, f32[256,512]{1,0:T(8,128)} %collective-permute-done.27.second_ref), custom_call_target="tpu_custom_call" | custom-call | tf_op jit(solution)/shard_map/finish/pallas_call | solution.py:254
  (52 shorter events, 0.6 us)
Async XLA Ops:
  0.6 89.2 %copy-start = (bf16[64,16,128]{2,1,0:T(8,128)(2,1)S(1)}, bf16[64,16,128]{2,1,0:T(8,128)(2,1)}, u32[]{:S(2)}) copy-start(bf16[64,16,128]{2,1,0:T(8,128)(2,1)} %param.12) | copy-start | bytes 786436
  1.4 1.0 %copy-start.1 = (bf16[1024,256]{1,0:T(8,128)(2,1)S(1)}, bf16[1024,256]{1,0:T(8,128)(2,1)}, u32[]{:S(2)}) copy-start(bf16[1024,256]{1,0:T(8,128)(2,1)} %matrix_ref.2) | copy-start | bytes 1572868
  2.5 3.8 %copy-start.2 = (bf16[512,512]{1,0:T(8,128)(2,1)S(1)}, bf16[512,512]{1,0:T(8,128)(2,1)}, u32[]{:S(2)}) copy-start(bf16[512,512]{1,0:T(8,128)(2,1)} %matrix_ref.3) | copy-start | bytes 1572868
  2.5 3.8 %copy-start.3 = (s32[8,8]{1,0:T(8,128)S(1)}, s32[8,8]{1,0:T(8,128)}, u32[]{:S(2)}) copy-start(s32[8,8]{1,0:T(8,128)} %pattern_ref.2) | copy-start | bytes 772
  2.9 12.4 %collective-permute-start.4 = (bf16[1024,256]{1,0:T(8,128)(2,1)S(1)}, bf16[1024,256]{1,0:T(8,128)(2,1)S(1)}, u32[]{:S(2)}, u32[]{:S(2)}) collective-permute-start(bf16[1024,256]{1,0:T(8,128)(2,1)S(1)} %mask_ham.1.refs_0_), channel_id=1, source_target_pairs={{0,4},{2,6},{4,0},{6,2},{8,12},{10,14},{12,8},{14,10},{16,20},{18,... | collective-permute-start | bytes 1572872 | tf_op jit(solution)/shard_map/ppermute | solution.py:49
  5.0 10.3 %collective-permute-start.8 = (bf16[1024,256]{1,0:T(8,128)(2,1)S(1)}, bf16[1024,256]{1,0:T(8,128)(2,1)S(1)}, u32[]{:S(2)}, u32[]{:S(2)}) collective-permute-start(bf16[1024,256]{1,0:T(8,128)(2,1)S(1)} %mask_ham.1.refs_0_), channel_id=1, source_target_pairs={{0,24},{2,10},{4,28},{6,14},{8,0},{10,18},{12,4},{14,22},{16,8},{1... | collective-permute-start | bytes 1572872 | tf_op jit(solution)/shard_map/ppermute | solution.py:40
  6.9 55.3 %copy-start.4 = (s32[8]{0:T(128)S(1)}, s32[8]{0:T(128)}, u32[]{:S(2)}) copy-start(s32[8]{0:T(128)} %param.13) | copy-start | bytes 100
  6.9 12.2 %collective-permute-start.12 = (bf16[512,512]{1,0:T(8,128)(2,1)S(1)}, bf16[512,512]{1,0:T(8,128)(2,1)S(1)}, u32[]{:S(2)}, u32[]{:S(2)}) collective-permute-start(bf16[512,512]{1,0:T(8,128)(2,1)S(1)} %get-tuple-element.36.refs_16_), channel_id=1, source_target_pairs={{0,224},{2,34},{4,228},{6,38},{8,232},{10,42},{12,236},{14,46},{16... | collective-permute-start | bytes 1572872 | tf_op jit(solution)/shard_map/ppermute | solution.py:33
  8.6 12.8 %collective-permute-start = (bf16[512,512]{1,0:T(8,128)(2,1)S(1)}, bf16[512,512]{1,0:T(8,128)(2,1)S(1)}, u32[]{:S(2)}, u32[]{:S(2)}) collective-permute-start(bf16[512,512]{1,0:T(8,128)(2,1)S(1)} %get-tuple-element.36.refs_16_), channel_id=1, source_target_pairs={{0,32},{2,226},{4,36},{6,230},{8,40},{10,234},{12,44},{14,238},{16... | collective-permute-start | bytes 1572872 | tf_op jit(solution)/shard_map/ppermute | solution.py:33
  12.5 17.7 %collective-permute-start.2 = (bf16[1024,256]{1,0:T(8,128)(2,1)S(1)}, bf16[1024,256]{1,0:T(8,128)(2,1)S(1)}, u32[]{:S(2)}, u32[]{:S(2)}) collective-permute-start(bf16[1024,256]{1,0:T(8,128)(2,1)S(1)} %mask_ham.1.refs_0_), channel_id=1, source_target_pairs={{0,8},{2,26},{4,12},{6,30},{8,16},{10,2},{12,20},{14,6},{16,24},{1... | collective-permute-start | bytes 1572872 | tf_op jit(solution)/shard_map/ppermute | solution.py:40
  15.3 15.4 %collective-permute-start.10 = (bf16[1024,256]{1,0:T(8,128)(2,1)S(1)}, bf16[1024,256]{1,0:T(8,128)(2,1)S(1)}, u32[]{:S(2)}, u32[]{:S(2)}) collective-permute-start(bf16[1024,256]{1,0:T(8,128)(2,1)S(1)} %collective-permute-done.4.refs_8_), channel_id=1, source_target_pairs={{0,24},{2,10},{4,28},{6,14},{8,0},{10,18},{12,4},{14,22},{16,8},{1... | collective-permute-start | bytes 1572872 | tf_op jit(solution)/shard_map/ppermute | solution.py:40
  19.1 12.7 %collective-permute-start.13 = (bf16[512,512]{1,0:T(8,128)(2,1)S(1)}, bf16[512,512]{1,0:T(8,128)(2,1)S(1)}, u32[]{:S(2)}, u32[]{:S(2)}) collective-permute-start(bf16[512,512]{1,0:T(8,128)(2,1)S(1)} %collective-permute-done.12.refs_18_), channel_id=1, source_target_pairs={{0,224},{2,34},{4,228},{6,38},{8,232},{10,42},{12,236},{14,46},{16... | collective-permute-start | bytes 1572872 | tf_op jit(solution)/shard_map/ppermute | solution.py:33
  21.3 10.5 %collective-permute-start.3 = (bf16[512,512]{1,0:T(8,128)(2,1)S(1)}, bf16[512,512]{1,0:T(8,128)(2,1)S(1)}, u32[]{:S(2)}, u32[]{:S(2)}) collective-permute-start(bf16[512,512]{1,0:T(8,128)(2,1)S(1)} %collective-permute-done.refs_17_), channel_id=1, source_target_pairs={{0,32},{2,226},{4,36},{6,230},{8,40},{10,234},{12,44},{14,238},{16... | collective-permute-start | bytes 1572872 | tf_op jit(solution)/shard_map/ppermute | solution.py:33
  24.5 10.3 %collective-permute-start.1 = (bf16[1024,256]{1,0:T(8,128)(2,1)S(1)}, bf16[1024,256]{1,0:T(8,128)(2,1)S(1)}, u32[]{:S(2)}, u32[]{:S(2)}) collective-permute-start(bf16[1024,256]{1,0:T(8,128)(2,1)S(1)} %mask_ham.1.refs_0_), channel_id=1, source_target_pairs={{0,2},{2,0},{4,6},{6,4},{8,10},{10,8},{12,14},{14,12},{16,18},{18,... | collective-permute-start | bytes 1572872 | tf_op jit(solution)/shard_map/ppermute | solution.py:49
  30.3 14.7 %collective-permute-start.16 = (bf16[1024,256]{1,0:T(8,128)(2,1)S(1)}, bf16[1024,256]{1,0:T(8,128)(2,1)S(1)}, u32[]{:S(2)}, u32[]{:S(2)}) collective-permute-start(bf16[1024,256]{1,0:T(8,128)(2,1)S(1)} %collective-permute-done.4.refs_8_), channel_id=1, source_target_pairs={{0,8},{2,26},{4,12},{6,30},{8,16},{10,2},{12,20},{14,6},{16,24},{1... | collective-permute-start | bytes 1572872 | tf_op jit(solution)/shard_map/ppermute | solution.py:40
  30.8 16.5 %collective-permute-start.11 = (bf16[1024,256]{1,0:T(8,128)(2,1)S(1)}, bf16[1024,256]{1,0:T(8,128)(2,1)S(1)}, u32[]{:S(2)}, u32[]{:S(2)}) collective-permute-start(bf16[1024,256]{1,0:T(8,128)(2,1)S(1)} %collective-permute-done.8.refs_4_), channel_id=1, source_target_pairs={{0,24},{2,10},{4,28},{6,14},{8,0},{10,18},{12,4},{14,22},{16,8},{1... | collective-permute-start | bytes 1572872 | tf_op jit(solution)/shard_map/ppermute | solution.py:40
  31.8 16.3 %collective-permute-start.14 = (bf16[512,512]{1,0:T(8,128)(2,1)S(1)}, bf16[512,512]{1,0:T(8,128)(2,1)S(1)}, u32[]{:S(2)}, u32[]{:S(2)}) collective-permute-start(bf16[512,512]{1,0:T(8,128)(2,1)S(1)} %collective-permute-done.13.refs_20_), channel_id=1, source_target_pairs={{0,224},{2,34},{4,228},{6,38},{8,232},{10,42},{12,236},{14,46},{16... | collective-permute-start | bytes 1572872 | tf_op jit(solution)/shard_map/ppermute | solution.py:33
  31.8 20.1 %collective-permute-start.17 = (bf16[512,512]{1,0:T(8,128)(2,1)S(1)}, bf16[512,512]{1,0:T(8,128)(2,1)S(1)}, u32[]{:S(2)}, u32[]{:S(2)}) collective-permute-start(bf16[512,512]{1,0:T(8,128)(2,1)S(1)} %collective-permute-done.3.refs_19_), channel_id=1, source_target_pairs={{0,32},{2,226},{4,36},{6,230},{8,40},{10,234},{12,44},{14,238},{16... | collective-permute-start | bytes 1572872 | tf_op jit(solution)/shard_map/ppermute | solution.py:33
  34.8 21.2 %collective-permute-start.5 = (bf16[1024,256]{1,0:T(8,128)(2,1)S(1)}, bf16[1024,256]{1,0:T(8,128)(2,1)S(1)}, u32[]{:S(2)}, u32[]{:S(2)}) collective-permute-start(bf16[1024,256]{1,0:T(8,128)(2,1)S(1)} %collective-permute-done.4.refs_8_), channel_id=1, source_target_pairs={{0,2},{2,0},{4,6},{6,4},{8,10},{10,8},{12,14},{14,12},{16,18},{18,... | collective-permute-start | bytes 1572872 | tf_op jit(solution)/shard_map/ppermute | solution.py:49
  45.0 11.1 %collective-permute-start.6 = (f32[8,512]{1,0:T(8,128)S(1)}, f32[8,512]{1,0:T(8,128)S(1)}, u32[]{:S(2)}, u32[]{:S(2)}) collective-permute-start(f32[8,512]{1,0:T(8,128)S(1)} %get-tuple-element.39), channel_id=1, source_target_pairs={{0,128},{2,130},{4,132},{6,134},{8,136},{10,138},{12,140},{14,142}... | collective-permute-start | bytes 49160 | tf_op jit(solution)/shard_map/ppermute | solution.py:33
  47.3 8.8 %collective-permute-start.20 = (bf16[1024,256]{1,0:T(8,128)(2,1)S(1)}, bf16[1024,256]{1,0:T(8,128)(2,1)S(1)}, u32[]{:S(2)}, u32[]{:S(2)}) collective-permute-start(bf16[1024,256]{1,0:T(8,128)(2,1)S(1)} %collective-permute-done.16.refs_10_), channel_id=1, source_target_pairs={{0,8},{2,26},{4,12},{6,30},{8,16},{10,2},{12,20},{14,6},{16,24},{1... | collective-permute-start | bytes 1572872 | tf_op jit(solution)/shard_map/ppermute | solution.py:40
  48.1 8.1 %collective-permute-start.15 = (bf16[1024,256]{1,0:T(8,128)(2,1)S(1)}, bf16[1024,256]{1,0:T(8,128)(2,1)S(1)}, u32[]{:S(2)}, u32[]{:S(2)}) collective-permute-start(bf16[1024,256]{1,0:T(8,128)(2,1)S(1)} %collective-permute-done.11.refs_6_), channel_id=1, source_target_pairs={{0,2},{2,0},{4,6},{6,4},{8,10},{10,8},{12,14},{14,12},{16,18},{18,... | collective-permute-start | bytes 1572872 | tf_op jit(solution)/shard_map/ppermute | solution.py:49
  51.9 6.3 %collective-permute-start.18 = (bf16[1024,256]{1,0:T(8,128)(2,1)S(1)}, bf16[1024,256]{1,0:T(8,128)(2,1)S(1)}, u32[]{:S(2)}, u32[]{:S(2)}) collective-permute-start(bf16[1024,256]{1,0:T(8,128)(2,1)S(1)} %collective-permute-done.16.refs_10_), channel_id=1, source_target_pairs={{0,2},{2,0},{4,6},{6,4},{8,10},{10,8},{12,14},{14,12},{16,18},{18,... | collective-permute-start | bytes 1572872 | tf_op jit(solution)/shard_map/ppermute | solution.py:49
  56.0 2.3 %collective-permute-start.7 = (bf16[1024,256]{1,0:T(8,128)(2,1)S(1)}, bf16[1024,256]{1,0:T(8,128)(2,1)S(1)}, u32[]{:S(2)}, u32[]{:S(2)}) collective-permute-start(bf16[1024,256]{1,0:T(8,128)(2,1)S(1)} %collective-permute-done.2.refs_2_), channel_id=1, source_target_pairs={{0,2},{2,0},{4,6},{6,4},{8,10},{10,8},{12,14},{14,12},{16,18},{18,... | collective-permute-start | bytes 1572872 | tf_op jit(solution)/shard_map/ppermute | solution.py:49
  56.1 6.0 %collective-permute-start.21 = (bf16[1024,256]{1,0:T(8,128)(2,1)S(1)}, bf16[1024,256]{1,0:T(8,128)(2,1)S(1)}, u32[]{:S(2)}, u32[]{:S(2)}) collective-permute-start(bf16[1024,256]{1,0:T(8,128)(2,1)S(1)} %collective-permute-done.20.refs_14_), channel_id=1, source_target_pairs={{0,2},{2,0},{4,6},{6,4},{8,10},{10,8},{12,14},{14,12},{16,18},{18,... | collective-permute-start | bytes 1572872 | tf_op jit(solution)/shard_map/ppermute | solution.py:49
  58.2 3.9 %collective-permute-start.19 = (bf16[1024,256]{1,0:T(8,128)(2,1)S(1)}, bf16[1024,256]{1,0:T(8,128)(2,1)S(1)}, u32[]{:S(2)}, u32[]{:S(2)}) collective-permute-start(bf16[1024,256]{1,0:T(8,128)(2,1)S(1)} %collective-permute-done.10.refs_12_), channel_id=1, source_target_pairs={{0,2},{2,0},{4,6},{6,4},{8,10},{10,8},{12,14},{14,12},{16,18},{18,... | collective-permute-start | bytes 1572872 | tf_op jit(solution)/shard_map/ppermute | solution.py:49
  58.3 3.8 %collective-permute-start.9 = (bf16[1024,256]{1,0:T(8,128)(2,1)S(1)}, bf16[1024,256]{1,0:T(8,128)(2,1)S(1)}, u32[]{:S(2)}, u32[]{:S(2)}) collective-permute-start(bf16[1024,256]{1,0:T(8,128)(2,1)S(1)} %collective-permute-done.8.refs_4_), channel_id=1, source_target_pairs={{0,2},{2,0},{4,6},{6,4},{8,10},{10,8},{12,14},{14,12},{16,18},{18,... | collective-permute-start | bytes 1572872 | tf_op jit(solution)/shard_map/ppermute | solution.py:49
  58.7 13.9 %collective-permute-start.22 = (bf16[512,512]{1,0:T(8,128)(2,1)S(1)}, bf16[512,512]{1,0:T(8,128)(2,1)S(1)}, u32[]{:S(2)}, u32[]{:S(2)}) collective-permute-start(bf16[512,512]{1,0:T(8,128)(2,1)S(1)} %collective-permute-done.17.refs_21_), channel_id=1, source_target_pairs={{0,32},{2,226},{4,36},{6,230},{8,40},{10,234},{12,44},{14,238},{16... | collective-permute-start | bytes 1572872 | tf_op jit(solution)/shard_map/ppermute | solution.py:33
  68.7 8.2 %collective-permute-start.24 = (f32[8,1024]{1,0:T(8,128)S(1)}, f32[8,1024]{1,0:T(8,128)S(1)}, u32[]{:S(2)}, u32[]{:S(2)}) collective-permute-start(f32[8,1024]{1,0:T(8,128)S(1)} %scatter.4), channel_id=1, source_target_pairs={{0,4},{1,5},{2,6},{3,7},{4,1},{5,0},{6,3},{7,2},{8,12},{9,13},{10,... | collective-permute-start | bytes 98312 | tf_op jit(solution)/shard_map/ppermute | solution.py:62
  69.0 7.8 %collective-permute-start.25 = (f32[8,1024]{1,0:T(8,128)S(1)}, f32[8,1024]{1,0:T(8,128)S(1)}, u32[]{:S(2)}, u32[]{:S(2)}) collective-permute-start(f32[8,1024]{1,0:T(8,128)S(1)} %scatter.4), channel_id=1, source_target_pairs={{0,5},{1,4},{2,7},{3,6},{4,0},{5,1},{6,2},{7,3},{8,13},{9,12},{10,... | collective-permute-start | bytes 98312 | tf_op jit(solution)/shard_map/ppermute | solution.py:62
  71.4 5.4 %collective-permute-start.26 = (f32[8,1024]{1,0:T(8,128)S(1)}, f32[8,1024]{1,0:T(8,128)S(1)}, u32[]{:S(2)}, u32[]{:S(2)}) collective-permute-start(f32[8,1024]{1,0:T(8,128)S(1)} %scatter.4), channel_id=1, source_target_pairs={{0,1},{1,0},{2,3},{3,2},{4,5},{5,4},{6,7},{7,6},{8,9},{9,8},{10,11... | collective-permute-start | bytes 98312 | tf_op jit(solution)/shard_map/ppermute | solution.py:62
  75.0 14.7 %collective-permute-start.23 = (f32[256,512]{1,0:T(8,128)S(1)}, f32[256,512]{1,0:T(8,128)S(1)}, u32[]{:S(2)}, u32[]{:S(2)}) collective-permute-start(f32[256,512]{1,0:T(8,128)S(1)} %get-tuple-element.52), channel_id=1, source_target_pairs={{0,1},{1,0},{2,3},{3,2},{4,5},{5,4},{6,7},{7,6},{8,9},{9,8},{10,11... | collective-permute-start | bytes 1572872 | tf_op jit(solution)/shard_map/ppermute | solution.py:53
  76.9 4.3 %collective-permute-start.28 = (f32[8,1024]{1,0:T(8,128)S(1)}, f32[8,1024]{1,0:T(8,128)S(1)}, u32[]{:S(2)}, u32[]{:S(2)}) collective-permute-start(f32[8,1024]{1,0:T(8,128)S(1)} %add_add_fusion.1), channel_id=1, source_target_pairs={{0,8},{2,10},{4,12},{6,14},{8,16},{10,18},{12,20},{14,22},{16,24},... | collective-permute-start | bytes 98312 | tf_op jit(solution)/shard_map/ppermute | solution.py:45
  76.9 4.3 %collective-permute-start.29 = (f32[8,1024]{1,0:T(8,128)S(1)}, f32[8,1024]{1,0:T(8,128)S(1)}, u32[]{:S(2)}, u32[]{:S(2)}) collective-permute-start(f32[8,1024]{1,0:T(8,128)S(1)} %add_add_fusion.1), channel_id=1, source_target_pairs={{0,24},{2,26},{4,28},{6,30},{8,0},{10,2},{12,4},{14,6},{16,8},{18,... | collective-permute-start | bytes 98312 | tf_op jit(solution)/shard_map/ppermute | solution.py:45
  79.6 4.6 %collective-permute-start.30 = (f32[8,1024]{1,0:T(8,128)S(1)}, f32[8,1024]{1,0:T(8,128)S(1)}, u32[]{:S(2)}, u32[]{:S(2)}) collective-permute-start(f32[8,1024]{1,0:T(8,128)S(1)} %add_add_fusion.1), channel_id=1, source_target_pairs={{0,16},{2,18},{4,20},{6,22},{8,24},{10,26},{12,28},{14,30},{16,0},... | collective-permute-start | bytes 98312 | tf_op jit(solution)/shard_map/ppermute | solution.py:45
  84.2 3.5 %collective-permute-start.31 = (f32[8,1024]{1,0:T(8,128)S(1)}, f32[8,1024]{1,0:T(8,128)S(1)}, u32[]{:S(2)}, u32[]{:S(2)}) collective-permute-start(f32[8,1024]{1,0:T(8,128)S(1)} %add_add_fusion), channel_id=1, source_target_pairs={{0,2},{2,0},{4,6},{6,4},{8,10},{10,8},{12,14},{14,12},{16,18},{18,... | collective-permute-start | bytes 98312 | tf_op jit(solution)/shard_map/ppermute | solution.py:49
  86.4 15.3 %collective-permute-start.27 = (f32[256,512]{1,0:T(8,128)}, f32[256,512]{1,0:T(8,128)}, u32[]{:S(2)}, u32[]{:S(2)}) collective-permute-start(f32[256,512]{1,0:T(8,128)} %get-tuple-element.56), channel_id=1, source_target_pairs={{0,1},{1,0},{2,3},{3,2},{4,5},{5,4},{6,7},{7,6},{8,9},{9,8},{10,11... | collective-permute-start | bytes 1572872 | tf_op jit(solution)/shard_map/ppermute | solution.py:53
  90.4 4.2 %collective-permute-start.32 = (f32[16,128]{1,0:T(8,128)S(1)}, f32[16,128]{1,0:T(8,128)S(1)}, u32[]{:S(2)}, u32[]{:S(2)}) collective-permute-start(f32[16,128]{1,0:T(8,128)S(1)} %slice_bitcast_fusion.2), channel_id=1, source_target_pairs={{0,32},{32,64},{64,96},{96,128},{128,160},{160,192},{192,224},{224... | collective-permute-start | bytes 24584 | tf_op jit(solution)/shard_map/ppermute | solution.py:335

commit v5 on v4

--- a/solution.py
+++ b/solution.py
@@ -17,7 +17,7 @@
 NY = 4
 F32 = jnp.float32
 BF16 = jnp.bfloat16
-FIRST = 256
+FIRST = 288
 
 
 def way(core):

time: 104 us -> 104 us (level)
    ppermute x1, waiting for transfers between devices: 2.99 us -> 0.01 us  [shards(): lax.ppermute(extended[1, SX:], 'row', [(i, (i + 1) % NZ) for i in range(N...]
    ppermute x2, waiting for transfers between devices: 8.55 us -> 11.2 us  [rep_swap(): return lax.ppermute(value, 'rep', [(0, 1), (1, 0)])]
  transfers between devices with their start and end apart: 33 -> 33, of which waited for: 9 -> 8; matrix products, arithmetic and copies ran while one was open for 2% -> 2% of each run, Pallas kernels for 9% -> 11%
where the time goes in v5:
time: 104 us
  starting transfers between devices  66.6 us (64%)
  waiting for transfers between devices  20.6 us (20%)
  Pallas kernels  11.8 us (11%)
  local copies, waits for them, and re-layouts  2.18 us (2%)
  other arithmetic  1.53 us (1%)
    ppermute x10, starting transfers between devices, col_swap(): return lax.ppermute(value, 'col', [(c, c ^ bit) for c in range(4 * NY)])  30.8 us
    ppermute x8, starting transfers between devices, over_row(): return lax.ppermute(value, ('row', 'col'), pairs)  18.2 us
    ppermute x2, waiting for transfers between devices, rep_swap(): return lax.ppermute(value, 'rep', [(0, 1), (1, 0)])  11.2 us
    ppermute x6, starting transfers between devices, over_y(): return lax.ppermute(value, 'col', pairs)  7.07 us
    pallas_call x1, Pallas kernels, early(): pl.pallas_call(early_kernel, out_shape=[pltpu.HBM(*shapes[0])] + [jax.Sha...  6.23 us
    ppermute x3, waiting for transfers between devices, straight_y(): return lax.ppermute(value, 'col', pairs)  4.54 us
    ppermute x3, starting transfers between devices, over_x(): return lax.ppermute(value, ('col', 'rep'), pairs)  4.02 us
    ppermute x2, starting transfers between devices, rep_swap(): return lax.ppermute(value, 'rep', [(0, 1), (1, 0)])  3.07 us
  transfers between devices with their start and end apart: 33, of which 8 were waited for; matrix products, arithmetic and copies ran while one was open for 2% of the time, Pallas kernels for 11%

profile of v5, /device:TPU:1, one launch (start us, length us, event | category | flops | bytes accessed | tf_op | source)
XLA Modules:
  0.0 104.1 jit_solution(5740616725533947954)
XLA Ops:
  0.6 0.8 copy.8.pattern_ref
  1.4 1.0 copy-done.1
  2.5 0.4 mask_ham.1.refs_0_
  2.9 2.1 %collective-permute-start.4 = (bf16[1024,256]{1,0:T(8,128)(2,1)S(1)}, bf16[1024,256]{1,0:T(8,128)(2,1)S(1)}, u32[]{:S(2)}, u32[]{:S(2)}) collective-permute-start(bf16[1024,256]{1,0:T(8,128)(2,1)S(1)} %mask_ham.1.refs_0_), channel_id=1, source_target_pairs={{0,4},{2,6},{4,0},{6,2},{8,12},{10,14},{12,8},{14,10},{16,20},{18,... | collective-permute-start | bytes 1572872 | tf_op jit(solution)/shard_map/ppermute | solution.py:49
  5.0 1.3 %collective-permute-start.8 = (bf16[1024,256]{1,0:T(8,128)(2,1)S(1)}, bf16[1024,256]{1,0:T(8,128)(2,1)S(1)}, u32[]{:S(2)}, u32[]{:S(2)}) collective-permute-start(bf16[1024,256]{1,0:T(8,128)(2,1)S(1)} %mask_ham.1.refs_0_), channel_id=1, source_target_pairs={{0,24},{2,10},{4,28},{6,14},{8,0},{10,18},{12,4},{14,22},{16,8},{1... | collective-permute-start | bytes 1572872 | tf_op jit(solution)/shard_map/ppermute | solution.py:40
  6.3 0.5 mask_dens.1
  6.9 1.7 %collective-permute-start.12 = (bf16[512,512]{1,0:T(8,128)(2,1)S(1)}, bf16[512,512]{1,0:T(8,128)(2,1)S(1)}, u32[]{:S(2)}, u32[]{:S(2)}) collective-permute-start(bf16[512,512]{1,0:T(8,128)(2,1)S(1)} %get-tuple-element.36.refs_16_), channel_id=1, source_target_pairs={{0,224},{2,34},{4,228},{6,38},{8,232},{10,42},{12,236},{14,46},{16... | collective-permute-start | bytes 1572872 | tf_op jit(solution)/shard_map/ppermute | solution.py:33
  8.6 4.0 %collective-permute-start = (bf16[512,512]{1,0:T(8,128)(2,1)S(1)}, bf16[512,512]{1,0:T(8,128)(2,1)S(1)}, u32[]{:S(2)}, u32[]{:S(2)}) collective-permute-start(bf16[512,512]{1,0:T(8,128)(2,1)S(1)} %get-tuple-element.36.refs_16_), channel_id=1, source_target_pairs={{0,32},{2,226},{4,36},{6,230},{8,40},{10,234},{12,44},{14,238},{16... | collective-permute-start | bytes 1572872 | tf_op jit(solution)/shard_map/ppermute | solution.py:33
  12.5 1.4 %collective-permute-start.2 = (bf16[1024,256]{1,0:T(8,128)(2,1)S(1)}, bf16[1024,256]{1,0:T(8,128)(2,1)S(1)}, u32[]{:S(2)}, u32[]{:S(2)}) collective-permute-start(bf16[1024,256]{1,0:T(8,128)(2,1)S(1)} %mask_ham.1.refs_0_), channel_id=1, source_target_pairs={{0,8},{2,26},{4,12},{6,30},{8,16},{10,2},{12,20},{14,6},{16,24},{1... | collective-permute-start | bytes 1572872 | tf_op jit(solution)/shard_map/ppermute | solution.py:40
  14.0 1.4 %collective-permute-done.4.refs_8_ = bf16[1024,256]{1,0:T(8,128)(2,1)S(1)} collective-permute-done((bf16[1024,256]{1,0:T(8,128)(2,1)S(1)}, bf16[1024,256]{1,0:T(8,128)(2,1)S(1)}, u32[]{:S(2)}, u32[]{:S(2)}) %collective-permute-start.4) | collective-permute-done | bytes 524320 | tf_op jit(solution)/shard_map/ppermute | solution.py:49
  15.3 2.6 %collective-permute-start.10 = (bf16[1024,256]{1,0:T(8,128)(2,1)S(1)}, bf16[1024,256]{1,0:T(8,128)(2,1)S(1)}, u32[]{:S(2)}, u32[]{:S(2)}) collective-permute-start(bf16[1024,256]{1,0:T(8,128)(2,1)S(1)} %collective-permute-done.4.refs_8_), channel_id=1, source_target_pairs={{0,24},{2,10},{4,28},{6,14},{8,0},{10,18},{12,4},{14,22},{16,8},{1... | collective-permute-start | bytes 1572872 | tf_op jit(solution)/shard_map/ppermute | solution.py:40
  17.9 1.1 %collective-permute-done.12.refs_18_ = bf16[512,512]{1,0:T(8,128)(2,1)S(1)} collective-permute-done((bf16[512,512]{1,0:T(8,128)(2,1)S(1)}, bf16[512,512]{1,0:T(8,128)(2,1)S(1)}, u32[]{:S(2)}, u32[]{:S(2)}) %collective-permute-start.12) | collective-permute-done | bytes 524320 | tf_op jit(solution)/shard_map/ppermute | solution.py:33
  19.1 0.5 collective-permute-start.13
  19.5 1.8 %collective-permute-done.refs_17_ = bf16[512,512]{1,0:T(8,128)(2,1)S(1)} collective-permute-done((bf16[512,512]{1,0:T(8,128)(2,1)S(1)}, bf16[512,512]{1,0:T(8,128)(2,1)S(1)}, u32[]{:S(2)}, u32[]{:S(2)}) %collective-permute-start) | collective-permute-done | bytes 524320 | tf_op jit(solution)/shard_map/ppermute | solution.py:33
  21.3 3.2 %collective-permute-start.3 = (bf16[512,512]{1,0:T(8,128)(2,1)S(1)}, bf16[512,512]{1,0:T(8,128)(2,1)S(1)}, u32[]{:S(2)}, u32[]{:S(2)}) collective-permute-start(bf16[512,512]{1,0:T(8,128)(2,1)S(1)} %collective-permute-done.refs_17_), channel_id=1, source_target_pairs={{0,32},{2,226},{4,36},{6,230},{8,40},{10,234},{12,44},{14,238},{16... | collective-permute-start | bytes 1572872 | tf_op jit(solution)/shard_map/ppermute | solution.py:33
  24.5 5.7 %collective-permute-start.1 = (bf16[1024,256]{1,0:T(8,128)(2,1)S(1)}, bf16[1024,256]{1,0:T(8,128)(2,1)S(1)}, u32[]{:S(2)}, u32[]{:S(2)}) collective-permute-start(bf16[1024,256]{1,0:T(8,128)(2,1)S(1)} %mask_ham.1.refs_0_), channel_id=1, source_target_pairs={{0,2},{2,0},{4,6},{6,4},{8,10},{10,8},{12,14},{14,12},{16,18},{18,... | collective-permute-start | bytes 1572872 | tf_op jit(solution)/shard_map/ppermute | solution.py:49
  30.3 0.5 collective-permute-done.10.refs_12_
  30.8 1.0 collective-permute-start.11
  31.8 3.0 %collective-permute-start.17 = (bf16[512,512]{1,0:T(8,128)(2,1)S(1)}, bf16[512,512]{1,0:T(8,128)(2,1)S(1)}, u32[]{:S(2)}, u32[]{:S(2)}) collective-permute-start(bf16[512,512]{1,0:T(8,128)(2,1)S(1)} %collective-permute-done.3.refs_19_), channel_id=1, source_target_pairs={{0,32},{2,226},{4,36},{6,230},{8,40},{10,234},{12,44},{14,238},{16... | collective-permute-start | bytes 1572872 | tf_op jit(solution)/shard_map/ppermute | solution.py:33
  34.8 10.2 %collective-permute-start.5 = (bf16[1024,256]{1,0:T(8,128)(2,1)S(1)}, bf16[1024,256]{1,0:T(8,128)(2,1)S(1)}, u32[]{:S(2)}, u32[]{:S(2)}) collective-permute-start(bf16[1024,256]{1,0:T(8,128)(2,1)S(1)} %collective-permute-done.4.refs_8_), channel_id=1, source_target_pairs={{0,2},{2,0},{4,6},{6,4},{8,10},{10,8},{12,14},{14,12},{16,18},{18,... | collective-permute-start | bytes 1572872 | tf_op jit(solution)/shard_map/ppermute | solution.py:49
  45.0 2.3 %collective-permute-start.6 = (f32[8,512]{1,0:T(8,128)S(1)}, f32[8,512]{1,0:T(8,128)S(1)}, u32[]{:S(2)}, u32[]{:S(2)}) collective-permute-start(f32[8,512]{1,0:T(8,128)S(1)} %get-tuple-element.39), channel_id=1, source_target_pairs={{0,128},{2,130},{4,132},{6,134},{8,136},{10,138},{12,140},{14,142}... | collective-permute-start | bytes 49160 | tf_op jit(solution)/shard_map/ppermute | solution.py:33
  47.3 0.8 collective-permute-start.20
  48.1 3.8 %collective-permute-start.15 = (bf16[1024,256]{1,0:T(8,128)(2,1)S(1)}, bf16[1024,256]{1,0:T(8,128)(2,1)S(1)}, u32[]{:S(2)}, u32[]{:S(2)}) collective-permute-start(bf16[1024,256]{1,0:T(8,128)(2,1)S(1)} %collective-permute-done.11.refs_6_), channel_id=1, source_target_pairs={{0,2},{2,0},{4,6},{6,4},{8,10},{10,8},{12,14},{14,12},{16,18},{18,... | collective-permute-start | bytes 1572872 | tf_op jit(solution)/shard_map/ppermute | solution.py:49
  51.9 4.2 %collective-permute-start.18 = (bf16[1024,256]{1,0:T(8,128)(2,1)S(1)}, bf16[1024,256]{1,0:T(8,128)(2,1)S(1)}, u32[]{:S(2)}, u32[]{:S(2)}) collective-permute-start(bf16[1024,256]{1,0:T(8,128)(2,1)S(1)} %collective-permute-done.16.refs_10_), channel_id=1, source_target_pairs={{0,2},{2,0},{4,6},{6,4},{8,10},{10,8},{12,14},{14,12},{16,18},{18,... | collective-permute-start | bytes 1572872 | tf_op jit(solution)/shard_map/ppermute | solution.py:49
  56.1 2.1 %collective-permute-start.21 = (bf16[1024,256]{1,0:T(8,128)(2,1)S(1)}, bf16[1024,256]{1,0:T(8,128)(2,1)S(1)}, u32[]{:S(2)}, u32[]{:S(2)}) collective-permute-start(bf16[1024,256]{1,0:T(8,128)(2,1)S(1)} %collective-permute-done.20.refs_14_), channel_id=1, source_target_pairs={{0,2},{2,0},{4,6},{6,4},{8,10},{10,8},{12,14},{14,12},{16,18},{18,... | collective-permute-start | bytes 1572872 | tf_op jit(solution)/shard_map/ppermute | solution.py:49
  58.3 0.4 collective-permute-start.9
  58.7 3.4 %collective-permute-start.22 = (bf16[512,512]{1,0:T(8,128)(2,1)S(1)}, bf16[512,512]{1,0:T(8,128)(2,1)S(1)}, u32[]{:S(2)}, u32[]{:S(2)}) collective-permute-start(bf16[512,512]{1,0:T(8,128)(2,1)S(1)} %collective-permute-done.17.refs_21_), channel_id=1, source_target_pairs={{0,32},{2,226},{4,36},{6,230},{8,40},{10,234},{12,44},{14,238},{16... | collective-permute-start | bytes 1572872 | tf_op jit(solution)/shard_map/ppermute | solution.py:33
  62.2 6.2 %early.1 = (f32[512,512]{1,0:T(8,128)}, f32[512,512]{1,0:T(8,128)S(1)}, bf16[2,1024,256]{2,1,0:T(8,128)(2,1)S(1)}, f32[8,1024]{1,0:T(8,128)S(1)}) custom-call(bf16[1024,256]{1,0:T(8,128)(2,1)S(1)} %mask_ham.1.refs_0_, bf16[1024,256]{1,0:T(8,128)(2,1)S(1)} %collective-permute-done.1.refs_1_, bf16[1024,256]{1,0:T(8,128)(2,1)S(1)} %collective-permute-done.2.refs_2_, ...), custom_call_target="tpu_custom_call" | custom-call | flops 4294967296 | bytes 4194304 | tf_op jit(solution)/shard_map/early/pallas_call | solution.py:183
  68.4 0.2 scatter.4
  68.7 0.3 collective-permute-start.24
  69.0 2.4 %collective-permute-start.25 = (f32[8,1024]{1,0:T(8,128)S(1)}, f32[8,1024]{1,0:T(8,128)}, u32[]{:S(2)}, u32[]{:S(2)}) collective-permute-start(f32[8,1024]{1,0:T(8,128)S(1)} %scatter.4), channel_id=1, source_target_pairs={{0,5},{1,4},{2,7},{3,6},{4,0},{5,1},{6,2},{7,3},{8,13},{9,12},{10,... | collective-permute-start | bytes 98312 | tf_op jit(solution)/shard_map/ppermute | solution.py:62
  71.4 1.3 %collective-permute-start.26 = (f32[8,1024]{1,0:T(8,128)S(1)}, f32[8,1024]{1,0:T(8,128)S(1)}, u32[]{:S(2)}, u32[]{:S(2)}) collective-permute-start(f32[8,1024]{1,0:T(8,128)S(1)} %scatter.4), channel_id=1, source_target_pairs={{0,1},{1,0},{2,3},{3,2},{4,5},{5,4},{6,7},{7,6},{8,9},{9,8},{10,11... | collective-permute-start | bytes 98312 | tf_op jit(solution)/shard_map/ppermute | solution.py:62
  72.7 2.3 %late.1 = (f32[288,512]{1,0:T(8,128)S(1)}, f32[224,512]{1,0:T(8,128)}) custom-call(f32[512,512]{1,0:T(8,128)} %get-tuple-element.50.other_ref, bf16[2,1024,256]{2,1,0:T(8,128)(2,1)S(1)} %get-tuple-element.51.ham_ref, bf16[512,512]{1,0:T(8,128)(2,1)S(1)} %collective-permute-done.22.den_ref), custom_call_target="tpu_custom_call" | custom-call | tf_op jit(solution)/shard_map/late/pallas_call | solution.py:222
  75.0 1.8 %collective-permute-start.23 = (f32[288,512]{1,0:T(8,128)S(1)}, f32[288,512]{1,0:T(8,128)S(1)}, u32[]{:S(2)}, u32[]{:S(2)}) collective-permute-start(f32[288,512]{1,0:T(8,128)S(1)} %get-tuple-element.52), channel_id=1, source_target_pairs={{0,1},{1,0},{2,3},{3,2},{4,5},{5,4},{6,7},{7,6},{8,9},{9,8},{10,11... | collective-permute-start | bytes 1769480 | tf_op jit(solution)/shard_map/ppermute | solution.py:53
  76.8 0.8 add_add_fusion.1
  77.7 2.7 %collective-permute-start.29 = (f32[8,1024]{1,0:T(8,128)S(1)}, f32[8,1024]{1,0:T(8,128)S(1)}, u32[]{:S(2)}, u32[]{:S(2)}) collective-permute-start(f32[8,1024]{1,0:T(8,128)S(1)} %add_add_fusion.1), channel_id=1, source_target_pairs={{0,24},{2,26},{4,28},{6,30},{8,0},{10,2},{12,4},{14,6},{16,8},{18,... | collective-permute-start | bytes 98312 | tf_op jit(solution)/shard_map/ppermute | solution.py:45
  80.4 1.6 %collective-permute-done.28 = f32[8,1024]{1,0:T(8,128)S(1)} collective-permute-done((f32[8,1024]{1,0:T(8,128)S(1)}, f32[8,1024]{1,0:T(8,128)S(1)}, u32[]{:S(2)}, u32[]{:S(2)}) %collective-permute-start.28) | collective-permute-done | bytes 32800 | tf_op jit(solution)/shard_map/ppermute | solution.py:45
  81.9 3.0 %collective-permute-done.30 = f32[8,1024]{1,0:T(8,128)S(1)} collective-permute-done((f32[8,1024]{1,0:T(8,128)S(1)}, f32[8,1024]{1,0:T(8,128)S(1)}, u32[]{:S(2)}, u32[]{:S(2)}) %collective-permute-start.30) | collective-permute-done | bytes 32800 | tf_op jit(solution)/shard_map/ppermute | solution.py:45
  84.9 2.1 %collective-permute-start.31 = (f32[8,1024]{1,0:T(8,128)S(1)}, f32[8,1024]{1,0:T(8,128)S(1)}, u32[]{:S(2)}, u32[]{:S(2)}) collective-permute-start(f32[8,1024]{1,0:T(8,128)S(1)} %add_add_fusion), channel_id=1, source_target_pairs={{0,2},{2,0},{4,6},{6,4},{8,10},{10,8},{12,14},{14,12},{16,18},{18,... | collective-permute-start | bytes 98312 | tf_op jit(solution)/shard_map/ppermute | solution.py:49
  87.1 1.3 %collective-permute-start.27 = (f32[224,512]{1,0:T(8,128)}, f32[224,512]{1,0:T(8,128)}, u32[]{:S(2)}, u32[]{:S(2)}) collective-permute-start(f32[224,512]{1,0:T(8,128)} %get-tuple-element.56), channel_id=1, source_target_pairs={{0,1},{1,0},{2,3},{3,2},{4,5},{5,4},{6,7},{7,6},{8,9},{9,8},{10,11... | collective-permute-start | bytes 1376264 | tf_op jit(solution)/shard_map/ppermute | solution.py:53
  88.4 2.7 %collective-permute-done.23.first_ref = f32[288,512]{1,0:T(8,128)S(1)} collective-permute-done((f32[288,512]{1,0:T(8,128)S(1)}, f32[288,512]{1,0:T(8,128)S(1)}, u32[]{:S(2)}, u32[]{:S(2)}) %collective-permute-start.23) | collective-permute-done | bytes 589856 | tf_op jit(solution)/shard_map/ppermute | solution.py:53
  91.2 0.2 fusion
  91.5 0.3 convolution_bitcast_fusion
  91.8 0.8 collective-permute-start.32
  92.6 0.4 kept.1.kept_ref
  93.0 8.5 %collective-permute-done.27.second_ref = f32[224,512]{1,0:T(8,128)} collective-permute-done((f32[224,512]{1,0:T(8,128)}, f32[224,512]{1,0:T(8,128)}, u32[]{:S(2)}, u32[]{:S(2)}) %collective-permute-start.27) | collective-permute-done | bytes 458784 | tf_op jit(solution)/shard_map/ppermute | solution.py:53
  101.6 1.9 %finish.1 = bf16[512,512]{1,0:T(8,128)(2,1)} custom-call(f32[512,512]{1,0:T(8,128)S(1)} %kept.1.kept_ref, f32[288,512]{1,0:T(8,128)S(1)} %collective-permute-done.23.first_ref, f32[224,512]{1,0:T(8,128)} %collective-permute-done.27.second_ref), custom_call_target="tpu_custom_call" | custom-call | tf_op jit(solution)/shard_map/finish/pallas_call | solution.py:254
  103.5 0.6 pad_maximum_fusion
  (52 shorter events, 0.6 us)
Async XLA Ops:
  0.6 90.6 %copy-start = (bf16[64,16,128]{2,1,0:T(8,128)(2,1)S(1)}, bf16[64,16,128]{2,1,0:T(8,128)(2,1)}, u32[]{:S(2)}) copy-start(bf16[64,16,128]{2,1,0:T(8,128)(2,1)} %param.12) | copy-start | bytes 786436
  1.4 1.0 %copy-start.1 = (bf16[1024,256]{1,0:T(8,128)(2,1)S(1)}, bf16[1024,256]{1,0:T(8,128)(2,1)}, u32[]{:S(2)}) copy-start(bf16[1024,256]{1,0:T(8,128)(2,1)} %matrix_ref.2) | copy-start | bytes 1572868
  2.5 3.8 %copy-start.2 = (bf16[512,512]{1,0:T(8,128)(2,1)S(1)}, bf16[512,512]{1,0:T(8,128)(2,1)}, u32[]{:S(2)}) copy-start(bf16[512,512]{1,0:T(8,128)(2,1)} %matrix_ref.3) | copy-start | bytes 1572868
  2.5 3.8 %copy-start.3 = (s32[8,8]{1,0:T(8,128)S(1)}, s32[8,8]{1,0:T(8,128)}, u32[]{:S(2)}) copy-start(s32[8,8]{1,0:T(8,128)} %pattern_ref.2) | copy-start | bytes 772
  2.9 12.4 %collective-permute-start.4 = (bf16[1024,256]{1,0:T(8,128)(2,1)S(1)}, bf16[1024,256]{1,0:T(8,128)(2,1)S(1)}, u32[]{:S(2)}, u32[]{:S(2)}) collective-permute-start(bf16[1024,256]{1,0:T(8,128)(2,1)S(1)} %mask_ham.1.refs_0_), channel_id=1, source_target_pairs={{0,4},{2,6},{4,0},{6,2},{8,12},{10,14},{12,8},{14,10},{16,20},{18,... | collective-permute-start | bytes 1572872 | tf_op jit(solution)/shard_map/ppermute | solution.py:49
  5.0 10.3 %collective-permute-start.8 = (bf16[1024,256]{1,0:T(8,128)(2,1)S(1)}, bf16[1024,256]{1,0:T(8,128)(2,1)S(1)}, u32[]{:S(2)}, u32[]{:S(2)}) collective-permute-start(bf16[1024,256]{1,0:T(8,128)(2,1)S(1)} %mask_ham.1.refs_0_), channel_id=1, source_target_pairs={{0,24},{2,10},{4,28},{6,14},{8,0},{10,18},{12,4},{14,22},{16,8},{1... | collective-permute-start | bytes 1572872 | tf_op jit(solution)/shard_map/ppermute | solution.py:40
  6.9 55.3 %copy-start.4 = (s32[8]{0:T(128)S(1)}, s32[8]{0:T(128)}, u32[]{:S(2)}) copy-start(s32[8]{0:T(128)} %param.13) | copy-start | bytes 100
  6.9 12.2 %collective-permute-start.12 = (bf16[512,512]{1,0:T(8,128)(2,1)S(1)}, bf16[512,512]{1,0:T(8,128)(2,1)S(1)}, u32[]{:S(2)}, u32[]{:S(2)}) collective-permute-start(bf16[512,512]{1,0:T(8,128)(2,1)S(1)} %get-tuple-element.36.refs_16_), channel_id=1, source_target_pairs={{0,224},{2,34},{4,228},{6,38},{8,232},{10,42},{12,236},{14,46},{16... | collective-permute-start | bytes 1572872 | tf_op jit(solution)/shard_map/ppermute | solution.py:33
  8.6 12.8 %collective-permute-start = (bf16[512,512]{1,0:T(8,128)(2,1)S(1)}, bf16[512,512]{1,0:T(8,128)(2,1)S(1)}, u32[]{:S(2)}, u32[]{:S(2)}) collective-permute-start(bf16[512,512]{1,0:T(8,128)(2,1)S(1)} %get-tuple-element.36.refs_16_), channel_id=1, source_target_pairs={{0,32},{2,226},{4,36},{6,230},{8,40},{10,234},{12,44},{14,238},{16... | collective-permute-start | bytes 1572872 | tf_op jit(solution)/shard_map/ppermute | solution.py:33
  12.5 17.7 %collective-permute-start.2 = (bf16[1024,256]{1,0:T(8,128)(2,1)S(1)}, bf16[1024,256]{1,0:T(8,128)(2,1)S(1)}, u32[]{:S(2)}, u32[]{:S(2)}) collective-permute-start(bf16[1024,256]{1,0:T(8,128)(2,1)S(1)} %mask_ham.1.refs_0_), channel_id=1, source_target_pairs={{0,8},{2,26},{4,12},{6,30},{8,16},{10,2},{12,20},{14,6},{16,24},{1... | collective-permute-start | bytes 1572872 | tf_op jit(solution)/shard_map/ppermute | solution.py:40
  15.3 15.4 %collective-permute-start.10 = (bf16[1024,256]{1,0:T(8,128)(2,1)S(1)}, bf16[1024,256]{1,0:T(8,128)(2,1)S(1)}, u32[]{:S(2)}, u32[]{:S(2)}) collective-permute-start(bf16[1024,256]{1,0:T(8,128)(2,1)S(1)} %collective-permute-done.4.refs_8_), channel_id=1, source_target_pairs={{0,24},{2,10},{4,28},{6,14},{8,0},{10,18},{12,4},{14,22},{16,8},{1... | collective-permute-start | bytes 1572872 | tf_op jit(solution)/shard_map/ppermute | solution.py:40
  19.1 12.7 %collective-permute-start.13 = (bf16[512,512]{1,0:T(8,128)(2,1)S(1)}, bf16[512,512]{1,0:T(8,128)(2,1)S(1)}, u32[]{:S(2)}, u32[]{:S(2)}) collective-permute-start(bf16[512,512]{1,0:T(8,128)(2,1)S(1)} %collective-permute-done.12.refs_18_), channel_id=1, source_target_pairs={{0,224},{2,34},{4,228},{6,38},{8,232},{10,42},{12,236},{14,46},{16... | collective-permute-start | bytes 1572872 | tf_op jit(solution)/shard_map/ppermute | solution.py:33
  21.3 10.5 %collective-permute-start.3 = (bf16[512,512]{1,0:T(8,128)(2,1)S(1)}, bf16[512,512]{1,0:T(8,128)(2,1)S(1)}, u32[]{:S(2)}, u32[]{:S(2)}) collective-permute-start(bf16[512,512]{1,0:T(8,128)(2,1)S(1)} %collective-permute-done.refs_17_), channel_id=1, source_target_pairs={{0,32},{2,226},{4,36},{6,230},{8,40},{10,234},{12,44},{14,238},{16... | collective-permute-start | bytes 1572872 | tf_op jit(solution)/shard_map/ppermute | solution.py:33
  24.5 10.3 %collective-permute-start.1 = (bf16[1024,256]{1,0:T(8,128)(2,1)S(1)}, bf16[1024,256]{1,0:T(8,128)(2,1)S(1)}, u32[]{:S(2)}, u32[]{:S(2)}) collective-permute-start(bf16[1024,256]{1,0:T(8,128)(2,1)S(1)} %mask_ham.1.refs_0_), channel_id=1, source_target_pairs={{0,2},{2,0},{4,6},{6,4},{8,10},{10,8},{12,14},{14,12},{16,18},{18,... | collective-permute-start | bytes 1572872 | tf_op jit(solution)/shard_map/ppermute | solution.py:49
  30.3 14.7 %collective-permute-start.16 = (bf16[1024,256]{1,0:T(8,128)(2,1)S(1)}, bf16[1024,256]{1,0:T(8,128)(2,1)S(1)}, u32[]{:S(2)}, u32[]{:S(2)}) collective-permute-start(bf16[1024,256]{1,0:T(8,128)(2,1)S(1)} %collective-permute-done.4.refs_8_), channel_id=1, source_target_pairs={{0,8},{2,26},{4,12},{6,30},{8,16},{10,2},{12,20},{14,6},{16,24},{1... | collective-permute-start | bytes 1572872 | tf_op jit(solution)/shard_map/ppermute | solution.py:40
  30.8 16.5 %collective-permute-start.11 = (bf16[1024,256]{1,0:T(8,128)(2,1)S(1)}, bf16[1024,256]{1,0:T(8,128)(2,1)S(1)}, u32[]{:S(2)}, u32[]{:S(2)}) collective-permute-start(bf16[1024,256]{1,0:T(8,128)(2,1)S(1)} %collective-permute-done.8.refs_4_), channel_id=1, source_target_pairs={{0,24},{2,10},{4,28},{6,14},{8,0},{10,18},{12,4},{14,22},{16,8},{1... | collective-permute-start | bytes 1572872 | tf_op jit(solution)/shard_map/ppermute | solution.py:40
  31.8 16.3 %collective-permute-start.14 = (bf16[512,512]{1,0:T(8,128)(2,1)S(1)}, bf16[512,512]{1,0:T(8,128)(2,1)S(1)}, u32[]{:S(2)}, u32[]{:S(2)}) collective-permute-start(bf16[512,512]{1,0:T(8,128)(2,1)S(1)} %collective-permute-done.13.refs_20_), channel_id=1, source_target_pairs={{0,224},{2,34},{4,228},{6,38},{8,232},{10,42},{12,236},{14,46},{16... | collective-permute-start | bytes 1572872 | tf_op jit(solution)/shard_map/ppermute | solution.py:33
  31.8 20.1 %collective-permute-start.17 = (bf16[512,512]{1,0:T(8,128)(2,1)S(1)}, bf16[512,512]{1,0:T(8,128)(2,1)S(1)}, u32[]{:S(2)}, u32[]{:S(2)}) collective-permute-start(bf16[512,512]{1,0:T(8,128)(2,1)S(1)} %collective-permute-done.3.refs_19_), channel_id=1, source_target_pairs={{0,32},{2,226},{4,36},{6,230},{8,40},{10,234},{12,44},{14,238},{16... | collective-permute-start | bytes 1572872 | tf_op jit(solution)/shard_map/ppermute | solution.py:33
  34.8 21.2 %collective-permute-start.5 = (bf16[1024,256]{1,0:T(8,128)(2,1)S(1)}, bf16[1024,256]{1,0:T(8,128)(2,1)S(1)}, u32[]{:S(2)}, u32[]{:S(2)}) collective-permute-start(bf16[1024,256]{1,0:T(8,128)(2,1)S(1)} %collective-permute-done.4.refs_8_), channel_id=1, source_target_pairs={{0,2},{2,0},{4,6},{6,4},{8,10},{10,8},{12,14},{14,12},{16,18},{18,... | collective-permute-start | bytes 1572872 | tf_op jit(solution)/shard_map/ppermute | solution.py:49
  45.0 11.1 %collective-permute-start.6 = (f32[8,512]{1,0:T(8,128)S(1)}, f32[8,512]{1,0:T(8,128)S(1)}, u32[]{:S(2)}, u32[]{:S(2)}) collective-permute-start(f32[8,512]{1,0:T(8,128)S(1)} %get-tuple-element.39), channel_id=1, source_target_pairs={{0,128},{2,130},{4,132},{6,134},{8,136},{10,138},{12,140},{14,142}... | collective-permute-start | bytes 49160 | tf_op jit(solution)/shard_map/ppermute | solution.py:33
  47.3 8.8 %collective-permute-start.20 = (bf16[1024,256]{1,0:T(8,128)(2,1)S(1)}, bf16[1024,256]{1,0:T(8,128)(2,1)S(1)}, u32[]{:S(2)}, u32[]{:S(2)}) collective-permute-start(bf16[1024,256]{1,0:T(8,128)(2,1)S(1)} %collective-permute-done.16.refs_10_), channel_id=1, source_target_pairs={{0,8},{2,26},{4,12},{6,30},{8,16},{10,2},{12,20},{14,6},{16,24},{1... | collective-permute-start | bytes 1572872 | tf_op jit(solution)/shard_map/ppermute | solution.py:40
  48.1 8.1 %collective-permute-start.15 = (bf16[1024,256]{1,0:T(8,128)(2,1)S(1)}, bf16[1024,256]{1,0:T(8,128)(2,1)S(1)}, u32[]{:S(2)}, u32[]{:S(2)}) collective-permute-start(bf16[1024,256]{1,0:T(8,128)(2,1)S(1)} %collective-permute-done.11.refs_6_), channel_id=1, source_target_pairs={{0,2},{2,0},{4,6},{6,4},{8,10},{10,8},{12,14},{14,12},{16,18},{18,... | collective-permute-start | bytes 1572872 | tf_op jit(solution)/shard_map/ppermute | solution.py:49
  51.9 6.3 %collective-permute-start.18 = (bf16[1024,256]{1,0:T(8,128)(2,1)S(1)}, bf16[1024,256]{1,0:T(8,128)(2,1)S(1)}, u32[]{:S(2)}, u32[]{:S(2)}) collective-permute-start(bf16[1024,256]{1,0:T(8,128)(2,1)S(1)} %collective-permute-done.16.refs_10_), channel_id=1, source_target_pairs={{0,2},{2,0},{4,6},{6,4},{8,10},{10,8},{12,14},{14,12},{16,18},{18,... | collective-permute-start | bytes 1572872 | tf_op jit(solution)/shard_map/ppermute | solution.py:49
  56.0 2.3 %collective-permute-start.7 = (bf16[1024,256]{1,0:T(8,128)(2,1)S(1)}, bf16[1024,256]{1,0:T(8,128)(2,1)S(1)}, u32[]{:S(2)}, u32[]{:S(2)}) collective-permute-start(bf16[1024,256]{1,0:T(8,128)(2,1)S(1)} %collective-permute-done.2.refs_2_), channel_id=1, source_target_pairs={{0,2},{2,0},{4,6},{6,4},{8,10},{10,8},{12,14},{14,12},{16,18},{18,... | collective-permute-start | bytes 1572872 | tf_op jit(solution)/shard_map/ppermute | solution.py:49
  56.1 6.0 %collective-permute-start.21 = (bf16[1024,256]{1,0:T(8,128)(2,1)S(1)}, bf16[1024,256]{1,0:T(8,128)(2,1)S(1)}, u32[]{:S(2)}, u32[]{:S(2)}) collective-permute-start(bf16[1024,256]{1,0:T(8,128)(2,1)S(1)} %collective-permute-done.20.refs_14_), channel_id=1, source_target_pairs={{0,2},{2,0},{4,6},{6,4},{8,10},{10,8},{12,14},{14,12},{16,18},{18,... | collective-permute-start | bytes 1572872 | tf_op jit(solution)/shard_map/ppermute | solution.py:49
  58.2 3.9 %collective-permute-start.19 = (bf16[1024,256]{1,0:T(8,128)(2,1)S(1)}, bf16[1024,256]{1,0:T(8,128)(2,1)S(1)}, u32[]{:S(2)}, u32[]{:S(2)}) collective-permute-start(bf16[1024,256]{1,0:T(8,128)(2,1)S(1)} %collective-permute-done.10.refs_12_), channel_id=1, source_target_pairs={{0,2},{2,0},{4,6},{6,4},{8,10},{10,8},{12,14},{14,12},{16,18},{18,... | collective-permute-start | bytes 1572872 | tf_op jit(solution)/shard_map/ppermute | solution.py:49
  58.3 3.8 %collective-permute-start.9 = (bf16[1024,256]{1,0:T(8,128)(2,1)S(1)}, bf16[1024,256]{1,0:T(8,128)(2,1)S(1)}, u32[]{:S(2)}, u32[]{:S(2)}) collective-permute-start(bf16[1024,256]{1,0:T(8,128)(2,1)S(1)} %collective-permute-done.8.refs_4_), channel_id=1, source_target_pairs={{0,2},{2,0},{4,6},{6,4},{8,10},{10,8},{12,14},{14,12},{16,18},{18,... | collective-permute-start | bytes 1572872 | tf_op jit(solution)/shard_map/ppermute | solution.py:49
  58.7 13.9 %collective-permute-start.22 = (bf16[512,512]{1,0:T(8,128)(2,1)S(1)}, bf16[512,512]{1,0:T(8,128)(2,1)S(1)}, u32[]{:S(2)}, u32[]{:S(2)}) collective-permute-start(bf16[512,512]{1,0:T(8,128)(2,1)S(1)} %collective-permute-done.17.refs_21_), channel_id=1, source_target_pairs={{0,32},{2,226},{4,36},{6,230},{8,40},{10,234},{12,44},{14,238},{16... | collective-permute-start | bytes 1572872 | tf_op jit(solution)/shard_map/ppermute | solution.py:33
  68.7 8.1 %collective-permute-start.24 = (f32[8,1024]{1,0:T(8,128)S(1)}, f32[8,1024]{1,0:T(8,128)}, u32[]{:S(2)}, u32[]{:S(2)}) collective-permute-start(f32[8,1024]{1,0:T(8,128)S(1)} %scatter.4), channel_id=1, source_target_pairs={{0,4},{1,5},{2,6},{3,7},{4,1},{5,0},{6,3},{7,2},{8,12},{9,13},{10,... | collective-permute-start | bytes 98312 | tf_op jit(solution)/shard_map/ppermute | solution.py:62
  69.0 7.8 %collective-permute-start.25 = (f32[8,1024]{1,0:T(8,128)S(1)}, f32[8,1024]{1,0:T(8,128)}, u32[]{:S(2)}, u32[]{:S(2)}) collective-permute-start(f32[8,1024]{1,0:T(8,128)S(1)} %scatter.4), channel_id=1, source_target_pairs={{0,5},{1,4},{2,7},{3,6},{4,0},{5,1},{6,2},{7,3},{8,13},{9,12},{10,... | collective-permute-start | bytes 98312 | tf_op jit(solution)/shard_map/ppermute | solution.py:62
  71.4 5.4 %collective-permute-start.26 = (f32[8,1024]{1,0:T(8,128)S(1)}, f32[8,1024]{1,0:T(8,128)S(1)}, u32[]{:S(2)}, u32[]{:S(2)}) collective-permute-start(f32[8,1024]{1,0:T(8,128)S(1)} %scatter.4), channel_id=1, source_target_pairs={{0,1},{1,0},{2,3},{3,2},{4,5},{5,4},{6,7},{7,6},{8,9},{9,8},{10,11... | collective-permute-start | bytes 98312 | tf_op jit(solution)/shard_map/ppermute | solution.py:62
  75.0 16.1 %collective-permute-start.23 = (f32[288,512]{1,0:T(8,128)S(1)}, f32[288,512]{1,0:T(8,128)S(1)}, u32[]{:S(2)}, u32[]{:S(2)}) collective-permute-start(f32[288,512]{1,0:T(8,128)S(1)} %get-tuple-element.52), channel_id=1, source_target_pairs={{0,1},{1,0},{2,3},{3,2},{4,5},{5,4},{6,7},{7,6},{8,9},{9,8},{10,11... | collective-permute-start | bytes 1769480 | tf_op jit(solution)/shard_map/ppermute | solution.py:53
  77.6 4.3 %collective-permute-start.28 = (f32[8,1024]{1,0:T(8,128)S(1)}, f32[8,1024]{1,0:T(8,128)S(1)}, u32[]{:S(2)}, u32[]{:S(2)}) collective-permute-start(f32[8,1024]{1,0:T(8,128)S(1)} %add_add_fusion.1), channel_id=1, source_target_pairs={{0,8},{2,10},{4,12},{6,14},{8,16},{10,18},{12,20},{14,22},{16,24},... | collective-permute-start | bytes 98312 | tf_op jit(solution)/shard_map/ppermute | solution.py:45
  77.7 4.3 %collective-permute-start.29 = (f32[8,1024]{1,0:T(8,128)S(1)}, f32[8,1024]{1,0:T(8,128)S(1)}, u32[]{:S(2)}, u32[]{:S(2)}) collective-permute-start(f32[8,1024]{1,0:T(8,128)S(1)} %add_add_fusion.1), channel_id=1, source_target_pairs={{0,24},{2,26},{4,28},{6,30},{8,0},{10,2},{12,4},{14,6},{16,8},{18,... | collective-permute-start | bytes 98312 | tf_op jit(solution)/shard_map/ppermute | solution.py:45
  80.3 4.6 %collective-permute-start.30 = (f32[8,1024]{1,0:T(8,128)S(1)}, f32[8,1024]{1,0:T(8,128)S(1)}, u32[]{:S(2)}, u32[]{:S(2)}) collective-permute-start(f32[8,1024]{1,0:T(8,128)S(1)} %add_add_fusion.1), channel_id=1, source_target_pairs={{0,16},{2,18},{4,20},{6,22},{8,24},{10,26},{12,28},{14,30},{16,0},... | collective-permute-start | bytes 98312 | tf_op jit(solution)/shard_map/ppermute | solution.py:45
  84.9 3.5 %collective-permute-start.31 = (f32[8,1024]{1,0:T(8,128)S(1)}, f32[8,1024]{1,0:T(8,128)S(1)}, u32[]{:S(2)}, u32[]{:S(2)}) collective-permute-start(f32[8,1024]{1,0:T(8,128)S(1)} %add_add_fusion), channel_id=1, source_target_pairs={{0,2},{2,0},{4,6},{6,4},{8,10},{10,8},{12,14},{14,12},{16,18},{18,... | collective-permute-start | bytes 98312 | tf_op jit(solution)/shard_map/ppermute | solution.py:49
  87.1 14.4 %collective-permute-start.27 = (f32[224,512]{1,0:T(8,128)}, f32[224,512]{1,0:T(8,128)}, u32[]{:S(2)}, u32[]{:S(2)}) collective-permute-start(f32[224,512]{1,0:T(8,128)} %get-tuple-element.56), channel_id=1, source_target_pairs={{0,1},{1,0},{2,3},{3,2},{4,5},{5,4},{6,7},{7,6},{8,9},{9,8},{10,11... | collective-permute-start | bytes 1376264 | tf_op jit(solution)/shard_map/ppermute | solution.py:53
  91.8 11.7 %collective-permute-start.32 = (f32[16,128]{1,0:T(8,128)S(1)}, f32[16,128]{1,0:T(8,128)S(1)}, u32[]{:S(2)}, u32[]{:S(2)}) collective-permute-start(f32[16,128]{1,0:T(8,128)S(1)} %slice_bitcast_fusion.2), channel_id=1, source_target_pairs={{0,32},{32,64},{64,96},{96,128},{128,160},{160,192},{192,224},{224... | collective-permute-start | bytes 24584 | tf_op jit(solution)/shard_map/ppermute | solution.py:335
